TPU v7x, 32 devices: a whole 2x2x4 slice. The times are simulated.
32 devices in a mesh: camp: 2 (over x), wide: 16 (over z, y, core).
Axes of the slice: x: 2, y: 2, z: 4, core: 2. Of those that a mesh axis runs over, the one named last changes fastest.
Arguments:
- coords: float32 [3, 16384], P(None, ('camp', 'wide')), parts along dimension 1, may hold values from 0 to 1
- intensity: float32 [16384], P(('camp', 'wide')), parts along dimension 0, may hold values from 0.3 to 3
- start: bfloat16 [16, 16384], P(None, ('camp', 'wide')), parts along dimension 1, may hold values from -6 to 6
Outputs:
- basis: float32 [16, 16384], P(None, ('camp', 'wide')), parts along dimension 1
- factor_out: float32 [32, 16], P('camp'), parts along dimension 0
There are 2 independent parts, one for each index of `camp`. A program takes and returns all parts, laid end to end along the dimension named above; each array names one. Nothing has to cross between parts.
All inputs are finite; a program needn't handle non-finite values.
Results may differ from a plain program's by a relative error of at most 0.00075.
Values may be sent and summed in bfloat16 or wider, within the bound.
No kernel may reach another device: no remote copies, remote signals or barrier semaphores. Data moves between devices by JAX's collectives and lax.ppermute only.
A program may use at most 64 MiB of HBM per device.

v0:
```python
import jax
import jax.numpy as jnp
from jax import lax
from jax.sharding import PartitionSpec as P

ITERS = 2


rate_scale = 3.0**0.5 / 0.15


def kernel_tile(left_xyz, left_scale, right_xyz, right_scale):
    squared = (left_xyz[0][:, None] - right_xyz[0][None, :]) ** 2
    squared = squared + (left_xyz[1][:, None] - right_xyz[1][None, :]) ** 2
    squared = squared + (left_xyz[2][:, None] - right_xyz[2][None, :]) ** 2
    scaled = rate_scale * jnp.sqrt(squared)
    value = left_scale[:, None] * right_scale[None, :] * (1.0 + scaled) * jnp.exp(-scaled)
    return value.astype(jnp.bfloat16)


def body(coords, intensity, start):
    width = lax.axis_size("wide")
    shard_rows = coords.shape[1]
    columns_count = start.shape[0]
    total_points = shard_rows * width
    all_xyz, all_scale = (
        lax.all_gather(coords, "wide", axis=1, tiled=True),
        lax.all_gather(intensity, "wide", axis=0, tiled=True),
    )
    basis = start
    factor_lower = jnp.zeros((columns_count, columns_count), jnp.float32)
    for sweep_index in range(ITERS):
        vectors = basis.astype(jnp.bfloat16)

        def apply_range(running, segment, anchor, length):
            right_xyz = lax.dynamic_slice_in_dim(all_xyz, anchor, length, 1)
            right_scale = lax.dynamic_slice_in_dim(all_scale, anchor, length, 0)
            block_tile = kernel_tile(coords, intensity, right_xyz, right_scale)
            return running + jnp.dot(segment, block_tile.T, preferred_element_type=jnp.float32)

        empty = jnp.zeros((columns_count, shard_rows), jnp.float32)
        add_segment = lax.all_gather(vectors, "wide", axis=1, tiled=True)
        span = add_segment.shape[1]

        def one_block(block_index, inner_sum):
            offset = (block_index * shard_rows).astype(jnp.int32)
            part_cols = lax.dynamic_slice_in_dim(add_segment, offset, shard_rows, 1)
            return apply_range(inner_sum, part_cols, offset, shard_rows)

        product = lax.fori_loop(0, span // shard_rows, one_block, empty)
        local_gram = jnp.dot(product, product.T, precision=lax.Precision.HIGHEST)
        gram = lax.psum(local_gram, "wide") / total_points
        factor_lower = jnp.linalg.cholesky(gram)
        basis = lax.linalg.triangular_solve(factor_lower, product, left_side=True, lower=True)
    return (basis, factor_lower)


def solution(mesh):
    placed = (P(None, ("camp", "wide")), P(("camp", "wide")), P(None, ("camp", "wide")))
    return jax.shard_map(
        body,
        mesh=mesh,
        in_specs=placed,
        out_specs=(P(None, ("camp", "wide")), P("camp", None)),
        check_vma=False,
    )
```

profile of v0, /device:TPU:0, one launch (start us, length us, event | category | flops | bytes accessed | tf_op | source)
XLA Modules:
  0.0 190.7 jit_solution(4200694979449054040)
XLA Ops:
  0.6 23.7 %all_gather.14 = f32[3,8192]{1,0:T(4,128)S(1)} all-gather(f32[3,512]{1,0:T(4,128)} %param.10), channel_id=1, replica_groups=mesh['camp'=2,'wide'=16] {'wide'}, dimensions={1}, use_global_device_ids=true | all-gather | bytes 104448 | tf_op jit(solution)/shard_map/all_gather | solution.py:27
  24.3 17.6 %all-gather = f32[16,1,512]{2,1,0:T(1,128)S(1)} all-gather(f32[1,1,512]{2,1,0:T(1,128)S(1)} %bitcast.75), channel_id=1, replica_groups=mesh['camp'=2,'wide'=16] {'wide'}, dimensions={0}, use_global_device_ids=true | all-gather | bytes 34816 | tf_op jit(solution)/shard_map/all_gather | solution.py:28
  42.0 19.6 %all_gather.12 = bf16[16,8192]{1,0:T(8,128)(2,1)S(1)} all-gather(bf16[16,512]{1,0:T(8,128)(2,1)S(1)} %copy-done.1), channel_id=1, replica_groups=mesh['camp'=2,'wide'=16] {'wide'}, dimensions={1}, use_global_device_ids=true | all-gather | bytes 278528 | tf_op jit(solution)/shard_map/all_gather | solution.py:42
  61.6 19.3 %while.28 = (s32[]{:T(128)}, f32[16,512]{1,0:T(8,128)S(1)}, bf16[16,8192]{1,0:T(8,128)(2,1)S(1)}, f32[512]{0:T(512)S(1)}, f32[8192]{0:T(1024)S(1)}, /*index=5*/f...) while((s32[]{:T(128)}, f32[16,512]{1,0:T(8,128)S(1)}, ...), condition=%wide.region_1.0_spmd.clone, body=%wide.region_0.0_spmd.clone.sunk | while | flops 12337161 | bytes 127201 | solution.py:50
  61.7 1.0 convolution_add_fusion.4
  62.9 1.0 convolution_add_fusion.4
  64.1 1.0 convolution_add_fusion.4
  65.3 1.0 convolution_add_fusion.4
  66.6 1.0 convolution_add_fusion.4
  67.8 1.0 convolution_add_fusion.4
  69.0 1.0 convolution_add_fusion.4
  70.2 1.0 convolution_add_fusion.4
  71.4 1.0 convolution_add_fusion.4
  72.6 1.0 convolution_add_fusion.4
  73.8 1.0 convolution_add_fusion.4
  75.0 1.0 convolution_add_fusion.4
  76.2 1.0 convolution_add_fusion.4
  77.4 1.0 convolution_add_fusion.4
  78.6 1.0 convolution_add_fusion.4
  79.8 1.0 convolution_add_fusion.4
  81.0 30.3 %psum.14 = f32[16,16]{0,1:T(8,128)S(1)} all-reduce(f32[16,16]{0,1:T(8,128)S(1)} %fusion.40), channel_id=1, replica_groups=mesh['camp'=2,'wide'=16] {'wide'}, use_global_device_ids=true, to_apply=%region_2.0 | all-reduce | flops 256 | bytes 2048 | tf_op jit(solution)/shard_map/psum | solution.py:52
  111.5 1.5 cholesky.44
  112.9 0.6 compare_reduce_fusion.1
  113.6 0.6 fusion.28
  114.2 1.2 custom-call.8
  115.7 17.8 %all_gather.15 = bf16[16,8192]{1,0:T(8,128)(2,1)S(1)} all-gather(bf16[16,512]{1,0:T(8,128)(2,1)S(1)} %convolution_convert_fusion), channel_id=1, replica_groups=mesh['camp'=2,'wide'=16] {'wide'}, dimensions={1}, use_global_device_ids=true | all-gather | bytes 278528 | tf_op jit(solution)/shard_map/all_gather | solution.py:42
  133.5 19.3 %while.29 = (s32[]{:T(128)}, f32[16,512]{1,0:T(8,128)S(1)}, bf16[16,8192]{1,0:T(8,128)(2,1)S(1)}, f32[512]{0:T(512)S(1)}, f32[8192]{0:T(1024)S(1)}, /*index=5*/f...) while((s32[]{:T(128)}, f32[16,512]{1,0:T(8,128)S(1)}, ...), condition=%wide.region_6.9_spmd.clone, body=%wide.region_5.8_spmd.clone.sunk | while | flops 12337161 | bytes 127201 | solution.py:50
  133.7 1.0 convolution_add_fusion.5
  134.9 1.0 convolution_add_fusion.5
  136.1 1.0 convolution_add_fusion.5
  137.3 1.0 convolution_add_fusion.5
  138.5 1.0 convolution_add_fusion.5
  139.7 1.0 convolution_add_fusion.5
  141.0 1.0 convolution_add_fusion.5
  142.2 1.0 convolution_add_fusion.5
  143.4 1.0 convolution_add_fusion.5
  144.6 1.0 convolution_add_fusion.5
  145.8 1.0 convolution_add_fusion.5
  147.0 1.0 convolution_add_fusion.5
  148.2 1.0 convolution_add_fusion.5
  149.4 1.0 convolution_add_fusion.5
  150.6 1.0 convolution_add_fusion.5
  151.8 1.0 convolution_add_fusion.5
  153.0 32.1 %psum.15 = f32[16,16]{0,1:T(8,128)S(1)} all-reduce(f32[16,16]{0,1:T(8,128)S(1)} %fusion.41), channel_id=1, replica_groups=mesh['camp'=2,'wide'=16] {'wide'}, use_global_device_ids=true, to_apply=%region_7.10 | all-reduce | flops 256 | bytes 2048 | tf_op jit(solution)/shard_map/psum | solution.py:52
  185.2 1.5 cholesky.55
  187.4 1.2 select_bitcast_fusion
  188.6 1.2 custom-call.9
  189.8 0.9 fusion.29
  (84 shorter events, 6.5 us)
Async XLA Ops:
  0.6 23.7 %copy-start.2 = (f32[512]{0:T(512)S(1)}, f32[512]{0:T(512)}, u32[]{:S(2)}) copy-start(f32[512]{0:T(512)} %param.11) | copy-start | bytes 6148
  24.3 17.6 %copy-start.1 = (bf16[16,512]{1,0:T(8,128)(2,1)S(1)}, bf16[16,512]{1,0:T(8,128)(2,1)}, u32[]{:S(2)}) copy-start(bf16[16,512]{1,0:T(8,128)(2,1)} %param.12) | copy-start | bytes 49156
  42.0 19.6 %copy-start = (f32[3,512]{1,0:T(4,128)S(1)}, f32[3,512]{1,0:T(4,128)}, u32[]{:S(2)}) copy-start(f32[3,512]{1,0:T(4,128)} %param.10) | copy-start | bytes 18436
where the time goes:
time: 191 us
  blocking collectives  141 us (74%)
  matrix products  33.9 us (18%)
  other arithmetic  8.63 us (5%)
  local copies, waits for them, and re-layouts  5.28 us (3%)
    psum x2, blocking collectives, body(): gram = lax.psum(local_gram, 'wide') / total_points  62.5 us
    all_gather x2, blocking collectives, body(): add_segment = lax.all_gather(vectors, 'wide', axis=1, tiled=True)  37.4 us
    dot_general x32, matrix products, apply_range(): jnp.dot(segment, block_tile.T, preferred_element_type=jnp.float32)  32.6 us
    all_gather x1, blocking collectives, body(): lax.all_gather(coords, 'wide', axis=1, tiled=True)  23.7 us
    all_gather x1, blocking collectives, body(): lax.all_gather(intensity, 'wide', axis=0, tiled=True)  17.6 us
    another operation x4, other arithmetic, body(): lax.linalg.triangular_solve(factor_lower, product, left_side=True, lower=...  4.35 us
    another operation x6, other arithmetic, body(): factor_lower = jnp.linalg.cholesky(gram)  4.26 us

commit v1 on v0

v1 whole, which is shorter than its diff:
```python
import functools
import math

import jax
import jax.numpy as jnp
from jax import lax
from jax.experimental import pallas as pl
from jax.experimental.pallas import tpu as pltpu
from jax.sharding import PartitionSpec as P

LOG2E = 1.0 / math.log(2.0)
SCALE = 3.0**0.5 / 0.15 * LOG2E
LOG2_LN2 = math.log2(math.log(2.0))
TINY = 1e-20
FEATS = 8
STORE_LIMIT = 16 * 2**20
VMEM_LIMIT = 40 * 2**20


def split(value, parts):
    out = []
    for _ in range(parts):
        part = value.astype(jnp.bfloat16).astype(jnp.float32)
        out.append(part)
        value = value - part
    return out


def row_of(shape):
    return lax.broadcasted_iota(jnp.int32, shape, 0)


def norms(feats):
    whole = feats + jnp.roll(feats, -3, axis=0)
    squares = jnp.where(row_of(feats.shape) < 3, whole * whole, 0.0)
    return split(jnp.sum(squares, axis=0, keepdims=True), 3)


def stack_rows(rows, shape):
    index = row_of(shape)
    out = jnp.zeros(shape, jnp.float32)
    for k, row in rows.items():
        out = jnp.where(index == k, row, out)
    return out


def prepare_kernel(coords_ref, intensity_ref, start_ref, packed_ref, own_ref):
    points = coords_ref.shape[1]
    shape = (FEATS, points)
    centred = (coords_ref[...] - 0.5) * SCALE
    logs = jnp.log2(intensity_ref[...])
    hi, lo = split(centred, 2)
    log_hi, log_lo = split(logs, 2)
    feats = stack_rows(
        {
            **{k: hi[k : k + 1] for k in range(3)},
            **{3 + k: lo[k : k + 1] for k in range(3)},
            6: log_hi,
            7: log_lo,
        },
        shape,
    )
    packed_ref[...] = jnp.concatenate([start_ref[...].astype(jnp.float32), feats], axis=0).astype(jnp.bfloat16)
    n1, n2, n3 = norms(feats)
    p1, p2, p3 = split(logs + LOG2_LN2, 3)
    index = row_of(shape)
    double = -2.0 * feats
    with_hi = jnp.where(index < 3, double, jnp.where(index < 6, jnp.roll(double, 3, axis=0), 0.0))
    with_lo = jnp.where(index < 3, jnp.roll(double, -3, axis=0), jnp.where(index < 6, double, 0.0))
    with_norm = stack_rows({0: 1.0, 1: 1.0, 2: 1.0, 3: n1, 4: n2, 5: n3}, shape)
    with_log = stack_rows({6: 1.0, 7: 1.0}, shape)
    with_own = stack_rows({3: p1, 4: p2, 5: p3}, shape)
    distance = jnp.concatenate([with_hi, with_lo, with_norm], axis=0)
    weight = jnp.concatenate([with_log, jnp.zeros(shape, jnp.float32), with_own], axis=0)
    own_ref[...] = jnp.concatenate([distance, weight], axis=1).astype(jnp.bfloat16)


def prepare(coords, intensity, start):
    points = coords.shape[1]
    columns = start.shape[0]
    return pl.pallas_call(
        prepare_kernel,
        out_shape=(
            jax.ShapeDtypeStruct((columns + FEATS, points), jnp.bfloat16),
            jax.ShapeDtypeStruct((3 * FEATS, 2 * points), jnp.bfloat16),
        ),
        name="prepare",
    )(coords, intensity[None], start)


def block_product(packed, vectors, own_ref, cov_ref, first):
    points = packed.shape[1]
    columns = packed.shape[0] - FEATS
    feats = packed[columns:].astype(jnp.float32)
    n1, n2, n3 = norms(feats)
    with_norm = stack_rows({0: n1, 1: n2, 2: n3, 3: 1.0, 4: 1.0, 5: 1.0}, feats.shape)
    left = jnp.concatenate([feats, feats, with_norm], axis=0).astype(jnp.bfloat16)
    step = min(128, points)
    total = None
    for at in range(0, points, step):
        both = lax.dot_general(
            left[:, at : at + step], own_ref[...], (((0,), (0,)), ((), ())), preferred_element_type=jnp.float32
        )
        squared = jnp.maximum(both[:, :points], TINY)
        scaled = squared * lax.rsqrt(squared)
        value = (scaled + LOG2E) * jnp.exp2(both[:, points:] - scaled)
        tile = value.astype(jnp.bfloat16)
        if cov_ref is not None:
            cov_ref[pl.ds(first + at, step), :] = tile
        term = jnp.dot(vectors[:, at : at + step], tile, preferred_element_type=jnp.float32)
        total = term if total is None else total + term
    return total


def covariance_kernel(count, store, *refs):
    packed_refs, own_ref, sum_ref, out_ref = refs[:count], refs[count], refs[count + 1], refs[count + 2]
    cov_ref = refs[count + 3] if store else None
    points = own_ref.shape[1] // 2
    columns = sum_ref.shape[0]
    out_ref[...] = sum_ref[...]
    done = 0
    for ref in packed_refs:
        blocks = ref.shape[0]

        def step(k, carry, ref=ref, done=done):
            packed = ref[k]
            first = pl.multiple_of((done + k) * points, points)
            out_ref[...] += block_product(packed, packed[:columns], own_ref, cov_ref, first)
            return carry

        lax.fori_loop(0, blocks, step, 0)
        done += blocks


def covariance(packed, own, running, store):
    points = own.shape[1] // 2
    columns = running.shape[0]
    blocks = sum(p.shape[0] for p in packed)
    out_shape = [jax.ShapeDtypeStruct((columns, points), jnp.float32)]
    if store:
        out_shape.append(pltpu.VMEM((blocks * points, points), jnp.bfloat16))
    elements = blocks * points * points
    return pl.pallas_call(
        functools.partial(covariance_kernel, len(packed), store),
        out_shape=out_shape,
        compiler_params=pltpu.CompilerParams(vmem_limit_bytes=VMEM_LIMIT),
        cost_estimate=pl.CostEstimate(flops=8 * elements, bytes_accessed=2 * elements, transcendentals=2 * elements),
        name="covariance",
    )(*packed, own, running)


def gram_of(product):
    return lax.dot_general(
        product, product, (((1,), (1,)), ((), ())), precision=lax.Precision.HIGHEST, preferred_element_type=jnp.float32
    )


def second_kernel(count, *refs):
    vector_refs, cov_refs = refs[:count], refs[count : 2 * count]
    first_ref, out_ref, gram_ref = refs[2 * count :]
    points = out_ref.shape[1]
    columns = out_ref.shape[0]
    total = jnp.zeros(out_ref.shape, jnp.float32)
    for vectors, cov in zip(vector_refs, cov_refs):
        for k in range(vectors.shape[0]):
            total += jnp.dot(vectors[k], cov[pl.ds(k * points, points), :], preferred_element_type=jnp.float32)
    out_ref[...] = total
    gram_ref[:columns] = gram_of(total)
    gram_ref[columns:] = gram_of(first_ref[...])


def second(vectors, covs, first):
    columns, points = first.shape
    return pl.pallas_call(
        functools.partial(second_kernel, len(vectors)),
        out_shape=(
            jax.ShapeDtypeStruct((columns, points), jnp.float32),
            jax.ShapeDtypeStruct((2 * columns, columns), jnp.float32),
        ),
        compiler_params=pltpu.CompilerParams(vmem_limit_bytes=VMEM_LIMIT),
        name="second",
    )(*vectors, *covs, first)


def grams_kernel(second_ref, first_ref, gram_ref):
    columns = second_ref.shape[0]
    gram_ref[:columns] = gram_of(second_ref[...])
    gram_ref[columns:] = gram_of(first_ref[...])


def grams(second_product, first):
    columns = first.shape[0]
    return pl.pallas_call(
        grams_kernel, out_shape=jax.ShapeDtypeStruct((2 * columns, columns), jnp.float32), name="grams"
    )(second_product, first)


def eliminate(gram):
    size = gram.shape[0]
    wide = (size, 128)
    index = row_of(wide)
    cols = [jnp.broadcast_to(gram[:, k : k + 1], wide) for k in range(size)]
    multipliers, factor_cols = [], []
    scale = jnp.zeros(wide, jnp.float32)
    for k in range(size):
        pivot = jnp.broadcast_to(cols[k][k : k + 1], wide)
        root = 1.0 / jnp.sqrt(pivot)
        multiplier = jnp.where(index > k, cols[k] / pivot, 0.0)
        for j in range(k + 1, size):
            cols[j] = cols[j] - multiplier * jnp.broadcast_to(cols[j][k : k + 1], wide)
        multipliers.append(multiplier)
        factor_cols.append(jnp.where(index >= k, cols[k] * root, 0.0))
        scale = jnp.where(index == k, root, scale)
    return multipliers, factor_cols, scale


def finish_kernel(total_points, gram_ref, product_ref, basis_ref, factor_ref):
    size, points = product_ref.shape
    gram = gram_ref[...] / total_points
    steps, cols, scale = eliminate(gram[:size])
    first_steps, _, first_scale = eliminate(gram[size:])
    for at in range(0, points, 128):
        part = product_ref[:, at : at + 128]
        for k in range(size):
            part = part - steps[k] * part[k : k + 1]
        basis_ref[:, at : at + 128] = part * scale
    lane = lax.broadcasted_iota(jnp.int32, (size, 128), 1)
    factor = jnp.zeros((size, 128), jnp.float32)
    for k in range(size):
        factor = jnp.where(lane == k, cols[k], factor)
    for k in range(size):
        factor = factor - first_steps[k] * factor[k : k + 1]
    factor_ref[...] = (factor * first_scale)[:, :size]


def finish(gram, product, total_points):
    size, points = product.shape
    return pl.pallas_call(
        functools.partial(finish_kernel, total_points),
        out_shape=(
            jax.ShapeDtypeStruct((size, points), jnp.float32),
            jax.ShapeDtypeStruct((size, size), jnp.float32),
        ),
        name="finish",
    )(gram, product)


def rounds_of(width):
    bits = [1 << k for k in range(width.bit_length() - 1)][::-1]
    out = []
    while bits:
        take = 1 if len(bits) % 2 else 2
        group, bits = bits[:take], bits[take:]
        out.append([group[0]] if take == 1 else [group[1], group[0], group[0] + group[1]])
    return out


def exchange(value, distance, width):
    return lax.ppermute(value, "wide", [(k, k ^ distance) for k in range(width)])


def sum_all(value, width):
    for distances in rounds_of(width):
        got = [exchange(value, d, width) for d in distances]
        value = value + got[0]
        if len(got) > 1:
            value = value + (got[1] + got[2])
    return value


def gather_blocks(value, width):
    held = [value[None]]
    for distances in rounds_of(width):
        sent = held[0] if len(held) == 1 else jnp.concatenate(held, axis=0)
        held = held + [exchange(sent, d, width) for d in distances]
    return held


def body(coords, intensity, start):
    width = lax.axis_size("wide")
    columns, points = start.shape
    total_points = points * width
    packed, own = prepare(coords, intensity, start)
    zero = jnp.zeros((columns, points), jnp.float32)
    store = total_points * points * 2 <= STORE_LIMIT
    blocks = gather_blocks(packed, width)
    if store:
        running, groups, covs = zero, [], []
        rounds = len(rounds_of(width))
        at = 0
        for k in range(rounds + 1):
            size = 1 if k == 0 else len(rounds_of(width)[k - 1])
            running, cov = covariance(blocks[at : at + size], own, running, True)
            groups.append((at, size))
            covs.append(cov)
            at += size
        vectors = gather_blocks(running.astype(jnp.bfloat16), width)
        grouped = [
            vectors[a] if n == 1 else jnp.concatenate(vectors[a : a + n], axis=0) for a, n in groups
        ]
        product, gram = second(grouped, covs, running)
    else:
        everything = jnp.concatenate(blocks, axis=0)
        (running,) = covariance([everything], own, zero, False)
        vectors = jnp.concatenate(gather_blocks(running.astype(jnp.bfloat16), width), axis=0)
        again = jnp.concatenate([vectors, everything[:, columns:]], axis=1)
        (product,) = covariance([again], own, zero, False)
        gram = grams(product, running)
    return finish(sum_all(gram, width), product, float(total_points))


def solution(mesh):
    placed = (P(None, ("camp", "wide")), P(("camp", "wide")), P(None, ("camp", "wide")))
    return jax.shard_map(
        body,
        mesh=mesh,
        in_specs=placed,
        out_specs=(P(None, ("camp", "wide")), P("camp", None)),
        check_vma=False,
    )
```

time: 191 us -> 60.1 us (0.31)
  blocking collectives: 141 us -> 0 us
  matrix products: 33.9 us -> 0 us
  starting transfers between devices: 0 us -> 20.2 us
  Pallas kernels: 0 us -> 19.3 us
  waiting for transfers between devices: 0 us -> 15 us
  other arithmetic: 8.63 us -> 1.41 us
  local copies, waits for them, and re-layouts: 5.28 us -> 2.98 us
    all_gather x4 -> x0, blocking collectives: 78.8 us -> none  [the longest x2 37.4 us: body(): add_segment = lax.all_gather(vectors, 'wide', axis=1, tiled=True)]
    psum x2 -> x0, blocking collectives: 62.5 us -> none  [body(): gram = lax.psum(local_gram, 'wide') / total_points]
    dot_general x34 -> x0, matrix products: 32.9 us -> none  [the longest x32 32.6 us: apply_range(): jnp.dot(segment, block_tile.T, preferred_element_type=jnp.float32)]
    ppermute x0 -> x18, starting transfers between devices: none -> 20.2 us  [exchange(): lax.ppermute(value, 'wide', [(k, k ^ distance) for k in range(width)])]
    pallas_call x0 -> x6, Pallas kernels: none -> 19.3 us  [the longest x3 14.7 us: covariance(): pl.pallas_call(functools.partial(covariance_kernel, len(packed), store),...]
    ppermute x0 -> x18, waiting for transfers between devices: none -> 15 us  [exchange(): lax.ppermute(value, 'wide', [(k, k ^ distance) for k in range(width)])]
    another operation x10 -> x0, other arithmetic: 8.61 us -> none  [the longest x4 4.35 us: body(): lax.linalg.triangular_solve(factor_lower, product, left_side=True, lower=...]
    unnamed x6 -> x8, local copies, waits for them, and re-layouts: 0.01 us -> 2.97 us
  transfers between devices with their start and end apart: 0 -> 18, of which waited for: 0 -> 12; matrix products, arithmetic and copies ran while one was open for 0% -> 0% of each run, Pallas kernels for 0% -> 6%
where the time goes in v1:
time: 60.1 us; the launch traced here: 59.6 us
  starting transfers between devices  20.2 us (34%)
  Pallas kernels  19.3 us (32%)
  waiting for transfers between devices  15 us (25%)
  local copies, waits for them, and re-layouts  2.98 us (5%)
  other arithmetic  1.41 us (2%)
  between operations  0.71 us (1%)
    ppermute x18, starting transfers between devices, exchange(): lax.ppermute(value, 'wide', [(k, k ^ distance) for k in range(width)])  20.2 us
    ppermute x18, waiting for transfers between devices, exchange(): lax.ppermute(value, 'wide', [(k, k ^ distance) for k in range(width)])  15 us
    pallas_call x3, Pallas kernels, covariance(): pl.pallas_call(functools.partial(covariance_kernel, len(packed), store),...  14.7 us
    unnamed x8, local copies, waits for them, and re-layouts  2.97 us
    pallas_call x1, Pallas kernels, finish(): pl.pallas_call(functools.partial(finish_kernel, total_points), out_shape=...  1.82 us
    pallas_call x1, Pallas kernels, prepare(): pl.pallas_call(prepare_kernel, out_shape=(jax.ShapeDtypeStruct((columns +...  1.42 us
    pallas_call x1, Pallas kernels, second(): pl.pallas_call(functools.partial(second_kernel, len(vectors)), out_shape=...  1.39 us
  transfers between devices with their start and end apart: 18, of which 12 were waited for; matrix products, arithmetic and copies ran while one was open for 0% of the time, Pallas kernels for 6%

profile of v1, /device:TPU:0, one launch (start us, length us, event | category | flops | bytes accessed | tf_op | source)
XLA Modules:
  0.0 59.6 jit_solution(13317630707253514049)
XLA Ops:
  0.6 1.4 %prepare.1 = (bf16[24,512]{1,0:T(8,128)(2,1)}, bf16[24,1024]{1,0:T(8,128)(2,1)}) custom-call(f32[3,512]{1,0:T(4,128)} %coords_ref.1, f32[1,512]{1,0:T(1,128)} %bitcast.9, bf16[16,512]{1,0:T(8,128)(2,1)} %start_ref.1), custom_call_target="tpu_custom_call" | custom-call | tf_op jit(solution)/shard_map/prepare/pallas_call | solution.py:81
  2.0 5.0 %collective-permute-start.2 = (bf16[1,24,512]{2,1,0:T(8,128)(2,1)}, bf16[1,24,512]{2,1,0:T(8,128)(2,1)S(1)}, u32[]{:S(2)}, u32[]{:S(2)}) collective-permute-start(bf16[1,24,512]{2,1,0:T(8,128)(2,1)} %bitcast.4), channel_id=1, source_target_pairs={{0,12},{1,13},{2,14},{3,15},{4,8},{5,9},{6,10},{7,11},{8,4},{9,5},... | collective-permute-start | bytes 73736 | tf_op jit(solution)/shard_map/ppermute | solution.py:259
  7.1 0.0 collective-permute-start.1
  7.1 0.6 collective-permute-start
  7.7 1.4 %collective-permute-done.2.refs_2_ = bf16[1,24,512]{2,1,0:T(8,128)(2,1)S(1)} collective-permute-done((bf16[1,24,512]{2,1,0:T(8,128)(2,1)}, bf16[1,24,512]{2,1,0:T(8,128)(2,1)S(1)}, u32[]{:S(2)}, u32[]{:S(2)}) %collective-permute-start.2) | collective-permute-done | bytes 24608 | tf_op jit(solution)/shard_map/ppermute | solution.py:259
  9.1 2.9 %collective-permute-done.1.refs_1_ = bf16[1,24,512]{2,1,0:T(8,128)(2,1)S(1)} collective-permute-done((bf16[1,24,512]{2,1,0:T(8,128)(2,1)}, bf16[1,24,512]{2,1,0:T(8,128)(2,1)S(1)}, u32[]{:S(2)}, u32[]{:S(2)}) %collective-permute-start.1) | collective-permute-done | bytes 24608 | tf_op jit(solution)/shard_map/ppermute | solution.py:259
  12.0 0.0 collective-permute-done.refs_0_
  12.0 0.8 %pad_maximum_fusion.1 = bf16[4,24,512]{2,1,0:T(8,128)(2,1)S(1)} fusion(bf16[1,24,512]{2,1,0:T(8,128)(2,1)S(1)} %collective-permute-done.2.refs_2_, bf16[1,24,512]{2,1,0:T(8,128)(2,1)S(1)} %collective-permute-done.1.refs_1_, bf16[1,24,512]{2,1,0:T(8,128)(2,1)S(1)} %collective-permute-done.refs_0_, bf16[1,24,512]{2,1,0:T(8,128)(2,1)} %bitcast.7), kind=kLoop, calls=%fused_computation.1 | loop fusion | flops 147456 | bytes 196608 | tf_op jit(solution)/shard_map/concatenate | solution.py:274
  12.8 0.1 collective-permute-start.5
  12.9 1.6 %collective-permute-start.4 = (bf16[4,24,512]{2,1,0:T(8,128)(2,1)S(1)}, bf16[4,24,512]{2,1,0:T(8,128)(2,1)S(1)}, u32[]{:S(2)}, u32[]{:S(2)}) collective-permute-start(bf16[4,24,512]{2,1,0:T(8,128)(2,1)S(1)} %pad_maximum_fusion.1), channel_id=1, source_target_pairs={{0,2},{1,3},{2,0},{3,1},{4,6},{5,7},{6,4},{7,5},{8,10},{9,11},{10,... | collective-permute-start | bytes 294920 | tf_op jit(solution)/shard_map/ppermute | solution.py:259
  14.5 0.3 collective-permute-start.3
  14.7 0.7 %copy-done.1 = bf16[24,512]{1,0:T(8,128)(2,1)S(1)} copy-done((bf16[24,512]{1,0:T(8,128)(2,1)S(1)}, bf16[24,512]{1,0:T(8,128)(2,1)}, u32[]{:S(2)}) %copy-start.1) | copy-done | bytes 24600
  15.5 0.8 %copy-done.2 = bf16[24,1024]{1,0:T(8,128)(2,1)S(1)} copy-done((bf16[24,1024]{1,0:T(8,128)(2,1)S(1)}, bf16[24,1024]{1,0:T(8,128)(2,1)}, u32[]{:S(2)}) %copy-start.2) | copy-done | bytes 49176
  16.3 0.9 %covariance.3 = (f32[16,512]{1,0:T(8,128)S(1)}, bf16[512,512]{1,0:T(8,128)(2,1)S(1)}) custom-call(bf16[1,24,512]{2,1,0:T(8,128)(2,1)S(1)} %bitcast.8, bf16[24,1024]{1,0:T(8,128)(2,1)S(1)} %copy-done.2, f32[16,512]{1,0:T(8,128)S(1)} %broadcast_in_dim.14.refs_2_), custom_call_target="tpu_custom_call" | custom-call | flops 2097152 | bytes 524288 | tf_op jit(solution)/shard_map/covariance/pallas_call | solution.py:143
  17.2 0.8 %copy-done.3 = bf16[24,1024]{1,0:T(8,128)(2,1)S(1)} copy-done((bf16[24,1024]{1,0:T(8,128)(2,1)S(1)}, bf16[24,1024]{1,0:T(8,128)(2,1)}, u32[]{:S(2)}) %copy-start.3) | copy-done | bytes 49176
  18.0 2.4 %covariance.4 = (f32[16,512]{1,0:T(8,128)S(1)}, bf16[1536,512]{1,0:T(8,128)(2,1)S(1)}) custom-call(bf16[1,24,512]{2,1,0:T(8,128)(2,1)S(1)} %collective-permute-done.refs_0_, bf16[1,24,512]{2,1,0:T(8,128)(2,1)S(1)} %collective-permute-done.1.refs_1_, bf16[1,24,512]{2,1,0:T(8,128)(2,1)S(1)} %collective-permute-done.2.refs_2_, bf16[24,1024]{1,0:T(8,128)(2,1)S(1)} %copy-done.3, ...), custom_call_target="tpu_custom_call" | custom-call | flops 6291456 | bytes 1572864 | tf_op jit(solution)/shard_map/covariance/pallas_call | solution.py:143
  20.4 0.0 collective-permute-done.5.refs_2_
  20.4 0.0 collective-permute-done.4.refs_1_
  20.5 0.0 collective-permute-done.3.refs_0_
  20.5 11.3 %covariance.5 = (f32[16,512]{1,0:T(8,128)S(1)}, bf16[6144,512]{1,0:T(8,128)(2,1)S(1)}) custom-call(bf16[4,24,512]{2,1,0:T(8,128)(2,1)S(1)} %collective-permute-done.3.refs_0_, bf16[4,24,512]{2,1,0:T(8,128)(2,1)S(1)} %collective-permute-done.4.refs_1_, bf16[4,24,512]{2,1,0:T(8,128)(2,1)S(1)} %collective-permute-done.5.refs_2_, ...), custom_call_target="tpu_custom_call" | custom-call | flops 25165824 | bytes 6291456 | tf_op jit(solution)/shard_map/covariance/pallas_call | solution.py:143
  31.8 1.5 %collective-permute-start.8 = (bf16[1,16,512]{2,1,0:T(8,128)(2,1)S(1)}, bf16[1,16,512]{2,1,0:T(8,128)(2,1)S(1)}, u32[]{:S(2)}, u32[]{:S(2)}) collective-permute-start(bf16[1,16,512]{2,1,0:T(8,128)(2,1)S(1)} %convert_bitcast_fusion.refs_0_), channel_id=1, source_target_pairs={{0,12},{1,13},{2,14},{3,15},{4,8},{5,9},{6,10},{7,11},{8,4},{9,5},... | collective-permute-start | bytes 49160 | tf_op jit(solution)/shard_map/ppermute | solution.py:259
  33.3 0.6 %collective-permute-start.7 = (bf16[1,16,512]{2,1,0:T(8,128)(2,1)S(1)}, bf16[1,16,512]{2,1,0:T(8,128)(2,1)S(1)}, u32[]{:S(2)}, u32[]{:S(2)}) collective-permute-start(bf16[1,16,512]{2,1,0:T(8,128)(2,1)S(1)} %convert_bitcast_fusion.refs_0_), channel_id=1, source_target_pairs={{0,8},{1,9},{2,10},{3,11},{4,12},{5,13},{6,14},{7,15},{8,0},{9,1},... | collective-permute-start | bytes 49160 | tf_op jit(solution)/shard_map/ppermute | solution.py:259
  33.9 2.3 %collective-permute-start.6 = (bf16[1,16,512]{2,1,0:T(8,128)(2,1)S(1)}, bf16[1,16,512]{2,1,0:T(8,128)(2,1)S(1)}, u32[]{:S(2)}, u32[]{:S(2)}) collective-permute-start(bf16[1,16,512]{2,1,0:T(8,128)(2,1)S(1)} %convert_bitcast_fusion.refs_0_), channel_id=1, source_target_pairs={{0,4},{1,5},{2,6},{3,7},{4,0},{5,1},{6,2},{7,3},{8,12},{9,13},{10,... | collective-permute-start | bytes 49160 | tf_op jit(solution)/shard_map/ppermute | solution.py:259
  36.2 1.2 %collective-permute-done.8 = bf16[1,16,512]{2,1,0:T(8,128)(2,1)S(1)} collective-permute-done((bf16[1,16,512]{2,1,0:T(8,128)(2,1)S(1)}, bf16[1,16,512]{2,1,0:T(8,128)(2,1)S(1)}, u32[]{:S(2)}, u32[]{:S(2)}) %collective-permute-start.8) | collective-permute-done | bytes 16416 | tf_op jit(solution)/shard_map/ppermute | solution.py:259
  37.5 0.5 collective-permute-done.7
  38.0 0.1 collective-permute-done.6
  38.2 0.1 collective-permute-start.11
  38.2 1.6 %collective-permute-start.10 = (bf16[4,16,512]{2,1,0:T(8,128)(2,1)S(1)}, bf16[4,16,512]{2,1,0:T(8,128)(2,1)S(1)}, u32[]{:S(2)}, u32[]{:S(2)}) collective-permute-start(bf16[4,16,512]{2,1,0:T(8,128)(2,1)S(1)} %pad_maximum_fusion.2), channel_id=1, source_target_pairs={{0,2},{1,3},{2,0},{3,1},{4,6},{5,7},{6,4},{7,5},{8,10},{9,11},{10,... | collective-permute-start | bytes 196616 | tf_op jit(solution)/shard_map/ppermute | solution.py:259
  39.8 0.3 collective-permute-start.9
  40.1 2.5 %collective-permute-done.11 = bf16[4,16,512]{2,1,0:T(8,128)(2,1)S(1)} collective-permute-done((bf16[4,16,512]{2,1,0:T(8,128)(2,1)S(1)}, bf16[4,16,512]{2,1,0:T(8,128)(2,1)S(1)}, u32[]{:S(2)}, u32[]{:S(2)}) %collective-permute-start.11) | collective-permute-done | bytes 65568 | tf_op jit(solution)/shard_map/ppermute | solution.py:259
  42.5 1.5 %collective-permute-done.10 = bf16[4,16,512]{2,1,0:T(8,128)(2,1)S(1)} collective-permute-done((bf16[4,16,512]{2,1,0:T(8,128)(2,1)S(1)}, bf16[4,16,512]{2,1,0:T(8,128)(2,1)S(1)}, u32[]{:S(2)}, u32[]{:S(2)}) %collective-permute-start.10) | collective-permute-done | bytes 65568 | tf_op jit(solution)/shard_map/ppermute | solution.py:259
  44.0 0.0 collective-permute-done.9
  44.0 1.4 %second.1 = (f32[16,512]{1,0:T(8,128)S(1)}, f32[32,16]{1,0:T(8,128)S(1)}) custom-call(bf16[1,16,512]{2,1,0:T(8,128)(2,1)S(1)} %convert_bitcast_fusion.refs_0_, bf16[3,16,512]{2,1,0:T(8,128)(2,1)S(1)} %pad_maximum_fusion.3.refs_1_, bf16[12,16,512]{2,1,0:T(8,128)(2,1)S(1)} %pad_maximum_fusion.refs_2_, bf16[512,512]{1,0:T(8,128)(2,1)S(1)} %get-tuple-element.17.refs_3_, ...), custom_call_target="tpu_custom_call" | custom-call | tf_op jit(solution)/shard_map/second/pallas_call | solution.py:174
  45.4 0.6 %copy-done = f32[16,512]{1,0:T(8,128)} copy-done((f32[16,512]{1,0:T(8,128)}, f32[16,512]{1,0:T(8,128)S(1)}, u32[]{:S(2)}) %copy-start) | copy-done | bytes 32792
  46.1 2.4 %collective-permute-start.14 = (f32[32,16]{1,0:T(8,128)S(1)}, f32[32,16]{1,0:T(8,128)S(1)}, u32[]{:S(2)}, u32[]{:S(2)}) collective-permute-start(f32[32,16]{1,0:T(8,128)S(1)} %get-tuple-element.20), channel_id=1, source_target_pairs={{0,12},{1,13},{2,14},{3,15},{4,8},{5,9},{6,10},{7,11},{8,4},{9,5},... | collective-permute-start | bytes 6152 | tf_op jit(solution)/shard_map/ppermute | solution.py:259
  48.5 0.9 %collective-permute-start.13 = (f32[32,16]{1,0:T(8,128)S(1)}, f32[32,16]{1,0:T(8,128)S(1)}, u32[]{:S(2)}, u32[]{:S(2)}) collective-permute-start(f32[32,16]{1,0:T(8,128)S(1)} %get-tuple-element.20), channel_id=1, source_target_pairs={{0,8},{1,9},{2,10},{3,11},{4,12},{5,13},{6,14},{7,15},{8,0},{9,1},... | collective-permute-start | bytes 6152 | tf_op jit(solution)/shard_map/ppermute | solution.py:259
  49.4 1.1 %collective-permute-start.12 = (f32[32,16]{1,0:T(8,128)S(1)}, f32[32,16]{1,0:T(8,128)S(1)}, u32[]{:S(2)}, u32[]{:S(2)}) collective-permute-start(f32[32,16]{1,0:T(8,128)S(1)} %get-tuple-element.20), channel_id=1, source_target_pairs={{0,4},{1,5},{2,6},{3,7},{4,0},{5,1},{6,2},{7,3},{8,12},{9,13},{10,... | collective-permute-start | bytes 6152 | tf_op jit(solution)/shard_map/ppermute | solution.py:259
  50.5 1.2 %collective-permute-done.14 = f32[32,16]{1,0:T(8,128)S(1)} collective-permute-done((f32[32,16]{1,0:T(8,128)S(1)}, f32[32,16]{1,0:T(8,128)S(1)}, u32[]{:S(2)}, u32[]{:S(2)}) %collective-permute-start.14) | collective-permute-done | bytes 2080 | tf_op jit(solution)/shard_map/ppermute | solution.py:259
  51.6 1.5 %collective-permute-done.13 = f32[32,16]{1,0:T(8,128)S(1)} collective-permute-done((f32[32,16]{1,0:T(8,128)S(1)}, f32[32,16]{1,0:T(8,128)S(1)}, u32[]{:S(2)}, u32[]{:S(2)}) %collective-permute-start.13) | collective-permute-done | bytes 2080 | tf_op jit(solution)/shard_map/ppermute | solution.py:259
  53.1 0.2 collective-permute-done.12
  53.3 0.1 collective-permute-start.17
  53.4 0.8 %collective-permute-start.16 = (f32[32,16]{1,0:T(8,128)S(1)}, f32[32,16]{1,0:T(8,128)S(1)}, u32[]{:S(2)}, u32[]{:S(2)}) collective-permute-start(f32[32,16]{1,0:T(8,128)S(1)} %add_add_fusion.1), channel_id=1, source_target_pairs={{0,2},{1,3},{2,0},{3,1},{4,6},{5,7},{6,4},{7,5},{8,10},{9,11},{10,... | collective-permute-start | bytes 6152 | tf_op jit(solution)/shard_map/ppermute | solution.py:259
  54.1 1.1 %collective-permute-start.15 = (f32[32,16]{1,0:T(8,128)S(1)}, f32[32,16]{1,0:T(8,128)S(1)}, u32[]{:S(2)}, u32[]{:S(2)}) collective-permute-start(f32[32,16]{1,0:T(8,128)S(1)} %add_add_fusion.1), channel_id=1, source_target_pairs={{0,1},{1,0},{2,3},{3,2},{4,5},{5,4},{6,7},{7,6},{8,9},{9,8},{10,11... | collective-permute-start | bytes 6152 | tf_op jit(solution)/shard_map/ppermute | solution.py:259
  55.2 1.3 %collective-permute-done.17 = f32[32,16]{1,0:T(8,128)S(1)} collective-permute-done((f32[32,16]{1,0:T(8,128)S(1)}, f32[32,16]{1,0:T(8,128)S(1)}, u32[]{:S(2)}, u32[]{:S(2)}) %collective-permute-start.17) | collective-permute-done | bytes 2080 | tf_op jit(solution)/shard_map/ppermute | solution.py:259
  56.5 0.7 %collective-permute-done.16 = f32[32,16]{1,0:T(8,128)S(1)} collective-permute-done((f32[32,16]{1,0:T(8,128)S(1)}, f32[32,16]{1,0:T(8,128)S(1)}, u32[]{:S(2)}, u32[]{:S(2)}) %collective-permute-start.16) | collective-permute-done | bytes 2080 | tf_op jit(solution)/shard_map/ppermute | solution.py:259
  57.2 0.0 collective-permute-done.15
  57.2 0.6 %add_add_fusion.gram_ref = f32[32,16]{1,0:T(8,128)} fusion(f32[32,16]{1,0:T(8,128)S(1)} %collective-permute-done.16, f32[32,16]{1,0:T(8,128)S(1)} %collective-permute-done.17, f32[32,16]{1,0:T(8,128)S(1)} %add_add_fusion.1, f32[32,16]{1,0:T(8,128)S(1)} %collective-permute-done.15), kind=kLoop, calls=%fused_computation.4 | loop fusion | flops 1536 | bytes 10240 | tf_op jit(solution)/shard_map/add | solution.py:267
  57.8 1.8 %finish.1 = (f32[16,512]{1,0:T(8,128)}, f32[16,16]{1,0:T(8,128)}) custom-call(f32[32,16]{1,0:T(8,128)} %add_add_fusion.gram_ref, f32[16,512]{1,0:T(8,128)} %copy-done), custom_call_target="tpu_custom_call" | custom-call | tf_op jit(solution)/shard_map/finish/pallas_call | solution.py:238
  (10 shorter events, 0.1 us)
Async XLA Ops:
  2.0 7.1 %collective-permute-start.2 = (bf16[1,24,512]{2,1,0:T(8,128)(2,1)}, bf16[1,24,512]{2,1,0:T(8,128)(2,1)S(1)}, u32[]{:S(2)}, u32[]{:S(2)}) collective-permute-start(bf16[1,24,512]{2,1,0:T(8,128)(2,1)} %bitcast.4), channel_id=1, source_target_pairs={{0,12},{1,13},{2,14},{3,15},{4,8},{5,9},{6,10},{7,11},{8,4},{9,5},... | collective-permute-start | bytes 73736 | tf_op jit(solution)/shard_map/ppermute | solution.py:259
  7.1 4.9 %collective-permute-start.1 = (bf16[1,24,512]{2,1,0:T(8,128)(2,1)}, bf16[1,24,512]{2,1,0:T(8,128)(2,1)S(1)}, u32[]{:S(2)}, u32[]{:S(2)}) collective-permute-start(bf16[1,24,512]{2,1,0:T(8,128)(2,1)} %bitcast.5), channel_id=1, source_target_pairs={{0,8},{1,9},{2,10},{3,11},{4,12},{5,13},{6,14},{7,15},{8,0},{9,1},... | collective-permute-start | bytes 73736 | tf_op jit(solution)/shard_map/ppermute | solution.py:259
  7.1 4.9 %collective-permute-start = (bf16[1,24,512]{2,1,0:T(8,128)(2,1)}, bf16[1,24,512]{2,1,0:T(8,128)(2,1)S(1)}, u32[]{:S(2)}, u32[]{:S(2)}) collective-permute-start(bf16[1,24,512]{2,1,0:T(8,128)(2,1)} %bitcast.6), channel_id=1, source_target_pairs={{0,4},{1,5},{2,6},{3,7},{4,0},{5,1},{6,2},{7,3},{8,12},{9,13},{10,... | collective-permute-start | bytes 73736 | tf_op jit(solution)/shard_map/ppermute | solution.py:259
  12.8 7.7 %collective-permute-start.5 = (bf16[4,24,512]{2,1,0:T(8,128)(2,1)S(1)}, bf16[4,24,512]{2,1,0:T(8,128)(2,1)S(1)}, u32[]{:S(2)}, u32[]{:S(2)}) collective-permute-start(bf16[4,24,512]{2,1,0:T(8,128)(2,1)S(1)} %pad_maximum_fusion.1), channel_id=1, source_target_pairs={{0,3},{1,2},{2,1},{3,0},{4,7},{5,6},{6,5},{7,4},{8,11},{9,10},{10,... | collective-permute-start | bytes 294920 | tf_op jit(solution)/shard_map/ppermute | solution.py:259
  12.9 7.6 %collective-permute-start.4 = (bf16[4,24,512]{2,1,0:T(8,128)(2,1)S(1)}, bf16[4,24,512]{2,1,0:T(8,128)(2,1)S(1)}, u32[]{:S(2)}, u32[]{:S(2)}) collective-permute-start(bf16[4,24,512]{2,1,0:T(8,128)(2,1)S(1)} %pad_maximum_fusion.1), channel_id=1, source_target_pairs={{0,2},{1,3},{2,0},{3,1},{4,6},{5,7},{6,4},{7,5},{8,10},{9,11},{10,... | collective-permute-start | bytes 294920 | tf_op jit(solution)/shard_map/ppermute | solution.py:259
  14.5 6.0 %collective-permute-start.3 = (bf16[4,24,512]{2,1,0:T(8,128)(2,1)S(1)}, bf16[4,24,512]{2,1,0:T(8,128)(2,1)S(1)}, u32[]{:S(2)}, u32[]{:S(2)}) collective-permute-start(bf16[4,24,512]{2,1,0:T(8,128)(2,1)S(1)} %pad_maximum_fusion.1), channel_id=1, source_target_pairs={{0,1},{1,0},{2,3},{3,2},{4,5},{5,4},{6,7},{7,6},{8,9},{9,8},{10,11... | collective-permute-start | bytes 294920 | tf_op jit(solution)/shard_map/ppermute | solution.py:259
  14.7 0.7 %copy-start.1 = (bf16[24,512]{1,0:T(8,128)(2,1)S(1)}, bf16[24,512]{1,0:T(8,128)(2,1)}, u32[]{:S(2)}) copy-start(bf16[24,512]{1,0:T(8,128)(2,1)} %get-tuple-element.12) | copy-start | bytes 73732
  15.5 0.8 %copy-start.2 = (bf16[24,1024]{1,0:T(8,128)(2,1)S(1)}, bf16[24,1024]{1,0:T(8,128)(2,1)}, u32[]{:S(2)}) copy-start(bf16[24,1024]{1,0:T(8,128)(2,1)} %get-tuple-element.13.refs_1_.refs_3_) | copy-start | bytes 147460
  17.2 0.8 %copy-start.3 = (bf16[24,1024]{1,0:T(8,128)(2,1)S(1)}, bf16[24,1024]{1,0:T(8,128)(2,1)}, u32[]{:S(2)}) copy-start(bf16[24,1024]{1,0:T(8,128)(2,1)} %get-tuple-element.13.refs_1_.refs_3_) | copy-start | bytes 147460
  31.8 5.7 %collective-permute-start.8 = (bf16[1,16,512]{2,1,0:T(8,128)(2,1)S(1)}, bf16[1,16,512]{2,1,0:T(8,128)(2,1)S(1)}, u32[]{:S(2)}, u32[]{:S(2)}) collective-permute-start(bf16[1,16,512]{2,1,0:T(8,128)(2,1)S(1)} %convert_bitcast_fusion.refs_0_), channel_id=1, source_target_pairs={{0,12},{1,13},{2,14},{3,15},{4,8},{5,9},{6,10},{7,11},{8,4},{9,5},... | collective-permute-start | bytes 49160 | tf_op jit(solution)/shard_map/ppermute | solution.py:259
  33.3 4.7 %collective-permute-start.7 = (bf16[1,16,512]{2,1,0:T(8,128)(2,1)S(1)}, bf16[1,16,512]{2,1,0:T(8,128)(2,1)S(1)}, u32[]{:S(2)}, u32[]{:S(2)}) collective-permute-start(bf16[1,16,512]{2,1,0:T(8,128)(2,1)S(1)} %convert_bitcast_fusion.refs_0_), channel_id=1, source_target_pairs={{0,8},{1,9},{2,10},{3,11},{4,12},{5,13},{6,14},{7,15},{8,0},{9,1},... | collective-permute-start | bytes 49160 | tf_op jit(solution)/shard_map/ppermute | solution.py:259
  33.9 4.2 %collective-permute-start.6 = (bf16[1,16,512]{2,1,0:T(8,128)(2,1)S(1)}, bf16[1,16,512]{2,1,0:T(8,128)(2,1)S(1)}, u32[]{:S(2)}, u32[]{:S(2)}) collective-permute-start(bf16[1,16,512]{2,1,0:T(8,128)(2,1)S(1)} %convert_bitcast_fusion.refs_0_), channel_id=1, source_target_pairs={{0,4},{1,5},{2,6},{3,7},{4,0},{5,1},{6,2},{7,3},{8,12},{9,13},{10,... | collective-permute-start | bytes 49160 | tf_op jit(solution)/shard_map/ppermute | solution.py:259
  38.2 4.4 %collective-permute-start.11 = (bf16[4,16,512]{2,1,0:T(8,128)(2,1)S(1)}, bf16[4,16,512]{2,1,0:T(8,128)(2,1)S(1)}, u32[]{:S(2)}, u32[]{:S(2)}) collective-permute-start(bf16[4,16,512]{2,1,0:T(8,128)(2,1)S(1)} %pad_maximum_fusion.2), channel_id=1, source_target_pairs={{0,3},{1,2},{2,1},{3,0},{4,7},{5,6},{6,5},{7,4},{8,11},{9,10},{10,... | collective-permute-start | bytes 196616 | tf_op jit(solution)/shard_map/ppermute | solution.py:259
  38.2 5.8 %collective-permute-start.10 = (bf16[4,16,512]{2,1,0:T(8,128)(2,1)S(1)}, bf16[4,16,512]{2,1,0:T(8,128)(2,1)S(1)}, u32[]{:S(2)}, u32[]{:S(2)}) collective-permute-start(bf16[4,16,512]{2,1,0:T(8,128)(2,1)S(1)} %pad_maximum_fusion.2), channel_id=1, source_target_pairs={{0,2},{1,3},{2,0},{3,1},{4,6},{5,7},{6,4},{7,5},{8,10},{9,11},{10,... | collective-permute-start | bytes 196616 | tf_op jit(solution)/shard_map/ppermute | solution.py:259
  39.8 4.2 %collective-permute-start.9 = (bf16[4,16,512]{2,1,0:T(8,128)(2,1)S(1)}, bf16[4,16,512]{2,1,0:T(8,128)(2,1)S(1)}, u32[]{:S(2)}, u32[]{:S(2)}) collective-permute-start(bf16[4,16,512]{2,1,0:T(8,128)(2,1)S(1)} %pad_maximum_fusion.2), channel_id=1, source_target_pairs={{0,1},{1,0},{2,3},{3,2},{4,5},{5,4},{6,7},{7,6},{8,9},{9,8},{10,11... | collective-permute-start | bytes 196616 | tf_op jit(solution)/shard_map/ppermute | solution.py:259
  45.4 0.6 %copy-start = (f32[16,512]{1,0:T(8,128)}, f32[16,512]{1,0:T(8,128)S(1)}, u32[]{:S(2)}) copy-start(f32[16,512]{1,0:T(8,128)S(1)} %get-tuple-element.21.product_ref) | copy-start | bytes 98308
  46.1 5.5 %collective-permute-start.14 = (f32[32,16]{1,0:T(8,128)S(1)}, f32[32,16]{1,0:T(8,128)S(1)}, u32[]{:S(2)}, u32[]{:S(2)}) collective-permute-start(f32[32,16]{1,0:T(8,128)S(1)} %get-tuple-element.20), channel_id=1, source_target_pairs={{0,12},{1,13},{2,14},{3,15},{4,8},{5,9},{6,10},{7,11},{8,4},{9,5},... | collective-permute-start | bytes 6152 | tf_op jit(solution)/shard_map/ppermute | solution.py:259
  48.5 4.7 %collective-permute-start.13 = (f32[32,16]{1,0:T(8,128)S(1)}, f32[32,16]{1,0:T(8,128)S(1)}, u32[]{:S(2)}, u32[]{:S(2)}) collective-permute-start(f32[32,16]{1,0:T(8,128)S(1)} %get-tuple-element.20), channel_id=1, source_target_pairs={{0,8},{1,9},{2,10},{3,11},{4,12},{5,13},{6,14},{7,15},{8,0},{9,1},... | collective-permute-start | bytes 6152 | tf_op jit(solution)/shard_map/ppermute | solution.py:259
  49.4 3.9 %collective-permute-start.12 = (f32[32,16]{1,0:T(8,128)S(1)}, f32[32,16]{1,0:T(8,128)S(1)}, u32[]{:S(2)}, u32[]{:S(2)}) collective-permute-start(f32[32,16]{1,0:T(8,128)S(1)} %get-tuple-element.20), channel_id=1, source_target_pairs={{0,4},{1,5},{2,6},{3,7},{4,0},{5,1},{6,2},{7,3},{8,12},{9,13},{10,... | collective-permute-start | bytes 6152 | tf_op jit(solution)/shard_map/ppermute | solution.py:259
  53.3 3.2 %collective-permute-start.17 = (f32[32,16]{1,0:T(8,128)S(1)}, f32[32,16]{1,0:T(8,128)S(1)}, u32[]{:S(2)}, u32[]{:S(2)}) collective-permute-start(f32[32,16]{1,0:T(8,128)S(1)} %add_add_fusion.1), channel_id=1, source_target_pairs={{0,3},{1,2},{2,1},{3,0},{4,7},{5,6},{6,5},{7,4},{8,11},{9,10},{10,... | collective-permute-start | bytes 6152 | tf_op jit(solution)/shard_map/ppermute | solution.py:259
  53.4 3.8 %collective-permute-start.16 = (f32[32,16]{1,0:T(8,128)S(1)}, f32[32,16]{1,0:T(8,128)S(1)}, u32[]{:S(2)}, u32[]{:S(2)}) collective-permute-start(f32[32,16]{1,0:T(8,128)S(1)} %add_add_fusion.1), channel_id=1, source_target_pairs={{0,2},{1,3},{2,0},{3,1},{4,6},{5,7},{6,4},{7,5},{8,10},{9,11},{10,... | collective-permute-start | bytes 6152 | tf_op jit(solution)/shard_map/ppermute | solution.py:259
  54.1 3.0 %collective-permute-start.15 = (f32[32,16]{1,0:T(8,128)S(1)}, f32[32,16]{1,0:T(8,128)S(1)}, u32[]{:S(2)}, u32[]{:S(2)}) collective-permute-start(f32[32,16]{1,0:T(8,128)S(1)} %add_add_fusion.1), channel_id=1, source_target_pairs={{0,1},{1,0},{2,3},{3,2},{4,5},{5,4},{6,7},{7,6},{8,9},{9,8},{10,11... | collective-permute-start | bytes 6152 | tf_op jit(solution)/shard_map/ppermute | solution.py:259

commit v2 on v0

v2 whole, which is shorter than its diff:
```python
import functools
import math

import jax
import jax.numpy as jnp
from jax import lax
from jax.experimental import pallas as pl
from jax.experimental.pallas import tpu as pltpu
from jax.sharding import PartitionSpec as P

LOG2E = 1.0 / math.log(2.0)
SCALE = 3.0**0.5 / 0.15 * LOG2E
LOG2_LN2 = math.log2(math.log(2.0))
TINY = 1e-20
FEATS = 8
DEPTH = 4 * FEATS
LANES = 128
F32, BF16 = jnp.float32, jnp.bfloat16
NT = (((1,), (1,)), ((), ()))
PARAMS = pltpu.CompilerParams(vmem_limit_bytes=24 * 2**20)
SMALL = pltpu.CompilerParams(vmem_limit_bytes=8 * 2**20)


def split(value, parts):
    out = []
    for _ in range(parts):
        part = value.astype(BF16).astype(F32)
        out.append(part)
        value = value - part
    return out


def row_of(shape):
    return lax.broadcasted_iota(jnp.int32, shape, 0)


def stack_rows(rows, shape):
    index = row_of(shape)
    out = jnp.zeros(shape, F32)
    for k, row in rows.items():
        out = jnp.where(index == k, row, out)
    return out


def norms(feats):
    whole = feats + jnp.roll(feats, -3, axis=0)
    squares = jnp.where(row_of(feats.shape) < 3, whole * whole, 0.0)
    return split(jnp.sum(squares, axis=0, keepdims=True), 3)


def row_features(feats):
    shape = feats.shape
    n1, n2, n3 = norms(feats)
    p1, p2, p3 = split(feats[6:7] + feats[7:8] + LOG2_LN2, 3)
    index = row_of(shape)
    double = -2.0 * feats
    with_hi = jnp.where(index < 3, double, jnp.where(index < 6, jnp.roll(double, 3, axis=0), 0.0))
    with_lo = jnp.where(index < 3, jnp.roll(double, -3, axis=0), jnp.where(index < 6, double, 0.0))
    with_norm = stack_rows({0: 1.0, 1: 1.0, 2: 1.0, 3: n1, 4: n2, 5: n3}, shape)
    with_log = stack_rows({0: p1, 1: p2, 2: p3}, shape)
    rows = jnp.swapaxes(jnp.concatenate([with_hi, with_lo, with_norm, with_log], axis=0), 0, 1).astype(BF16)
    index = row_of((DEPTH, LANES))
    pick = jnp.where((index >= 3 * FEATS) & (index < 3 * FEATS + 3), 1.0, 0.0).astype(BF16)
    return rows, jnp.dot(rows, pick, preferred_element_type=F32)


def column_features(feats):
    n1, n2, n3 = norms(feats)
    with_norm = stack_rows({0: n1, 1: n2, 2: n3, 3: 1.0, 4: 1.0, 5: 1.0}, feats.shape)
    columns = jnp.concatenate([feats, feats, with_norm, jnp.zeros(feats.shape, F32)], axis=0).astype(BF16)
    return columns, feats[6:7] + feats[7:8]


def tile_of(rows, row_log, columns, column_log):
    points = columns.shape[1]
    squared = jnp.maximum(jnp.dot(rows, columns, preferred_element_type=F32), TINY)
    scaled = squared * lax.rsqrt(squared)
    logs = jnp.concatenate([row_log] * (points // LANES), axis=1) + column_log
    return ((scaled + LOG2E) * jnp.exp2(logs - scaled)).astype(BF16)


def prepare_kernel(coords_ref, intensity_ref, start_ref, packed_ref, feats_ref):
    hi, lo = split((coords_ref[...] - 0.5) * SCALE, 2)
    log_hi, log_lo = split(jnp.log2(intensity_ref[...]), 2)
    rows = {k: hi[k : k + 1] for k in range(3)}
    rows.update({3 + k: lo[k : k + 1] for k in range(3)})
    rows.update({6: log_hi, 7: log_lo})
    feats = stack_rows(rows, feats_ref.shape)
    packed_ref[...] = jnp.concatenate([start_ref[...].astype(F32), feats], axis=0).astype(BF16)
    feats_ref[...] = feats.astype(BF16)


def prepare(coords, intensity, start):
    columns, points = start.shape
    return pl.pallas_call(
        prepare_kernel,
        out_shape=(pltpu.VMEM((columns + FEATS, points), BF16), pltpu.VMEM((FEATS, points), BF16)),
        compiler_params=SMALL,
        name="prepare",
    )(coords, intensity[None], start)


def cost(elements):
    return pl.CostEstimate(flops=40 * elements, bytes_accessed=2 * elements, transcendentals=2 * elements)


def near_kernel(count, *refs):
    feats_refs, packed_ref = refs[:count], refs[count]
    rows_ref, logs_ref, cov_ref, part_ref = refs[count + 1 :]
    points = packed_ref.shape[1]
    size = packed_ref.shape[0] - FEATS
    packed = packed_ref[...]
    columns, column_log = column_features(packed[size:].astype(F32))
    made = [row_features(ref[...].astype(F32)) for ref in feats_refs]
    for k, (rows, row_log) in enumerate(made):
        at = slice(k * points, (k + 1) * points)
        rows_ref[at], logs_ref[at] = rows, row_log
        cov_ref[at] = tile_of(rows, row_log, columns, column_log)
        part_ref[k] = lax.dot_general(packed[:size], cov_ref[at], NT, preferred_element_type=F32)


def near(feats, packed):
    points = packed.shape[1]
    size = packed.shape[0] - FEATS
    total = len(feats) * points
    return pl.pallas_call(
        functools.partial(near_kernel, len(feats)),
        out_shape=(
            pltpu.VMEM((total, DEPTH), BF16),
            pltpu.VMEM((total, LANES), F32),
            pltpu.VMEM((total, points), BF16),
            pltpu.VMEM((len(feats), size, points), F32),
        ),
        compiler_params=PARAMS,
        cost_estimate=cost(total * points),
        name="near",
    )(*feats, packed)


def far_kernel(count, *refs):
    packed_refs = refs[:count]
    rows_ref, logs_ref, part_ref, cov_ref, sum_ref, sent_ref = refs[count:]
    points = packed_refs[0].shape[1]
    size = packed_refs[0].shape[0] - FEATS
    made = [column_features(ref[size:].astype(F32)) for ref in packed_refs]
    for k in range(part_ref.shape[0]):
        at = slice(k * points, (k + 1) * points)
        total = part_ref[k]
        for c, ref in enumerate(packed_refs):
            to = slice(c * points, (c + 1) * points)
            cov_ref[at, to] = tile_of(rows_ref[at], logs_ref[at], *made[c])
            total += lax.dot_general(ref[:size], cov_ref[at, to], NT, preferred_element_type=F32)
        sum_ref[k] = total
        sent_ref[k] = total.astype(BF16)


def far(packed, rows, logs, part):
    points = packed[0].shape[1]
    return pl.pallas_call(
        functools.partial(far_kernel, len(packed)),
        out_shape=(
            pltpu.VMEM((rows.shape[0], len(packed) * points), BF16),
            pltpu.VMEM(part.shape, F32),
            pltpu.VMEM(part.shape, BF16),
        ),
        compiler_params=PARAMS,
        cost_estimate=cost(rows.shape[0] * points * len(packed)),
        name="far",
    )(*packed, rows, logs, part)


def gram_of(product):
    return lax.dot_general(product, product, NT, precision=lax.Precision.HIGHEST, preferred_element_type=F32)


def second_kernel(own_ref, *refs):
    part_refs, near_ref, far_ref, outs, gram_ref = refs[:3], refs[3], refs[4], refs[5:-1], refs[-1]
    count, size, points = own_ref.shape
    totals = [jnp.zeros((2 * size, points), F32) for _ in outs]
    for k in range(count):
        a, b, c = (ref[k ^ (n + 1)].astype(F32) for n, ref in enumerate(part_refs))
        product = (own_ref[k] + a) + (b + c)
        if k == 0:
            gram_ref[...] = gram_of(product)
        vectors = jnp.concatenate(split(product, 2), axis=0).astype(BF16)
        at = slice(k * points, (k + 1) * points)
        for n in range(len(outs)):
            cov = near_ref[at] if n == 0 else far_ref[at, (n - 1) * points : n * points]
            totals[n] += jnp.dot(vectors, cov, preferred_element_type=F32)
    for ref, total in zip(outs, totals):
        ref[...] = total[:size] + total[size:]


def second(own, parts, near_cov, far_cov):
    _, size, points = own.shape
    blocks = 1 + far_cov.shape[1] // points
    return pl.pallas_call(
        second_kernel,
        out_shape=[pltpu.VMEM((size, points), F32)] * blocks + [pltpu.VMEM((size, size), F32)],
        compiler_params=PARAMS,
        name="second",
    )(own, *parts, near_cov, far_cov)


def gather_kernel(first_ref, own_ref, *refs):
    part_refs, (product_ref, gram_ref) = refs[:-2], refs[-2:]
    size = own_ref.shape[0]
    product = own_ref[...]
    for ref in part_refs:
        product += ref[...]
    product_ref[...] = product
    gram_ref[:size] = gram_of(product)
    gram_ref[size:] = first_ref[...]


def gather_parts(first_gram, own, parts):
    size, points = own.shape
    return pl.pallas_call(
        gather_kernel,
        out_shape=(pltpu.VMEM((size, points), F32), pltpu.VMEM((2 * size, size), F32)),
        compiler_params=SMALL,
        name="gather_parts",
    )(first_gram, own, *parts)


def row_kernel(packed_ref, feats_ref, out_ref):
    size = out_ref.shape[0]
    rows, row_log = row_features(feats_ref[...].astype(F32))
    out_ref[...] = jnp.zeros(out_ref.shape, F32)

    def step(k, carry):
        packed = packed_ref[k]
        columns, column_log = column_features(packed[size:].astype(F32))
        tile = tile_of(rows, row_log, columns, column_log)
        out_ref[...] += lax.dot_general(packed[:size], tile, NT, preferred_element_type=F32)
        return carry

    lax.fori_loop(0, packed_ref.shape[0], step, 0)


def row_product(packed, feats):
    _, rows, points = packed.shape
    return pl.pallas_call(
        row_kernel,
        out_shape=jax.ShapeDtypeStruct((rows - FEATS, points), F32),
        compiler_params=PARAMS,
        name="row_product",
    )(packed, feats)


def grams_kernel(second_ref, first_ref, gram_ref):
    size = second_ref.shape[0]
    gram_ref[:size] = gram_of(second_ref[...])
    gram_ref[size:] = gram_of(first_ref[...])


def grams(second_product, first_product):
    size = first_product.shape[0]
    return pl.pallas_call(
        grams_kernel,
        out_shape=jax.ShapeDtypeStruct((2 * size, size), F32),
        compiler_params=SMALL,
        name="grams",
    )(second_product, first_product)


def eliminate(gram):
    size = gram.shape[0]
    wide = (size, LANES)
    index = row_of(wide)
    cols = [jnp.broadcast_to(gram[:, k : k + 1], wide) for k in range(size)]
    multipliers, factor_cols = [], []
    scale = jnp.zeros(wide, F32)
    for k in range(size):
        pivot = jnp.broadcast_to(cols[k][k : k + 1], wide)
        root = 1.0 / jnp.sqrt(pivot)
        multiplier = jnp.where(index > k, cols[k] / pivot, 0.0)
        for j in range(k + 1, size):
            cols[j] = cols[j] - multiplier * jnp.broadcast_to(cols[j][k : k + 1], wide)
        multipliers.append(multiplier)
        factor_cols.append(jnp.where(index >= k, cols[k] * root, 0.0))
        scale = jnp.where(index == k, root, scale)
    return multipliers, factor_cols, scale


def finish_kernel(total_points, product_ref, *refs):
    gram_refs, (basis_ref, factor_ref) = refs[:-2], refs[-2:]
    size, points = product_ref.shape
    gram = gram_refs[0][...] + gram_refs[1][...]
    if len(gram_refs) > 2:
        gram = gram + (gram_refs[2][...] + gram_refs[3][...])
    gram = gram / total_points
    steps, cols, scale = eliminate(gram[:size])
    first_steps, _, first_scale = eliminate(gram[size:])
    for at in range(0, points, LANES):
        part = product_ref[:, at : at + LANES]
        for k in range(size):
            part = part - steps[k] * part[k : k + 1]
        basis_ref[:, at : at + LANES] = part * scale
    lane = lax.broadcasted_iota(jnp.int32, (size, LANES), 1)
    factor = jnp.zeros((size, LANES), F32)
    for k in range(size):
        factor = jnp.where(lane == k, cols[k], factor)
    for k in range(size):
        factor = factor - first_steps[k] * factor[k : k + 1]
    factor_ref[...] = (factor * first_scale)[:, :size]


def finish(product, gram_parts, total_points):
    size, points = product.shape
    return pl.pallas_call(
        functools.partial(finish_kernel, total_points),
        out_shape=(jax.ShapeDtypeStruct((size, points), F32), jax.ShapeDtypeStruct((size, size), F32)),
        compiler_params=SMALL,
        name="finish",
    )(product, *gram_parts)


def rounds_of(width):
    bits = [1 << k for k in range(width.bit_length() - 1)][::-1]
    out = []
    while bits:
        take = 1 if len(bits) % 2 else 2
        group, bits = bits[:take], bits[take:]
        out.append([group[0]] if take == 1 else [group[1], group[0], group[0] + group[1]])
    return out


def exchange(value, distance, width):
    return lax.ppermute(value, "wide", [(k, k ^ distance) for k in range(width)])


def sum_parts(value, width):
    rounds = rounds_of(width)
    for n, distances in enumerate(rounds):
        parts = [value] + [exchange(value, d, width) for d in distances]
        if n == len(rounds) - 1:
            return parts
        value = parts[0] + parts[1]
        if len(parts) > 2:
            value = value + (parts[2] + parts[3])


def gather_blocks(value, width):
    held = value[None]
    for distances in rounds_of(width):
        held = jnp.concatenate([held] + [exchange(held, d, width) for d in distances], axis=0)
    return held


def body(coords, intensity, start):
    width = lax.axis_size("wide")
    size, points = start.shape
    packed, feats = prepare(coords, intensity, start)
    rounds = rounds_of(width)
    if [len(r) for r in rounds] == [3, 3]:
        far_steps, near_steps = rounds
        near_feats = [feats] + [exchange(feats, d, width) for d in near_steps]
        far_packed = [exchange(packed, d, width) for d in far_steps]
        rows, logs, near_cov, part = near(near_feats, packed)
        far_cov, own, sent = far(far_packed, rows, logs, part)
        parts = [exchange(own if d == 1 else sent, d, width) for d in near_steps]
        *products, first_gram = second(own, parts, near_cov, far_cov)
        got = [exchange(p, d, width) for p, d in zip(products[1:], far_steps)]
        product, gram = gather_parts(first_gram, products[0], got)
    else:
        everything = gather_blocks(packed, width)
        first_product = row_product(everything, feats)
        vectors = gather_blocks(first_product.astype(BF16), width)
        product = row_product(jnp.concatenate([vectors, everything[:, size:]], axis=1), feats)
        gram = grams(product, first_product)
    return finish(product, sum_parts(gram, width), float(points * width))


def solution(mesh):
    placed = (P(None, ("camp", "wide")), P(("camp", "wide")), P(None, ("camp", "wide")))
    return jax.shard_map(
        body,
        mesh=mesh,
        in_specs=placed,
        out_specs=(P(None, ("camp", "wide")), P("camp", None)),
        check_vma=False,
    )
```

time: 191 us -> 48.9 us (0.26)
  blocking collectives: 141 us -> 0 us
  matrix products: 33.9 us -> 0 us
  starting transfers between devices: 0 us -> 20.6 us
  waiting for transfers between devices: 0 us -> 15.5 us
  Pallas kernels: 0 us -> 9.75 us
  other arithmetic: 8.63 us -> 0.01 us
  local copies, waits for them, and re-layouts: 5.28 us -> 2.09 us
    all_gather x4 -> x0, blocking collectives: 78.8 us -> none  [the longest x2 37.4 us: body(): add_segment = lax.all_gather(vectors, 'wide', axis=1, tiled=True)]
    psum x2 -> x0, blocking collectives: 62.5 us -> none  [body(): gram = lax.psum(local_gram, 'wide') / total_points]
    dot_general x34 -> x0, matrix products: 32.9 us -> none  [the longest x32 32.6 us: apply_range(): jnp.dot(segment, block_tile.T, preferred_element_type=jnp.float32)]
    ppermute x0 -> x18, starting transfers between devices: none -> 20.6 us  [exchange(): lax.ppermute(value, 'wide', [(k, k ^ distance) for k in range(width)])]
    ppermute x0 -> x18, waiting for transfers between devices: none -> 15.5 us  [exchange(): lax.ppermute(value, 'wide', [(k, k ^ distance) for k in range(width)])]
    pallas_call x0 -> x6, Pallas kernels: none -> 9.75 us  [the longest x1 5.15 us: far(): pl.pallas_call(functools.partial(far_kernel, len(packed)), out_shape=(plt...]
    another operation x10 -> x0, other arithmetic: 8.61 us -> none  [the longest x4 4.35 us: body(): lax.linalg.triangular_solve(factor_lower, product, left_side=True, lower=...]
    slice x32 -> x0, local copies, waits for them, and re-layouts: 2.75 us -> none  [kernel_tile(): squared = (left_xyz[0][:, None] - right_xyz[0][None, :]) ** 2]
  transfers between devices with their start and end apart: 0 -> 18, of which waited for: 0 -> 11; matrix products, arithmetic and copies ran while one was open for 0% -> 0% of each run, Pallas kernels for 0% -> 4%
where the time goes in v2:
time: 48.9 us; the launch traced here: 48.6 us
  starting transfers between devices  20.6 us (42%)
  waiting for transfers between devices  15.5 us (32%)
  Pallas kernels  9.75 us (20%)
  local copies, waits for them, and re-layouts  2.09 us (4%)
  between operations  0.68 us (1%)
    ppermute x18, starting transfers between devices, exchange(): lax.ppermute(value, 'wide', [(k, k ^ distance) for k in range(width)])  20.6 us
    ppermute x18, waiting for transfers between devices, exchange(): lax.ppermute(value, 'wide', [(k, k ^ distance) for k in range(width)])  15.5 us
    pallas_call x1, Pallas kernels, far(): pl.pallas_call(functools.partial(far_kernel, len(packed)), out_shape=(plt...  5.15 us
    unnamed x6, local copies, waits for them, and re-layouts  2.09 us
    pallas_call x1, Pallas kernels, near(): pl.pallas_call(functools.partial(near_kernel, len(feats)), out_shape=(plt...  2.05 us
    pallas_call x1, Pallas kernels, second(): pl.pallas_call(second_kernel, out_shape=[pltpu.VMEM((size, points), F32)]...  1.31 us
    pallas_call x1, Pallas kernels, finish(): pl.pallas_call(functools.partial(finish_kernel, total_points), out_shape=...  1.06 us
  transfers between devices with their start and end apart: 18, of which 11 were waited for; matrix products, arithmetic and copies ran while one was open for 0% of the time, Pallas kernels for 4%

profile of v2, /device:TPU:0, one launch (start us, length us, event | category | flops | bytes accessed | tf_op | source)
XLA Modules:
  0.0 48.6 jit_solution(10720995446359790030)
XLA Ops:
  0.6 0.0 copy-start
  0.6 0.7 %copy-done = bf16[16,512]{1,0:T(8,128)(2,1)S(1)} copy-done((bf16[16,512]{1,0:T(8,128)(2,1)S(1)}, bf16[16,512]{1,0:T(8,128)(2,1)}, u32[]{:S(2)}) %copy-start) | copy-done | bytes 16408
  1.3 0.0 copy-start.1
  1.4 0.7 %copy-done.1 = f32[3,512]{1,0:T(4,128)S(1)} copy-done((f32[3,512]{1,0:T(4,128)S(1)}, f32[3,512]{1,0:T(4,128)}, u32[]{:S(2)}) %copy-start.1) | copy-done | bytes 6168
  2.0 0.0 copy-start.2
  2.0 0.7 %copy-done.2 = f32[512]{0:T(512)S(1)} copy-done((f32[512]{0:T(512)S(1)}, f32[512]{0:T(512)}, u32[]{:S(2)}) %copy-start.2) | copy-done | bytes 2072
  2.8 5.1 %collective-permute-start.2 = (bf16[24,512]{1,0:T(8,128)(2,1)S(1)}, bf16[24,512]{1,0:T(8,128)(2,1)S(1)}, u32[]{:S(2)}, u32[]{:S(2)}) collective-permute-start(bf16[24,512]{1,0:T(8,128)(2,1)S(1)} %get-tuple-element.18.refs_4_), channel_id=1, source_target_pairs={{0,12},{1,13},{2,14},{3,15},{4,8},{5,9},{6,10},{7,11},{8,4},{9,5},... | collective-permute-start | bytes 73736 | tf_op jit(solution)/shard_map/ppermute | solution.py:330
  7.9 0.0 collective-permute-start.1
  7.9 0.6 %collective-permute-start = (bf16[24,512]{1,0:T(8,128)(2,1)S(1)}, bf16[24,512]{1,0:T(8,128)(2,1)S(1)}, u32[]{:S(2)}, u32[]{:S(2)}) collective-permute-start(bf16[24,512]{1,0:T(8,128)(2,1)S(1)} %get-tuple-element.18.refs_4_), channel_id=1, source_target_pairs={{0,4},{1,5},{2,6},{3,7},{4,0},{5,1},{6,2},{7,3},{8,12},{9,13},{10,... | collective-permute-start | bytes 73736 | tf_op jit(solution)/shard_map/ppermute | solution.py:330
  8.5 0.4 collective-permute-start.5
  8.9 1.3 %collective-permute-start.4 = (bf16[8,512]{1,0:T(8,128)(2,1)S(1)}, bf16[8,512]{1,0:T(8,128)(2,1)S(1)}, u32[]{:S(2)}, u32[]{:S(2)}) collective-permute-start(bf16[8,512]{1,0:T(8,128)(2,1)S(1)} %get-tuple-element.19.refs_0_), channel_id=1, source_target_pairs={{0,2},{1,3},{2,0},{3,1},{4,6},{5,7},{6,4},{7,5},{8,10},{9,11},{10,... | collective-permute-start | bytes 24584 | tf_op jit(solution)/shard_map/ppermute | solution.py:330
  10.2 1.4 %collective-permute-done.5.refs_3_ = bf16[8,512]{1,0:T(8,128)(2,1)S(1)} collective-permute-done((bf16[8,512]{1,0:T(8,128)(2,1)S(1)}, bf16[8,512]{1,0:T(8,128)(2,1)S(1)}, u32[]{:S(2)}, u32[]{:S(2)}) %collective-permute-start.5) | collective-permute-done | bytes 8224 | tf_op jit(solution)/shard_map/ppermute | solution.py:330
  11.6 0.2 collective-permute-start.3
  11.8 0.7 %collective-permute-done.4.refs_2_ = bf16[8,512]{1,0:T(8,128)(2,1)S(1)} collective-permute-done((bf16[8,512]{1,0:T(8,128)(2,1)S(1)}, bf16[8,512]{1,0:T(8,128)(2,1)S(1)}, u32[]{:S(2)}, u32[]{:S(2)}) %collective-permute-start.4) | collective-permute-done | bytes 8224 | tf_op jit(solution)/shard_map/ppermute | solution.py:330
  12.6 0.2 collective-permute-done.3.refs_1_
  12.8 2.1 %near.1 = (bf16[2048,32]{1,0:T(8,128)(2,1)S(1)}, f32[2048,128]{1,0:T(8,128)S(1)}, bf16[2048,512]{1,0:T(8,128)(2,1)S(1)}, f32[4,16,512]{2,1,0:T(8,128)S(1)}) custom-call(bf16[8,512]{1,0:T(8,128)(2,1)S(1)} %get-tuple-element.19.refs_0_, bf16[8,512]{1,0:T(8,128)(2,1)S(1)} %collective-permute-done.3.refs_1_, bf16[8,512]{1,0:T(8,128)(2,1)S(1)} %collective-permute-done.4.refs_2_, ...), custom_call_target="tpu_custom_call" | custom-call | flops 41943040 | bytes 2097152 | tf_op jit(solution)/shard_map/near/pallas_call | solution.py:126
  14.8 0.0 collective-permute-done.2.refs_2_
  14.8 0.0 collective-permute-done.1.refs_1_
  14.8 0.0 collective-permute-done.refs_0_
  14.8 5.1 %far.1 = (bf16[2048,1536]{1,0:T(8,128)(2,1)S(1)}, f32[4,16,512]{2,1,0:T(8,128)S(1)}, bf16[4,16,512]{2,1,0:T(8,128)(2,1)S(1)}) custom-call(bf16[24,512]{1,0:T(8,128)(2,1)S(1)} %collective-permute-done.refs_0_, bf16[24,512]{1,0:T(8,128)(2,1)S(1)} %collective-permute-done.1.refs_1_, bf16[24,512]{1,0:T(8,128)(2,1)S(1)} %collective-permute-done.2.refs_2_, ...), custom_call_target="tpu_custom_call" | custom-call | flops 125829120 | bytes 6291456 | tf_op jit(solution)/shard_map/far/pallas_call | solution.py:159
  20.0 0.2 collective-permute-start.6
  20.2 1.6 %collective-permute-start.8 = (bf16[4,16,512]{2,1,0:T(8,128)(2,1)S(1)}, bf16[4,16,512]{2,1,0:T(8,128)(2,1)S(1)}, u32[]{:S(2)}, u32[]{:S(2)}) collective-permute-start(bf16[4,16,512]{2,1,0:T(8,128)(2,1)S(1)} %get-tuple-element.24), channel_id=1, source_target_pairs={{0,3},{1,2},{2,1},{3,0},{4,7},{5,6},{6,5},{7,4},{8,11},{9,10},{10,... | collective-permute-start | bytes 196616 | tf_op jit(solution)/shard_map/ppermute | solution.py:330
  21.8 0.4 collective-permute-start.7
  22.1 2.1 %collective-permute-done.8.refs_2_ = bf16[4,16,512]{2,1,0:T(8,128)(2,1)S(1)} collective-permute-done((bf16[4,16,512]{2,1,0:T(8,128)(2,1)S(1)}, bf16[4,16,512]{2,1,0:T(8,128)(2,1)S(1)}, u32[]{:S(2)}, u32[]{:S(2)}) %collective-permute-start.8) | collective-permute-done | bytes 65568 | tf_op jit(solution)/shard_map/ppermute | solution.py:330
  24.3 1.8 %collective-permute-done.7.refs_1_ = bf16[4,16,512]{2,1,0:T(8,128)(2,1)S(1)} collective-permute-done((bf16[4,16,512]{2,1,0:T(8,128)(2,1)S(1)}, bf16[4,16,512]{2,1,0:T(8,128)(2,1)S(1)}, u32[]{:S(2)}, u32[]{:S(2)}) %collective-permute-start.7) | collective-permute-done | bytes 65568 | tf_op jit(solution)/shard_map/ppermute | solution.py:330
  26.1 0.0 collective-permute-done.6.refs_0_
  26.1 1.3 %second.1 = (f32[16,512]{1,0:T(8,128)S(1)}, f32[16,512]{1,0:T(8,128)S(1)}, f32[16,512]{1,0:T(8,128)S(1)}, f32[16,512]{1,0:T(8,128)S(1)}, f32[16,16]{1,0:T(8,128)S(1)}) custom-call(f32[4,16,512]{2,1,0:T(8,128)S(1)} %get-tuple-element.23.own_ref, f32[4,16,512]{2,1,0:T(8,128)S(1)} %collective-permute-done.6.refs_0_, ...), custom_call_target="tpu_custom_call" | custom-call | tf_op jit(solution)/shard_map/second/pallas_call | solution.py:197
  27.4 1.3 %collective-permute-start.9 = (f32[16,512]{1,0:T(8,128)S(1)}, f32[16,512]{1,0:T(8,128)S(1)}, u32[]{:S(2)}, u32[]{:S(2)}) collective-permute-start(f32[16,512]{1,0:T(8,128)S(1)} %get-tuple-element.29), channel_id=1, source_target_pairs={{0,4},{1,5},{2,6},{3,7},{4,0},{5,1},{6,2},{7,3},{8,12},{9,13},{10,... | collective-permute-start | bytes 98312 | tf_op jit(solution)/shard_map/ppermute | solution.py:330
  28.7 2.9 %collective-permute-start.10 = (f32[16,512]{1,0:T(8,128)S(1)}, f32[16,512]{1,0:T(8,128)S(1)}, u32[]{:S(2)}, u32[]{:S(2)}) collective-permute-start(f32[16,512]{1,0:T(8,128)S(1)} %get-tuple-element.30), channel_id=1, source_target_pairs={{0,8},{1,9},{2,10},{3,11},{4,12},{5,13},{6,14},{7,15},{8,0},{9,1},... | collective-permute-start | bytes 98312 | tf_op jit(solution)/shard_map/ppermute | solution.py:330
  31.6 0.2 collective-permute-start.11
  31.8 0.0 collective-permute-done.9.refs_0_
  31.8 2.2 %collective-permute-done.10.refs_1_ = f32[16,512]{1,0:T(8,128)S(1)} collective-permute-done((f32[16,512]{1,0:T(8,128)S(1)}, f32[16,512]{1,0:T(8,128)S(1)}, u32[]{:S(2)}, u32[]{:S(2)}) %collective-permute-start.10) | collective-permute-done | bytes 32800 | tf_op jit(solution)/shard_map/ppermute | solution.py:330
  34.0 3.3 %collective-permute-done.11.refs_2_ = f32[16,512]{1,0:T(8,128)S(1)} collective-permute-done((f32[16,512]{1,0:T(8,128)S(1)}, f32[16,512]{1,0:T(8,128)S(1)}, u32[]{:S(2)}, u32[]{:S(2)}) %collective-permute-start.11) | collective-permute-done | bytes 32800 | tf_op jit(solution)/shard_map/ppermute | solution.py:330
  37.3 0.2 gather_parts.1
  37.5 0.4 collective-permute-start.14
  37.9 0.0 collective-permute-start.13
  37.9 4.0 %collective-permute-start.12 = (f32[32,16]{1,0:T(8,128)S(1)}, f32[32,16]{1,0:T(8,128)S(1)}, u32[]{:S(2)}, u32[]{:S(2)}) collective-permute-start(f32[32,16]{1,0:T(8,128)S(1)} %get-tuple-element.33), channel_id=1, source_target_pairs={{0,4},{1,5},{2,6},{3,7},{4,0},{5,1},{6,2},{7,3},{8,12},{9,13},{10,... | collective-permute-start | bytes 6152 | tf_op jit(solution)/shard_map/ppermute | solution.py:330
  41.9 1.1 %collective-permute-done.14 = f32[32,16]{1,0:T(8,128)S(1)} collective-permute-done((f32[32,16]{1,0:T(8,128)S(1)}, f32[32,16]{1,0:T(8,128)S(1)}, u32[]{:S(2)}, u32[]{:S(2)}) %collective-permute-start.14) | collective-permute-done | bytes 2080 | tf_op jit(solution)/shard_map/ppermute | solution.py:330
  43.0 0.0 collective-permute-done.13
  43.1 0.6 %collective-permute-done.12 = f32[32,16]{1,0:T(8,128)S(1)} collective-permute-done((f32[32,16]{1,0:T(8,128)S(1)}, f32[32,16]{1,0:T(8,128)S(1)}, u32[]{:S(2)}, u32[]{:S(2)}) %collective-permute-start.12) | collective-permute-done | bytes 2080 | tf_op jit(solution)/shard_map/ppermute | solution.py:330
  43.6 0.1 collective-permute-start.17
  43.7 1.6 %collective-permute-start.16 = (f32[32,16]{1,0:T(8,128)S(1)}, f32[32,16]{1,0:T(8,128)S(1)}, u32[]{:S(2)}, u32[]{:S(2)}) collective-permute-start(f32[32,16]{1,0:T(8,128)S(1)} %add_add_fusion.refs_0_), channel_id=1, source_target_pairs={{0,2},{1,3},{2,0},{3,1},{4,6},{5,7},{6,4},{7,5},{8,10},{9,11},{10,... | collective-permute-start | bytes 6152 | tf_op jit(solution)/shard_map/ppermute | solution.py:330
  45.3 0.3 collective-permute-start.15
  45.5 1.4 %collective-permute-done.17.refs_3_ = f32[32,16]{1,0:T(8,128)S(1)} collective-permute-done((f32[32,16]{1,0:T(8,128)S(1)}, f32[32,16]{1,0:T(8,128)S(1)}, u32[]{:S(2)}, u32[]{:S(2)}) %collective-permute-start.17) | collective-permute-done | bytes 2080 | tf_op jit(solution)/shard_map/ppermute | solution.py:330
  47.0 0.5 %collective-permute-done.16.refs_2_ = f32[32,16]{1,0:T(8,128)S(1)} collective-permute-done((f32[32,16]{1,0:T(8,128)S(1)}, f32[32,16]{1,0:T(8,128)S(1)}, u32[]{:S(2)}, u32[]{:S(2)}) %collective-permute-start.16) | collective-permute-done | bytes 2080 | tf_op jit(solution)/shard_map/ppermute | solution.py:330
  47.5 0.0 collective-permute-done.15.refs_1_
  47.5 1.1 %finish.1 = (f32[16,512]{1,0:T(8,128)}, f32[16,16]{1,0:T(8,128)}) custom-call(f32[16,512]{1,0:T(8,128)S(1)} %get-tuple-element.32.product_ref, f32[32,16]{1,0:T(8,128)S(1)} %add_add_fusion.refs_0_, f32[32,16]{1,0:T(8,128)S(1)} %collective-permute-done.15.refs_1_, f32[32,16]{1,0:T(8,128)S(1)} %collective-permute-done.16.refs_2_, ...), custom_call_target="tpu_custom_call" | custom-call | tf_op jit(solution)/shard_map/finish/pallas_call | solution.py:311
  (2 shorter events, 0.0 us)
Async XLA Ops:
  0.6 0.7 %copy-start = (bf16[16,512]{1,0:T(8,128)(2,1)S(1)}, bf16[16,512]{1,0:T(8,128)(2,1)}, u32[]{:S(2)}) copy-start(bf16[16,512]{1,0:T(8,128)(2,1)} %start_ref.1) | copy-start | bytes 49156
  1.3 0.7 %copy-start.1 = (f32[3,512]{1,0:T(4,128)S(1)}, f32[3,512]{1,0:T(4,128)}, u32[]{:S(2)}) copy-start(f32[3,512]{1,0:T(4,128)} %coords_ref.1) | copy-start | bytes 18436
  2.0 0.7 %copy-start.2 = (f32[512]{0:T(512)S(1)}, f32[512]{0:T(512)}, u32[]{:S(2)}) copy-start(f32[512]{0:T(512)} %param.4) | copy-start | bytes 6148
  2.8 12.1 %collective-permute-start.2 = (bf16[24,512]{1,0:T(8,128)(2,1)S(1)}, bf16[24,512]{1,0:T(8,128)(2,1)S(1)}, u32[]{:S(2)}, u32[]{:S(2)}) collective-permute-start(bf16[24,512]{1,0:T(8,128)(2,1)S(1)} %get-tuple-element.18.refs_4_), channel_id=1, source_target_pairs={{0,12},{1,13},{2,14},{3,15},{4,8},{5,9},{6,10},{7,11},{8,4},{9,5},... | collective-permute-start | bytes 73736 | tf_op jit(solution)/shard_map/ppermute | solution.py:330
  7.9 7.0 %collective-permute-start.1 = (bf16[24,512]{1,0:T(8,128)(2,1)S(1)}, bf16[24,512]{1,0:T(8,128)(2,1)S(1)}, u32[]{:S(2)}, u32[]{:S(2)}) collective-permute-start(bf16[24,512]{1,0:T(8,128)(2,1)S(1)} %get-tuple-element.18.refs_4_), channel_id=1, source_target_pairs={{0,8},{1,9},{2,10},{3,11},{4,12},{5,13},{6,14},{7,15},{8,0},{9,1},... | collective-permute-start | bytes 73736 | tf_op jit(solution)/shard_map/ppermute | solution.py:330
  7.9 7.0 %collective-permute-start = (bf16[24,512]{1,0:T(8,128)(2,1)S(1)}, bf16[24,512]{1,0:T(8,128)(2,1)S(1)}, u32[]{:S(2)}, u32[]{:S(2)}) collective-permute-start(bf16[24,512]{1,0:T(8,128)(2,1)S(1)} %get-tuple-element.18.refs_4_), channel_id=1, source_target_pairs={{0,4},{1,5},{2,6},{3,7},{4,0},{5,1},{6,2},{7,3},{8,12},{9,13},{10,... | collective-permute-start | bytes 73736 | tf_op jit(solution)/shard_map/ppermute | solution.py:330
  8.5 3.1 %collective-permute-start.5 = (bf16[8,512]{1,0:T(8,128)(2,1)S(1)}, bf16[8,512]{1,0:T(8,128)(2,1)S(1)}, u32[]{:S(2)}, u32[]{:S(2)}) collective-permute-start(bf16[8,512]{1,0:T(8,128)(2,1)S(1)} %get-tuple-element.19.refs_0_), channel_id=1, source_target_pairs={{0,3},{1,2},{2,1},{3,0},{4,7},{5,6},{6,5},{7,4},{8,11},{9,10},{10,... | collective-permute-start | bytes 24584 | tf_op jit(solution)/shard_map/ppermute | solution.py:330
  8.9 3.7 %collective-permute-start.4 = (bf16[8,512]{1,0:T(8,128)(2,1)S(1)}, bf16[8,512]{1,0:T(8,128)(2,1)S(1)}, u32[]{:S(2)}, u32[]{:S(2)}) collective-permute-start(bf16[8,512]{1,0:T(8,128)(2,1)S(1)} %get-tuple-element.19.refs_0_), channel_id=1, source_target_pairs={{0,2},{1,3},{2,0},{3,1},{4,6},{5,7},{6,4},{7,5},{8,10},{9,11},{10,... | collective-permute-start | bytes 24584 | tf_op jit(solution)/shard_map/ppermute | solution.py:330
  11.6 1.2 %collective-permute-start.3 = (bf16[8,512]{1,0:T(8,128)(2,1)S(1)}, bf16[8,512]{1,0:T(8,128)(2,1)S(1)}, u32[]{:S(2)}, u32[]{:S(2)}) collective-permute-start(bf16[8,512]{1,0:T(8,128)(2,1)S(1)} %get-tuple-element.19.refs_0_), channel_id=1, source_target_pairs={{0,1},{1,0},{2,3},{3,2},{4,5},{5,4},{6,7},{7,6},{8,9},{9,8},{10,11... | collective-permute-start | bytes 24584 | tf_op jit(solution)/shard_map/ppermute | solution.py:330
  20.0 6.1 %collective-permute-start.6 = (f32[4,16,512]{2,1,0:T(8,128)S(1)}, f32[4,16,512]{2,1,0:T(8,128)S(1)}, u32[]{:S(2)}, u32[]{:S(2)}) collective-permute-start(f32[4,16,512]{2,1,0:T(8,128)S(1)} %get-tuple-element.23.own_ref), channel_id=1, source_target_pairs={{0,1},{1,0},{2,3},{3,2},{4,5},{5,4},{6,7},{7,6},{8,9},{9,8},{10,11... | collective-permute-start | bytes 393224 | tf_op jit(solution)/shard_map/ppermute | solution.py:330
  20.2 4.0 %collective-permute-start.8 = (bf16[4,16,512]{2,1,0:T(8,128)(2,1)S(1)}, bf16[4,16,512]{2,1,0:T(8,128)(2,1)S(1)}, u32[]{:S(2)}, u32[]{:S(2)}) collective-permute-start(bf16[4,16,512]{2,1,0:T(8,128)(2,1)S(1)} %get-tuple-element.24), channel_id=1, source_target_pairs={{0,3},{1,2},{2,1},{3,0},{4,7},{5,6},{6,5},{7,4},{8,11},{9,10},{10,... | collective-permute-start | bytes 196616 | tf_op jit(solution)/shard_map/ppermute | solution.py:330
  21.8 4.3 %collective-permute-start.7 = (bf16[4,16,512]{2,1,0:T(8,128)(2,1)S(1)}, bf16[4,16,512]{2,1,0:T(8,128)(2,1)S(1)}, u32[]{:S(2)}, u32[]{:S(2)}) collective-permute-start(bf16[4,16,512]{2,1,0:T(8,128)(2,1)S(1)} %get-tuple-element.24), channel_id=1, source_target_pairs={{0,2},{1,3},{2,0},{3,1},{4,6},{5,7},{6,4},{7,5},{8,10},{9,11},{10,... | collective-permute-start | bytes 196616 | tf_op jit(solution)/shard_map/ppermute | solution.py:330
  27.4 4.4 %collective-permute-start.9 = (f32[16,512]{1,0:T(8,128)S(1)}, f32[16,512]{1,0:T(8,128)S(1)}, u32[]{:S(2)}, u32[]{:S(2)}) collective-permute-start(f32[16,512]{1,0:T(8,128)S(1)} %get-tuple-element.29), channel_id=1, source_target_pairs={{0,4},{1,5},{2,6},{3,7},{4,0},{5,1},{6,2},{7,3},{8,12},{9,13},{10,... | collective-permute-start | bytes 98312 | tf_op jit(solution)/shard_map/ppermute | solution.py:330
  28.7 5.3 %collective-permute-start.10 = (f32[16,512]{1,0:T(8,128)S(1)}, f32[16,512]{1,0:T(8,128)S(1)}, u32[]{:S(2)}, u32[]{:S(2)}) collective-permute-start(f32[16,512]{1,0:T(8,128)S(1)} %get-tuple-element.30), channel_id=1, source_target_pairs={{0,8},{1,9},{2,10},{3,11},{4,12},{5,13},{6,14},{7,15},{8,0},{9,1},... | collective-permute-start | bytes 98312 | tf_op jit(solution)/shard_map/ppermute | solution.py:330
  31.6 5.7 %collective-permute-start.11 = (f32[16,512]{1,0:T(8,128)S(1)}, f32[16,512]{1,0:T(8,128)S(1)}, u32[]{:S(2)}, u32[]{:S(2)}) collective-permute-start(f32[16,512]{1,0:T(8,128)S(1)} %get-tuple-element.31), channel_id=1, source_target_pairs={{0,12},{1,13},{2,14},{3,15},{4,8},{5,9},{6,10},{7,11},{8,4},{9,5},... | collective-permute-start | bytes 98312 | tf_op jit(solution)/shard_map/ppermute | solution.py:330
  37.5 5.6 %collective-permute-start.14 = (f32[32,16]{1,0:T(8,128)S(1)}, f32[32,16]{1,0:T(8,128)S(1)}, u32[]{:S(2)}, u32[]{:S(2)}) collective-permute-start(f32[32,16]{1,0:T(8,128)S(1)} %get-tuple-element.33), channel_id=1, source_target_pairs={{0,12},{1,13},{2,14},{3,15},{4,8},{5,9},{6,10},{7,11},{8,4},{9,5},... | collective-permute-start | bytes 6152 | tf_op jit(solution)/shard_map/ppermute | solution.py:330
  37.9 5.2 %collective-permute-start.13 = (f32[32,16]{1,0:T(8,128)S(1)}, f32[32,16]{1,0:T(8,128)S(1)}, u32[]{:S(2)}, u32[]{:S(2)}) collective-permute-start(f32[32,16]{1,0:T(8,128)S(1)} %get-tuple-element.33), channel_id=1, source_target_pairs={{0,8},{1,9},{2,10},{3,11},{4,12},{5,13},{6,14},{7,15},{8,0},{9,1},... | collective-permute-start | bytes 6152 | tf_op jit(solution)/shard_map/ppermute | solution.py:330
  37.9 5.8 %collective-permute-start.12 = (f32[32,16]{1,0:T(8,128)S(1)}, f32[32,16]{1,0:T(8,128)S(1)}, u32[]{:S(2)}, u32[]{:S(2)}) collective-permute-start(f32[32,16]{1,0:T(8,128)S(1)} %get-tuple-element.33), channel_id=1, source_target_pairs={{0,4},{1,5},{2,6},{3,7},{4,0},{5,1},{6,2},{7,3},{8,12},{9,13},{10,... | collective-permute-start | bytes 6152 | tf_op jit(solution)/shard_map/ppermute | solution.py:330
  43.6 3.3 %collective-permute-start.17 = (f32[32,16]{1,0:T(8,128)S(1)}, f32[32,16]{1,0:T(8,128)S(1)}, u32[]{:S(2)}, u32[]{:S(2)}) collective-permute-start(f32[32,16]{1,0:T(8,128)S(1)} %add_add_fusion.refs_0_), channel_id=1, source_target_pairs={{0,3},{1,2},{2,1},{3,0},{4,7},{5,6},{6,5},{7,4},{8,11},{9,10},{10,... | collective-permute-start | bytes 6152 | tf_op jit(solution)/shard_map/ppermute | solution.py:330
  43.7 3.8 %collective-permute-start.16 = (f32[32,16]{1,0:T(8,128)S(1)}, f32[32,16]{1,0:T(8,128)S(1)}, u32[]{:S(2)}, u32[]{:S(2)}) collective-permute-start(f32[32,16]{1,0:T(8,128)S(1)} %add_add_fusion.refs_0_), channel_id=1, source_target_pairs={{0,2},{1,3},{2,0},{3,1},{4,6},{5,7},{6,4},{7,5},{8,10},{9,11},{10,... | collective-permute-start | bytes 6152 | tf_op jit(solution)/shard_map/ppermute | solution.py:330
  45.3 2.2 %collective-permute-start.15 = (f32[32,16]{1,0:T(8,128)S(1)}, f32[32,16]{1,0:T(8,128)S(1)}, u32[]{:S(2)}, u32[]{:S(2)}) collective-permute-start(f32[32,16]{1,0:T(8,128)S(1)} %add_add_fusion.refs_0_), channel_id=1, source_target_pairs={{0,1},{1,0},{2,3},{3,2},{4,5},{5,4},{6,7},{7,6},{8,9},{9,8},{10,11... | collective-permute-start | bytes 6152 | tf_op jit(solution)/shard_map/ppermute | solution.py:330

commit v3 on v2

--- a/solution.py
+++ b/solution.py
@@ -11,7 +11,7 @@
 LOG2E = 1.0 / math.log(2.0)
 SCALE = 3.0**0.5 / 0.15 * LOG2E
 LOG2_LN2 = math.log2(math.log(2.0))
-TINY = 1e-20
+SMALLEST = 1e-4
 FEATS = 8
 DEPTH = 4 * FEATS
 LANES = 128
@@ -73,13 +73,20 @@
 
 def tile_of(rows, row_log, columns, column_log):
     points = columns.shape[1]
-    squared = jnp.maximum(jnp.dot(rows, columns, preferred_element_type=F32), TINY)
-    scaled = squared * lax.rsqrt(squared)
+    squared = jnp.dot(rows, columns, preferred_element_type=F32)
+    scaled = squared * lax.rsqrt(jnp.maximum(squared, SMALLEST))
     logs = jnp.concatenate([row_log] * (points // LANES), axis=1) + column_log
     return ((scaled + LOG2E) * jnp.exp2(logs - scaled)).astype(BF16)
 
 
-def prepare_kernel(coords_ref, intensity_ref, start_ref, packed_ref, feats_ref):
+def prepare_kernel(*refs):
+    sources, (packed_ref, feats_ref), buffers, sems = refs[:3], refs[3:5], refs[5:8], refs[8]
+    copies = [pltpu.make_async_copy(a, b, sems.at[n]) for n, (a, b) in enumerate(zip(sources, buffers))]
+    for copy in copies:
+        copy.start()
+    for copy in copies:
+        copy.wait()
+    coords_ref, intensity_ref, start_ref = buffers
     hi, lo = split((coords_ref[...] - 0.5) * SCALE, 2)
     log_hi, log_lo = split(jnp.log2(intensity_ref[...]), 2)
     rows = {k: hi[k : k + 1] for k in range(3)}
@@ -94,8 +101,14 @@
     columns, points = start.shape
     return pl.pallas_call(
         prepare_kernel,
+        in_specs=[pl.BlockSpec(memory_space=pltpu.HBM)] * 3,
         out_shape=(pltpu.VMEM((columns + FEATS, points), BF16), pltpu.VMEM((FEATS, points), BF16)),
-        compiler_params=SMALL,
+        scratch_shapes=[
+            pltpu.VMEM(coords.shape, F32),
+            pltpu.VMEM((1, points), F32),
+            pltpu.VMEM(start.shape, BF16),
+            pltpu.SemaphoreType.DMA((3,)),
+        ],
         name="prepare",
     )(coords, intensity[None], start)
 
@@ -104,69 +117,68 @@
     return pl.CostEstimate(flops=40 * elements, bytes_accessed=2 * elements, transcendentals=2 * elements)
 
 
-def near_kernel(count, *refs):
-    feats_refs, packed_ref = refs[:count], refs[count]
-    rows_ref, logs_ref, cov_ref, part_ref = refs[count + 1 :]
-    points = packed_ref.shape[1]
-    size = packed_ref.shape[0] - FEATS
-    packed = packed_ref[...]
-    columns, column_log = column_features(packed[size:].astype(F32))
-    made = [row_features(ref[...].astype(F32)) for ref in feats_refs]
-    for k, (rows, row_log) in enumerate(made):
-        at = slice(k * points, (k + 1) * points)
-        rows_ref[at], logs_ref[at] = rows, row_log
-        cov_ref[at] = tile_of(rows, row_log, columns, column_log)
-        part_ref[k] = lax.dot_general(packed[:size], cov_ref[at], NT, preferred_element_type=F32)
+def near_kernel(count, feats_ref, *refs):
+    packed_refs, (columns_ref, logs_ref, cov_ref, part_ref) = refs[:count], refs[count:]
+    size, points = part_ref.shape
+    rows, row_log = row_features(feats_ref[...].astype(F32))
+    made = [column_features(ref[...].astype(F32)[size:]) for ref in packed_refs]
+    total = jnp.zeros(part_ref.shape, F32)
+    for c, ref in enumerate(packed_refs):
+        to = slice(c * points, (c + 1) * points)
+        columns_ref[:, to], logs_ref[:, to] = made[c]
+        cov_ref[:, to] = tile_of(rows, row_log, *made[c])
+        total += lax.dot_general(ref[:size], cov_ref[:, to], NT, preferred_element_type=F32)
+    part_ref[...] = total
 
 
 def near(feats, packed):
-    points = packed.shape[1]
-    size = packed.shape[0] - FEATS
-    total = len(feats) * points
-    return pl.pallas_call(
-        functools.partial(near_kernel, len(feats)),
+    rows, points = packed[0].shape
+    total = len(packed) * points
+    return pl.pallas_call(
+        functools.partial(near_kernel, len(packed)),
         out_shape=(
-            pltpu.VMEM((total, DEPTH), BF16),
-            pltpu.VMEM((total, LANES), F32),
-            pltpu.VMEM((total, points), BF16),
-            pltpu.VMEM((len(feats), size, points), F32),
+            pltpu.VMEM((DEPTH, total), BF16),
+            pltpu.VMEM((1, total), F32),
+            pltpu.VMEM((points, total), BF16),
+            pltpu.VMEM((rows - FEATS, points), F32),
         ),
         compiler_params=PARAMS,
         cost_estimate=cost(total * points),
         name="near",
-    )(*feats, packed)
-
-
-def far_kernel(count, *refs):
-    packed_refs = refs[:count]
-    rows_ref, logs_ref, part_ref, cov_ref, sum_ref, sent_ref = refs[count:]
-    points = packed_refs[0].shape[1]
-    size = packed_refs[0].shape[0] - FEATS
-    made = [column_features(ref[size:].astype(F32)) for ref in packed_refs]
-    for k in range(part_ref.shape[0]):
+    )(feats, *packed)
+
+
+def far_kernel(count, near_ref, columns_ref, logs_ref, *refs):
+    feats_refs, packed_refs, (cov_ref, sum_ref, sent_ref) = refs[:count], refs[count:-3], refs[-3:]
+    size, points = near_ref.shape
+    made = [row_features(ref[...].astype(F32)) for ref in feats_refs]
+    sum_ref[0] = near_ref[...]
+    sent_ref[0] = near_ref[...].astype(BF16)
+    for k in range(count):
         at = slice(k * points, (k + 1) * points)
-        total = part_ref[k]
+        total = jnp.zeros(near_ref.shape, F32)
         for c, ref in enumerate(packed_refs):
             to = slice(c * points, (c + 1) * points)
-            cov_ref[at, to] = tile_of(rows_ref[at], logs_ref[at], *made[c])
+            cov_ref[at, to] = tile_of(*made[k], columns_ref[:, to], logs_ref[:, to])
             total += lax.dot_general(ref[:size], cov_ref[at, to], NT, preferred_element_type=F32)
-        sum_ref[k] = total
-        sent_ref[k] = total.astype(BF16)
-
-
-def far(packed, rows, logs, part):
-    points = packed[0].shape[1]
-    return pl.pallas_call(
-        functools.partial(far_kernel, len(packed)),
+        sum_ref[k + 1] = total
+        sent_ref[k + 1] = total.astype(BF16)
+
+
+def far(near_part, columns, logs, feats, packed):
+    size, points = near_part.shape
+    rows = len(feats) * points
+    return pl.pallas_call(
+        functools.partial(far_kernel, len(feats)),
         out_shape=(
-            pltpu.VMEM((rows.shape[0], len(packed) * points), BF16),
-            pltpu.VMEM(part.shape, F32),
-            pltpu.VMEM(part.shape, BF16),
+            pltpu.VMEM((rows, columns.shape[1]), BF16),
+            pltpu.VMEM((1 + len(feats), size, points), F32),
+            pltpu.VMEM((1 + len(feats), size, points), BF16),
         ),
         compiler_params=PARAMS,
-        cost_estimate=cost(rows.shape[0] * points * len(packed)),
+        cost_estimate=cost(rows * columns.shape[1]),
         name="far",
-    )(*packed, rows, logs, part)
+    )(near_part, columns, logs, *feats, *packed)
 
 
 def gram_of(product):
@@ -183,9 +195,9 @@
         if k == 0:
             gram_ref[...] = gram_of(product)
         vectors = jnp.concatenate(split(product, 2), axis=0).astype(BF16)
-        at = slice(k * points, (k + 1) * points)
         for n in range(len(outs)):
-            cov = near_ref[at] if n == 0 else far_ref[at, (n - 1) * points : n * points]
+            to = slice(n * points, (n + 1) * points)
+            cov = near_ref[:, to] if k == 0 else far_ref[(k - 1) * points : k * points, to]
             totals[n] += jnp.dot(vectors, cov, preferred_element_type=F32)
     for ref, total in zip(outs, totals):
         ref[...] = total[:size] + total[size:]
@@ -193,7 +205,7 @@
 
 def second(own, parts, near_cov, far_cov):
     _, size, points = own.shape
-    blocks = 1 + far_cov.shape[1] // points
+    blocks = far_cov.shape[1] // points
     return pl.pallas_call(
         second_kernel,
         out_shape=[pltpu.VMEM((size, points), F32)] * blocks + [pltpu.VMEM((size, size), F32)],
@@ -331,14 +343,15 @@
 
 
 def sum_parts(value, width):
-    rounds = rounds_of(width)
+    rounds = rounds_of(width)[::-1]
+    rounds = rounds[:1] + [[d + 1 if d.bit_count() == 1 else d ^ 1 for d in r] for r in rounds[1:]]
     for n, distances in enumerate(rounds):
         parts = [value] + [exchange(value, d, width) for d in distances]
         if n == len(rounds) - 1:
             return parts
-        value = parts[0] + parts[1]
+        value = parts[1] + parts[0]
         if len(parts) > 2:
-            value = value + (parts[2] + parts[3])
+            value = value + (parts[3] + parts[2])
 
 
 def gather_blocks(value, width):
@@ -352,13 +365,12 @@
     width = lax.axis_size("wide")
     size, points = start.shape
     packed, feats = prepare(coords, intensity, start)
-    rounds = rounds_of(width)
-    if [len(r) for r in rounds] == [3, 3]:
-        far_steps, near_steps = rounds
-        near_feats = [feats] + [exchange(feats, d, width) for d in near_steps]
-        far_packed = [exchange(packed, d, width) for d in far_steps]
-        rows, logs, near_cov, part = near(near_feats, packed)
-        far_cov, own, sent = far(far_packed, rows, logs, part)
+    if width == 16:
+        near_steps, far_steps = (1, 2, 3), (8, 13, 5)
+        blocks = [packed] + [exchange(packed, d, width) for d in far_steps]
+        others = [exchange(feats, d, width) for d in near_steps]
+        features, logs, near_cov, part = near(feats, blocks)
+        far_cov, own, sent = far(part, features, logs, others, blocks)
         parts = [exchange(own if d == 1 else sent, d, width) for d in near_steps]
         *products, first_gram = second(own, parts, near_cov, far_cov)
         got = [exchange(p, d, width) for p, d in zip(products[1:], far_steps)]

time: 48.9 us -> 44.4 us (0.908)
  local copies, waits for them, and re-layouts: 2.09 us -> 0 us
  starting transfers between devices: 20.6 us -> 18.6 us
  waiting for transfers between devices: 15.5 us -> 14.3 us
  Pallas kernels: 9.75 us -> 10.6 us
    unnamed x6 -> x0, local copies, waits for them, and re-layouts: 2.09 us -> none
    ppermute x18, starting transfers between devices: 20.6 us -> 18.6 us  [exchange(): lax.ppermute(value, 'wide', [(k, k ^ distance) for k in range(width)])]
    ppermute x18, waiting for transfers between devices: 15.5 us -> 14.3 us  [exchange(): lax.ppermute(value, 'wide', [(k, k ^ distance) for k in range(width)])]
    pallas_call x3, Pallas kernels: 7.22 us -> 8.08 us  [the longest x1 5.31 us: far(): pl.pallas_call(functools.partial(far_kernel, len(feats)), out_shape=(pltp...]
  transfers between devices with their start and end apart: 18 -> 18, of which waited for: 11 -> 9; matrix products, arithmetic and copies ran while one was open for 0% -> 0% of each run, Pallas kernels for 4% -> 4%
where the time goes in v3:
time: 44.4 us; the launch traced here: 44.2 us
  starting transfers between devices  18.6 us (42%)
  waiting for transfers between devices  14.3 us (32%)
  Pallas kernels  10.6 us (24%)
  between operations  0.67 us (2%)
    ppermute x18, starting transfers between devices, exchange(): lax.ppermute(value, 'wide', [(k, k ^ distance) for k in range(width)])  18.6 us
    ppermute x18, waiting for transfers between devices, exchange(): lax.ppermute(value, 'wide', [(k, k ^ distance) for k in range(width)])  14.3 us
    pallas_call x1, Pallas kernels, far(): pl.pallas_call(functools.partial(far_kernel, len(feats)), out_shape=(pltp...  5.31 us
    pallas_call x1, Pallas kernels, near(): pl.pallas_call(functools.partial(near_kernel, len(packed)), out_shape=(pl...  1.96 us
    pallas_call x1, Pallas kernels, second(): pl.pallas_call(second_kernel, out_shape=[pltpu.VMEM((size, points), F32)]...  1.33 us
    pallas_call x1, Pallas kernels, finish(): pl.pallas_call(functools.partial(finish_kernel, total_points), out_shape=...  1.06 us
  transfers between devices with their start and end apart: 18, of which 9 were waited for; matrix products, arithmetic and copies ran while one was open for 0% of the time, Pallas kernels for 4%

profile of v3, /device:TPU:0, one launch (start us, length us, event | category | flops | bytes accessed | tf_op | source)
XLA Modules:
  0.0 44.2 jit_solution(17521726792959860916)
XLA Ops:
  0.6 0.8 %prepare.1 = (bf16[24,512]{1,0:T(8,128)(2,1)S(1)}, bf16[8,512]{1,0:T(8,128)(2,1)S(1)}) custom-call(f32[3,512]{1,0:T(4,128)} %refs_0_.1, f32[1,512]{1,0:T(1,128)} %bitcast.1, bf16[16,512]{1,0:T(8,128)(2,1)} %refs_2_.1), custom_call_target="tpu_custom_call" | custom-call | tf_op jit(solution)/shard_map/prepare/pallas_call | solution.py:102
  1.4 2.5 %collective-permute-start.2 = (bf16[24,512]{1,0:T(8,128)(2,1)S(1)}, bf16[24,512]{1,0:T(8,128)(2,1)S(1)}, u32[]{:S(2)}, u32[]{:S(2)}) collective-permute-start(bf16[24,512]{1,0:T(8,128)(2,1)S(1)} %get-tuple-element.19.refs_0_.refs_3_), channel_id=1, source_target_pairs={{0,5},{1,4},{2,7},{3,6},{4,1},{5,0},{6,3},{7,2},{8,13},{9,12},{10,... | collective-permute-start | bytes 73736 | tf_op jit(solution)/shard_map/ppermute | solution.py:342
  4.0 2.8 %collective-permute-start.1 = (bf16[24,512]{1,0:T(8,128)(2,1)S(1)}, bf16[24,512]{1,0:T(8,128)(2,1)S(1)}, u32[]{:S(2)}, u32[]{:S(2)}) collective-permute-start(bf16[24,512]{1,0:T(8,128)(2,1)S(1)} %get-tuple-element.19.refs_0_.refs_3_), channel_id=1, source_target_pairs={{0,13},{1,12},{2,15},{3,14},{4,9},{5,8},{6,11},{7,10},{8,5},{9,4},... | collective-permute-start | bytes 73736 | tf_op jit(solution)/shard_map/ppermute | solution.py:342
  6.7 0.0 collective-permute-start
  6.7 1.4 %collective-permute-start.5 = (bf16[8,512]{1,0:T(8,128)(2,1)S(1)}, bf16[8,512]{1,0:T(8,128)(2,1)S(1)}, u32[]{:S(2)}, u32[]{:S(2)}) collective-permute-start(bf16[8,512]{1,0:T(8,128)(2,1)S(1)} %get-tuple-element.18.feats_ref), channel_id=1, source_target_pairs={{0,3},{1,2},{2,1},{3,0},{4,7},{5,6},{6,5},{7,4},{8,11},{9,10},{10,... | collective-permute-start | bytes 24584 | tf_op jit(solution)/shard_map/ppermute | solution.py:342
  8.1 0.5 %collective-permute-start.4 = (bf16[8,512]{1,0:T(8,128)(2,1)S(1)}, bf16[8,512]{1,0:T(8,128)(2,1)S(1)}, u32[]{:S(2)}, u32[]{:S(2)}) collective-permute-start(bf16[8,512]{1,0:T(8,128)(2,1)S(1)} %get-tuple-element.18.feats_ref), channel_id=1, source_target_pairs={{0,2},{1,3},{2,0},{3,1},{4,6},{5,7},{6,4},{7,5},{8,10},{9,11},{10,... | collective-permute-start | bytes 24584 | tf_op jit(solution)/shard_map/ppermute | solution.py:342
  8.6 0.0 collective-permute-done.2.refs_3_.refs_6_
  8.6 0.0 collective-permute-start.3
  8.6 0.4 collective-permute-done.1.refs_2_.refs_5_
  9.0 2.7 %collective-permute-done.refs_1_.refs_4_ = bf16[24,512]{1,0:T(8,128)(2,1)S(1)} collective-permute-done((bf16[24,512]{1,0:T(8,128)(2,1)S(1)}, bf16[24,512]{1,0:T(8,128)(2,1)S(1)}, u32[]{:S(2)}, u32[]{:S(2)}) %collective-permute-start) | collective-permute-done | bytes 24608 | tf_op jit(solution)/shard_map/ppermute | solution.py:342
  11.7 2.0 %near.1 = (bf16[32,2048]{1,0:T(8,128)(2,1)S(1)}, f32[1,2048]{1,0:T(1,128)S(1)}, bf16[512,2048]{1,0:T(8,128)(2,1)S(1)}, f32[16,512]{1,0:T(8,128)S(1)}) custom-call(bf16[8,512]{1,0:T(8,128)(2,1)S(1)} %get-tuple-element.18.feats_ref, bf16[24,512]{1,0:T(8,128)(2,1)S(1)} %get-tuple-element.19.refs_0_.refs_3_, ...), custom_call_target="tpu_custom_call" | custom-call | flops 41943040 | bytes 2097152 | tf_op jit(solution)/shard_map/near/pallas_call | solution.py:137
  13.7 0.0 collective-permute-done.5.refs_2_
  13.7 0.0 collective-permute-done.4.refs_1_
  13.7 0.0 collective-permute-done.3.refs_0_
  13.7 5.3 %far.1 = (bf16[1536,2048]{1,0:T(8,128)(2,1)S(1)}, f32[4,16,512]{2,1,0:T(8,128)S(1)}, bf16[4,16,512]{2,1,0:T(8,128)(2,1)S(1)}) custom-call(f32[16,512]{1,0:T(8,128)S(1)} %get-tuple-element.20.near_ref, bf16[32,2048]{1,0:T(8,128)(2,1)S(1)} %get-tuple-element.21.columns_ref, f32[1,2048]{1,0:T(1,128)S(1)} %get-tuple-element.22.logs_ref, ...), custom_call_target="tpu_custom_call" | custom-call | flops 125829120 | bytes 6291456 | tf_op jit(solution)/shard_map/far/pallas_call | solution.py:171
  19.0 0.0 collective-permute-start.6
  19.0 1.6 %collective-permute-start.8 = (bf16[4,16,512]{2,1,0:T(8,128)(2,1)S(1)}, bf16[4,16,512]{2,1,0:T(8,128)(2,1)S(1)}, u32[]{:S(2)}, u32[]{:S(2)}) collective-permute-start(bf16[4,16,512]{2,1,0:T(8,128)(2,1)S(1)} %get-tuple-element.24), channel_id=1, source_target_pairs={{0,3},{1,2},{2,1},{3,0},{4,7},{5,6},{6,5},{7,4},{8,11},{9,10},{10,... | collective-permute-start | bytes 196616 | tf_op jit(solution)/shard_map/ppermute | solution.py:342
  20.7 0.5 %collective-permute-start.7 = (bf16[4,16,512]{2,1,0:T(8,128)(2,1)S(1)}, bf16[4,16,512]{2,1,0:T(8,128)(2,1)S(1)}, u32[]{:S(2)}, u32[]{:S(2)}) collective-permute-start(bf16[4,16,512]{2,1,0:T(8,128)(2,1)S(1)} %get-tuple-element.24), channel_id=1, source_target_pairs={{0,2},{1,3},{2,0},{3,1},{4,6},{5,7},{6,4},{7,5},{8,10},{9,11},{10,... | collective-permute-start | bytes 196616 | tf_op jit(solution)/shard_map/ppermute | solution.py:342
  21.2 1.9 %collective-permute-done.8.refs_2_ = bf16[4,16,512]{2,1,0:T(8,128)(2,1)S(1)} collective-permute-done((bf16[4,16,512]{2,1,0:T(8,128)(2,1)S(1)}, bf16[4,16,512]{2,1,0:T(8,128)(2,1)S(1)}, u32[]{:S(2)}, u32[]{:S(2)}) %collective-permute-start.8) | collective-permute-done | bytes 65568 | tf_op jit(solution)/shard_map/ppermute | solution.py:342
  23.1 1.8 %collective-permute-done.7.refs_1_ = bf16[4,16,512]{2,1,0:T(8,128)(2,1)S(1)} collective-permute-done((bf16[4,16,512]{2,1,0:T(8,128)(2,1)S(1)}, bf16[4,16,512]{2,1,0:T(8,128)(2,1)S(1)}, u32[]{:S(2)}, u32[]{:S(2)}) %collective-permute-start.7) | collective-permute-done | bytes 65568 | tf_op jit(solution)/shard_map/ppermute | solution.py:342
  24.9 0.0 collective-permute-done.6.refs_0_
  24.9 1.3 %second.1 = (f32[16,512]{1,0:T(8,128)S(1)}, f32[16,512]{1,0:T(8,128)S(1)}, f32[16,512]{1,0:T(8,128)S(1)}, f32[16,512]{1,0:T(8,128)S(1)}, f32[16,16]{1,0:T(8,128)S(1)}) custom-call(f32[4,16,512]{2,1,0:T(8,128)S(1)} %get-tuple-element.23.own_ref, f32[4,16,512]{2,1,0:T(8,128)S(1)} %collective-permute-done.6.refs_0_, ...), custom_call_target="tpu_custom_call" | custom-call | tf_op jit(solution)/shard_map/second/pallas_call | solution.py:209
  26.3 0.4 collective-permute-start.9
  26.7 0.9 %collective-permute-start.10 = (f32[16,512]{1,0:T(8,128)S(1)}, f32[16,512]{1,0:T(8,128)S(1)}, u32[]{:S(2)}, u32[]{:S(2)}) collective-permute-start(f32[16,512]{1,0:T(8,128)S(1)} %get-tuple-element.30), channel_id=1, source_target_pairs={{0,13},{1,12},{2,15},{3,14},{4,9},{5,8},{6,11},{7,10},{8,5},{9,4},... | collective-permute-start | bytes 98312 | tf_op jit(solution)/shard_map/ppermute | solution.py:342
  27.5 2.0 %collective-permute-start.11 = (f32[16,512]{1,0:T(8,128)S(1)}, f32[16,512]{1,0:T(8,128)S(1)}, u32[]{:S(2)}, u32[]{:S(2)}) collective-permute-start(f32[16,512]{1,0:T(8,128)S(1)} %get-tuple-element.31), channel_id=1, source_target_pairs={{0,5},{1,4},{2,7},{3,6},{4,1},{5,0},{6,3},{7,2},{8,13},{9,12},{10,... | collective-permute-start | bytes 98312 | tf_op jit(solution)/shard_map/ppermute | solution.py:342
  29.5 3.0 %collective-permute-done.9.refs_0_ = f32[16,512]{1,0:T(8,128)S(1)} collective-permute-done((f32[16,512]{1,0:T(8,128)S(1)}, f32[16,512]{1,0:T(8,128)S(1)}, u32[]{:S(2)}, u32[]{:S(2)}) %collective-permute-start.9) | collective-permute-done | bytes 32800 | tf_op jit(solution)/shard_map/ppermute | solution.py:342
  32.4 0.0 collective-permute-done.10.refs_1_
  32.4 0.0 collective-permute-done.11.refs_2_
  32.4 0.2 gather_parts.1
  32.6 1.5 %collective-permute-start.14 = (f32[32,16]{1,0:T(8,128)S(1)}, f32[32,16]{1,0:T(8,128)S(1)}, u32[]{:S(2)}, u32[]{:S(2)}) collective-permute-start(f32[32,16]{1,0:T(8,128)S(1)} %get-tuple-element.33), channel_id=1, source_target_pairs={{0,2},{1,3},{2,0},{3,1},{4,6},{5,7},{6,4},{7,5},{8,10},{9,11},{10,... | collective-permute-start | bytes 6152 | tf_op jit(solution)/shard_map/ppermute | solution.py:342
  34.1 0.1 collective-permute-start.13
  34.1 0.6 %collective-permute-start.12 = (f32[32,16]{1,0:T(8,128)S(1)}, f32[32,16]{1,0:T(8,128)S(1)}, u32[]{:S(2)}, u32[]{:S(2)}) collective-permute-start(f32[32,16]{1,0:T(8,128)S(1)} %get-tuple-element.33), channel_id=1, source_target_pairs={{0,1},{1,0},{2,3},{3,2},{4,5},{5,4},{6,7},{7,6},{8,9},{9,8},{10,11... | collective-permute-start | bytes 6152 | tf_op jit(solution)/shard_map/ppermute | solution.py:342
  34.8 1.6 %collective-permute-done.14 = f32[32,16]{1,0:T(8,128)S(1)} collective-permute-done((f32[32,16]{1,0:T(8,128)S(1)}, f32[32,16]{1,0:T(8,128)S(1)}, u32[]{:S(2)}, u32[]{:S(2)}) %collective-permute-start.14) | collective-permute-done | bytes 2080 | tf_op jit(solution)/shard_map/ppermute | solution.py:342
  36.4 1.0 %collective-permute-done.13 = f32[32,16]{1,0:T(8,128)S(1)} collective-permute-done((f32[32,16]{1,0:T(8,128)S(1)}, f32[32,16]{1,0:T(8,128)S(1)}, u32[]{:S(2)}, u32[]{:S(2)}) %collective-permute-start.13) | collective-permute-done | bytes 2080 | tf_op jit(solution)/shard_map/ppermute | solution.py:342
  37.3 0.0 collective-permute-done.12
  37.4 1.7 %collective-permute-start.17 = (f32[32,16]{1,0:T(8,128)S(1)}, f32[32,16]{1,0:T(8,128)S(1)}, u32[]{:S(2)}, u32[]{:S(2)}) collective-permute-start(f32[32,16]{1,0:T(8,128)S(1)} %add_add_fusion.refs_0_), channel_id=1, source_target_pairs={{0,13},{1,12},{2,15},{3,14},{4,9},{5,8},{6,11},{7,10},{8,5},{9,4},... | collective-permute-start | bytes 6152 | tf_op jit(solution)/shard_map/ppermute | solution.py:342
  39.0 0.1 collective-permute-start.16
  39.2 2.1 %collective-permute-start.15 = (f32[32,16]{1,0:T(8,128)S(1)}, f32[32,16]{1,0:T(8,128)S(1)}, u32[]{:S(2)}, u32[]{:S(2)}) collective-permute-start(f32[32,16]{1,0:T(8,128)S(1)} %add_add_fusion.refs_0_), channel_id=1, source_target_pairs={{0,5},{1,4},{2,7},{3,6},{4,1},{5,0},{6,3},{7,2},{8,13},{9,12},{10,... | collective-permute-start | bytes 6152 | tf_op jit(solution)/shard_map/ppermute | solution.py:342
  41.3 1.1 %collective-permute-done.17.refs_3_ = f32[32,16]{1,0:T(8,128)S(1)} collective-permute-done((f32[32,16]{1,0:T(8,128)S(1)}, f32[32,16]{1,0:T(8,128)S(1)}, u32[]{:S(2)}, u32[]{:S(2)}) %collective-permute-start.17) | collective-permute-done | bytes 2080 | tf_op jit(solution)/shard_map/ppermute | solution.py:342
  42.4 0.7 %collective-permute-done.16.refs_2_ = f32[32,16]{1,0:T(8,128)S(1)} collective-permute-done((f32[32,16]{1,0:T(8,128)S(1)}, f32[32,16]{1,0:T(8,128)S(1)}, u32[]{:S(2)}, u32[]{:S(2)}) %collective-permute-start.16) | collective-permute-done | bytes 2080 | tf_op jit(solution)/shard_map/ppermute | solution.py:342
  43.1 0.0 collective-permute-done.15.refs_1_
  43.1 1.1 %finish.1 = (f32[16,512]{1,0:T(8,128)}, f32[16,16]{1,0:T(8,128)}) custom-call(f32[16,512]{1,0:T(8,128)S(1)} %get-tuple-element.32.product_ref, f32[32,16]{1,0:T(8,128)S(1)} %add_add_fusion.refs_0_, f32[32,16]{1,0:T(8,128)S(1)} %collective-permute-done.15.refs_1_, f32[32,16]{1,0:T(8,128)S(1)} %collective-permute-done.16.refs_2_, ...), custom_call_target="tpu_custom_call" | custom-call | tf_op jit(solution)/shard_map/finish/pallas_call | solution.py:323
  (1 shorter events, 0.0 us)
Async XLA Ops:
  1.4 7.2 %collective-permute-start.2 = (bf16[24,512]{1,0:T(8,128)(2,1)S(1)}, bf16[24,512]{1,0:T(8,128)(2,1)S(1)}, u32[]{:S(2)}, u32[]{:S(2)}) collective-permute-start(bf16[24,512]{1,0:T(8,128)(2,1)S(1)} %get-tuple-element.19.refs_0_.refs_3_), channel_id=1, source_target_pairs={{0,5},{1,4},{2,7},{3,6},{4,1},{5,0},{6,3},{7,2},{8,13},{9,12},{10,... | collective-permute-start | bytes 73736 | tf_op jit(solution)/shard_map/ppermute | solution.py:342
  4.0 5.0 %collective-permute-start.1 = (bf16[24,512]{1,0:T(8,128)(2,1)S(1)}, bf16[24,512]{1,0:T(8,128)(2,1)S(1)}, u32[]{:S(2)}, u32[]{:S(2)}) collective-permute-start(bf16[24,512]{1,0:T(8,128)(2,1)S(1)} %get-tuple-element.19.refs_0_.refs_3_), channel_id=1, source_target_pairs={{0,13},{1,12},{2,15},{3,14},{4,9},{5,8},{6,11},{7,10},{8,5},{9,4},... | collective-permute-start | bytes 73736 | tf_op jit(solution)/shard_map/ppermute | solution.py:342
  6.7 5.0 %collective-permute-start = (bf16[24,512]{1,0:T(8,128)(2,1)S(1)}, bf16[24,512]{1,0:T(8,128)(2,1)S(1)}, u32[]{:S(2)}, u32[]{:S(2)}) collective-permute-start(bf16[24,512]{1,0:T(8,128)(2,1)S(1)} %get-tuple-element.19.refs_0_.refs_3_), channel_id=1, source_target_pairs={{0,8},{1,9},{2,10},{3,11},{4,12},{5,13},{6,14},{7,15},{8,0},{9,1},... | collective-permute-start | bytes 73736 | tf_op jit(solution)/shard_map/ppermute | solution.py:342
  6.7 7.0 %collective-permute-start.5 = (bf16[8,512]{1,0:T(8,128)(2,1)S(1)}, bf16[8,512]{1,0:T(8,128)(2,1)S(1)}, u32[]{:S(2)}, u32[]{:S(2)}) collective-permute-start(bf16[8,512]{1,0:T(8,128)(2,1)S(1)} %get-tuple-element.18.feats_ref), channel_id=1, source_target_pairs={{0,3},{1,2},{2,1},{3,0},{4,7},{5,6},{6,5},{7,4},{8,11},{9,10},{10,... | collective-permute-start | bytes 24584 | tf_op jit(solution)/shard_map/ppermute | solution.py:342
  8.1 5.6 %collective-permute-start.4 = (bf16[8,512]{1,0:T(8,128)(2,1)S(1)}, bf16[8,512]{1,0:T(8,128)(2,1)S(1)}, u32[]{:S(2)}, u32[]{:S(2)}) collective-permute-start(bf16[8,512]{1,0:T(8,128)(2,1)S(1)} %get-tuple-element.18.feats_ref), channel_id=1, source_target_pairs={{0,2},{1,3},{2,0},{3,1},{4,6},{5,7},{6,4},{7,5},{8,10},{9,11},{10,... | collective-permute-start | bytes 24584 | tf_op jit(solution)/shard_map/ppermute | solution.py:342
  8.6 5.1 %collective-permute-start.3 = (bf16[8,512]{1,0:T(8,128)(2,1)S(1)}, bf16[8,512]{1,0:T(8,128)(2,1)S(1)}, u32[]{:S(2)}, u32[]{:S(2)}) collective-permute-start(bf16[8,512]{1,0:T(8,128)(2,1)S(1)} %get-tuple-element.18.feats_ref), channel_id=1, source_target_pairs={{0,1},{1,0},{2,3},{3,2},{4,5},{5,4},{6,7},{7,6},{8,9},{9,8},{10,11... | collective-permute-start | bytes 24584 | tf_op jit(solution)/shard_map/ppermute | solution.py:342
  19.0 5.9 %collective-permute-start.6 = (f32[4,16,512]{2,1,0:T(8,128)S(1)}, f32[4,16,512]{2,1,0:T(8,128)S(1)}, u32[]{:S(2)}, u32[]{:S(2)}) collective-permute-start(f32[4,16,512]{2,1,0:T(8,128)S(1)} %get-tuple-element.23.own_ref), channel_id=1, source_target_pairs={{0,1},{1,0},{2,3},{3,2},{4,5},{5,4},{6,7},{7,6},{8,9},{9,8},{10,11... | collective-permute-start | bytes 393224 | tf_op jit(solution)/shard_map/ppermute | solution.py:342
  19.0 4.1 %collective-permute-start.8 = (bf16[4,16,512]{2,1,0:T(8,128)(2,1)S(1)}, bf16[4,16,512]{2,1,0:T(8,128)(2,1)S(1)}, u32[]{:S(2)}, u32[]{:S(2)}) collective-permute-start(bf16[4,16,512]{2,1,0:T(8,128)(2,1)S(1)} %get-tuple-element.24), channel_id=1, source_target_pairs={{0,3},{1,2},{2,1},{3,0},{4,7},{5,6},{6,5},{7,4},{8,11},{9,10},{10,... | collective-permute-start | bytes 196616 | tf_op jit(solution)/shard_map/ppermute | solution.py:342
  20.7 4.3 %collective-permute-start.7 = (bf16[4,16,512]{2,1,0:T(8,128)(2,1)S(1)}, bf16[4,16,512]{2,1,0:T(8,128)(2,1)S(1)}, u32[]{:S(2)}, u32[]{:S(2)}) collective-permute-start(bf16[4,16,512]{2,1,0:T(8,128)(2,1)S(1)} %get-tuple-element.24), channel_id=1, source_target_pairs={{0,2},{1,3},{2,0},{3,1},{4,6},{5,7},{6,4},{7,5},{8,10},{9,11},{10,... | collective-permute-start | bytes 196616 | tf_op jit(solution)/shard_map/ppermute | solution.py:342
  26.3 6.2 %collective-permute-start.9 = (f32[16,512]{1,0:T(8,128)S(1)}, f32[16,512]{1,0:T(8,128)S(1)}, u32[]{:S(2)}, u32[]{:S(2)}) collective-permute-start(f32[16,512]{1,0:T(8,128)S(1)} %get-tuple-element.29), channel_id=1, source_target_pairs={{0,8},{1,9},{2,10},{3,11},{4,12},{5,13},{6,14},{7,15},{8,0},{9,1},... | collective-permute-start | bytes 98312 | tf_op jit(solution)/shard_map/ppermute | solution.py:342
  26.7 5.8 %collective-permute-start.10 = (f32[16,512]{1,0:T(8,128)S(1)}, f32[16,512]{1,0:T(8,128)S(1)}, u32[]{:S(2)}, u32[]{:S(2)}) collective-permute-start(f32[16,512]{1,0:T(8,128)S(1)} %get-tuple-element.30), channel_id=1, source_target_pairs={{0,13},{1,12},{2,15},{3,14},{4,9},{5,8},{6,11},{7,10},{8,5},{9,4},... | collective-permute-start | bytes 98312 | tf_op jit(solution)/shard_map/ppermute | solution.py:342
  27.5 4.9 %collective-permute-start.11 = (f32[16,512]{1,0:T(8,128)S(1)}, f32[16,512]{1,0:T(8,128)S(1)}, u32[]{:S(2)}, u32[]{:S(2)}) collective-permute-start(f32[16,512]{1,0:T(8,128)S(1)} %get-tuple-element.31), channel_id=1, source_target_pairs={{0,5},{1,4},{2,7},{3,6},{4,1},{5,0},{6,3},{7,2},{8,13},{9,12},{10,... | collective-permute-start | bytes 98312 | tf_op jit(solution)/shard_map/ppermute | solution.py:342
  32.6 3.8 %collective-permute-start.14 = (f32[32,16]{1,0:T(8,128)S(1)}, f32[32,16]{1,0:T(8,128)S(1)}, u32[]{:S(2)}, u32[]{:S(2)}) collective-permute-start(f32[32,16]{1,0:T(8,128)S(1)} %get-tuple-element.33), channel_id=1, source_target_pairs={{0,2},{1,3},{2,0},{3,1},{4,6},{5,7},{6,4},{7,5},{8,10},{9,11},{10,... | collective-permute-start | bytes 6152 | tf_op jit(solution)/shard_map/ppermute | solution.py:342
  34.1 3.3 %collective-permute-start.13 = (f32[32,16]{1,0:T(8,128)S(1)}, f32[32,16]{1,0:T(8,128)S(1)}, u32[]{:S(2)}, u32[]{:S(2)}) collective-permute-start(f32[32,16]{1,0:T(8,128)S(1)} %get-tuple-element.33), channel_id=1, source_target_pairs={{0,3},{1,2},{2,1},{3,0},{4,7},{5,6},{6,5},{7,4},{8,11},{9,10},{10,... | collective-permute-start | bytes 6152 | tf_op jit(solution)/shard_map/ppermute | solution.py:342
  34.1 3.2 %collective-permute-start.12 = (f32[32,16]{1,0:T(8,128)S(1)}, f32[32,16]{1,0:T(8,128)S(1)}, u32[]{:S(2)}, u32[]{:S(2)}) collective-permute-start(f32[32,16]{1,0:T(8,128)S(1)} %get-tuple-element.33), channel_id=1, source_target_pairs={{0,1},{1,0},{2,3},{3,2},{4,5},{5,4},{6,7},{7,6},{8,9},{9,8},{10,11... | collective-permute-start | bytes 6152 | tf_op jit(solution)/shard_map/ppermute | solution.py:342
  37.4 5.0 %collective-permute-start.17 = (f32[32,16]{1,0:T(8,128)S(1)}, f32[32,16]{1,0:T(8,128)S(1)}, u32[]{:S(2)}, u32[]{:S(2)}) collective-permute-start(f32[32,16]{1,0:T(8,128)S(1)} %add_add_fusion.refs_0_), channel_id=1, source_target_pairs={{0,13},{1,12},{2,15},{3,14},{4,9},{5,8},{6,11},{7,10},{8,5},{9,4},... | collective-permute-start | bytes 6152 | tf_op jit(solution)/shard_map/ppermute | solution.py:342
  39.0 4.1 %collective-permute-start.16 = (f32[32,16]{1,0:T(8,128)S(1)}, f32[32,16]{1,0:T(8,128)S(1)}, u32[]{:S(2)}, u32[]{:S(2)}) collective-permute-start(f32[32,16]{1,0:T(8,128)S(1)} %add_add_fusion.refs_0_), channel_id=1, source_target_pairs={{0,9},{1,8},{2,11},{3,10},{4,13},{5,12},{6,15},{7,14},{8,1},{9,0},... | collective-permute-start | bytes 6152 | tf_op jit(solution)/shard_map/ppermute | solution.py:342
  39.2 3.9 %collective-permute-start.15 = (f32[32,16]{1,0:T(8,128)S(1)}, f32[32,16]{1,0:T(8,128)S(1)}, u32[]{:S(2)}, u32[]{:S(2)}) collective-permute-start(f32[32,16]{1,0:T(8,128)S(1)} %add_add_fusion.refs_0_), channel_id=1, source_target_pairs={{0,5},{1,4},{2,7},{3,6},{4,1},{5,0},{6,3},{7,2},{8,13},{9,12},{10,... | collective-permute-start | bytes 6152 | tf_op jit(solution)/shard_map/ppermute | solution.py:342

commit v4 on v3

--- a/solution.py
+++ b/solution.py
@@ -118,9 +118,10 @@
 
 
 def near_kernel(count, feats_ref, *refs):
-    packed_refs, (columns_ref, logs_ref, cov_ref, part_ref) = refs[:count], refs[count:]
+    packed_refs, (rows_ref, row_logs_ref, columns_ref, logs_ref, cov_ref, part_ref) = refs[:count], refs[count:]
     size, points = part_ref.shape
     rows, row_log = row_features(feats_ref[...].astype(F32))
+    rows_ref[...], row_logs_ref[...] = rows, row_log
     made = [column_features(ref[...].astype(F32)[size:]) for ref in packed_refs]
     total = jnp.zeros(part_ref.shape, F32)
     for c, ref in enumerate(packed_refs):
@@ -137,6 +138,8 @@
     return pl.pallas_call(
         functools.partial(near_kernel, len(packed)),
         out_shape=(
+            pltpu.VMEM((points, DEPTH), BF16),
+            pltpu.VMEM((points, LANES), F32),
             pltpu.VMEM((DEPTH, total), BF16),
             pltpu.VMEM((1, total), F32),
             pltpu.VMEM((points, total), BF16),
@@ -148,37 +151,49 @@
     )(feats, *packed)
 
 
-def far_kernel(count, near_ref, columns_ref, logs_ref, *refs):
-    feats_refs, packed_refs, (cov_ref, sum_ref, sent_ref) = refs[:count], refs[count:-3], refs[-3:]
+def far_kernel(count, near_ref, rows_ref, row_logs_ref, columns_ref, logs_ref, last_ref, *refs):
+    feats_refs, packed_refs, (edge_ref, cov_ref, sum_ref, sent_ref) = refs[:count], refs[count:-4], refs[-4:]
     size, points = near_ref.shape
     made = [row_features(ref[...].astype(F32)) for ref in feats_refs]
-    sum_ref[0] = near_ref[...]
-    sent_ref[0] = near_ref[...].astype(BF16)
+    columns, logs = [], []
+    for c in range(len(packed_refs)):
+        to = slice(c * points, (c + 1) * points)
+        columns.append(columns_ref[:, to])
+        logs.append(logs_ref[:, to])
+    last, last_log = column_features(last_ref[...].astype(F32)[size:])
+    columns.append(last)
+    logs.append(last_log)
+    sources = list(packed_refs) + [last_ref]
+    edge_ref[...] = tile_of(rows_ref[...], row_logs_ref[...], last, last_log)
+    total = near_ref[...] + lax.dot_general(last_ref[:size], edge_ref[...], NT, preferred_element_type=F32)
+    sum_ref[0] = total
+    sent_ref[0] = total.astype(BF16)
     for k in range(count):
         at = slice(k * points, (k + 1) * points)
         total = jnp.zeros(near_ref.shape, F32)
-        for c, ref in enumerate(packed_refs):
+        for c, ref in enumerate(sources):
             to = slice(c * points, (c + 1) * points)
-            cov_ref[at, to] = tile_of(*made[k], columns_ref[:, to], logs_ref[:, to])
+            cov_ref[at, to] = tile_of(*made[k], columns[c], logs[c])
             total += lax.dot_general(ref[:size], cov_ref[at, to], NT, preferred_element_type=F32)
         sum_ref[k + 1] = total
         sent_ref[k + 1] = total.astype(BF16)
 
 
-def far(near_part, columns, logs, feats, packed):
+def far(near_part, rows, row_logs, columns, logs, feats, packed, last):
     size, points = near_part.shape
-    rows = len(feats) * points
+    height, wide = len(feats) * points, (len(packed) + 1) * points
     return pl.pallas_call(
         functools.partial(far_kernel, len(feats)),
         out_shape=(
-            pltpu.VMEM((rows, columns.shape[1]), BF16),
+            pltpu.VMEM((points, points), BF16),
+            pltpu.VMEM((height, wide), BF16),
             pltpu.VMEM((1 + len(feats), size, points), F32),
             pltpu.VMEM((1 + len(feats), size, points), BF16),
         ),
         compiler_params=PARAMS,
-        cost_estimate=cost(rows * columns.shape[1]),
+        cost_estimate=cost((height + points) * wide),
         name="far",
-    )(near_part, columns, logs, *feats, *packed)
+    )(near_part, rows, row_logs, columns, logs, last, *feats, *packed)
 
 
 def gram_of(product):
@@ -186,7 +201,7 @@
 
 
 def second_kernel(own_ref, *refs):
-    part_refs, near_ref, far_ref, outs, gram_ref = refs[:3], refs[3], refs[4], refs[5:-1], refs[-1]
+    part_refs, near_ref, edge_ref, far_ref, outs, gram_ref = refs[:3], refs[3], refs[4], refs[5], refs[6:-1], refs[-1]
     count, size, points = own_ref.shape
     totals = [jnp.zeros((2 * size, points), F32) for _ in outs]
     for k in range(count):
@@ -197,13 +212,16 @@
         vectors = jnp.concatenate(split(product, 2), axis=0).astype(BF16)
         for n in range(len(outs)):
             to = slice(n * points, (n + 1) * points)
-            cov = near_ref[:, to] if k == 0 else far_ref[(k - 1) * points : k * points, to]
+            if k == 0:
+                cov = near_ref[:, to] if n < len(outs) - 1 else edge_ref[...]
+            else:
+                cov = far_ref[(k - 1) * points : k * points, to]
             totals[n] += jnp.dot(vectors, cov, preferred_element_type=F32)
     for ref, total in zip(outs, totals):
         ref[...] = total[:size] + total[size:]
 
 
-def second(own, parts, near_cov, far_cov):
+def second(own, parts, near_cov, edge_cov, far_cov):
     _, size, points = own.shape
     blocks = far_cov.shape[1] // points
     return pl.pallas_call(
@@ -211,7 +229,7 @@
         out_shape=[pltpu.VMEM((size, points), F32)] * blocks + [pltpu.VMEM((size, size), F32)],
         compiler_params=PARAMS,
         name="second",
-    )(own, *parts, near_cov, far_cov)
+    )(own, *parts, near_cov, edge_cov, far_cov)
 
 
 def gather_kernel(first_ref, own_ref, *refs):
@@ -369,10 +387,10 @@
         near_steps, far_steps = (1, 2, 3), (8, 13, 5)
         blocks = [packed] + [exchange(packed, d, width) for d in far_steps]
         others = [exchange(feats, d, width) for d in near_steps]
-        features, logs, near_cov, part = near(feats, blocks)
-        far_cov, own, sent = far(part, features, logs, others, blocks)
+        *features, near_cov, part = near(feats, blocks[:-1])
+        edge_cov, far_cov, own, sent = far(part, *features, others, blocks[:-1], blocks[-1])
         parts = [exchange(own if d == 1 else sent, d, width) for d in near_steps]
-        *products, first_gram = second(own, parts, near_cov, far_cov)
+        *products, first_gram = second(own, parts, near_cov, edge_cov, far_cov)
         got = [exchange(p, d, width) for p, d in zip(products[1:], far_steps)]
         product, gram = gather_parts(first_gram, products[0], got)
     else:

time: 44.4 us -> 43.4 us (0.977)
  waiting for transfers between devices: 14.3 us -> 13 us
    ppermute x18, waiting for transfers between devices: 14.3 us -> 13 us  [exchange(): lax.ppermute(value, 'wide', [(k, k ^ distance) for k in range(width)])]
where the time goes in v4:
time: 43.4 us; the launch traced here: 43.2 us
  starting transfers between devices  19 us (44%)
  waiting for transfers between devices  13 us (30%)
  Pallas kernels  10.6 us (24%)
  between operations  0.68 us (2%)
    ppermute x18, starting transfers between devices, exchange(): lax.ppermute(value, 'wide', [(k, k ^ distance) for k in range(width)])  19 us
    ppermute x18, waiting for transfers between devices, exchange(): lax.ppermute(value, 'wide', [(k, k ^ distance) for k in range(width)])  13 us
    pallas_call x1, Pallas kernels, far(): pl.pallas_call(functools.partial(far_kernel, len(feats)), out_shape=(pltp...  5.69 us
    pallas_call x1, Pallas kernels, near(): pl.pallas_call(functools.partial(near_kernel, len(packed)), out_shape=(pl...  1.54 us
    pallas_call x1, Pallas kernels, second(): pl.pallas_call(second_kernel, out_shape=[pltpu.VMEM((size, points), F32)]...  1.32 us
    pallas_call x1, Pallas kernels, finish(): pl.pallas_call(functools.partial(finish_kernel, total_points), out_shape=...  1.06 us
  transfers between devices with their start and end apart: 18, of which 9 were waited for; matrix products, arithmetic and copies ran while one was open for 0% of the time, Pallas kernels for 4%

profile of v4, /device:TPU:0, one launch (start us, length us, event | category | flops | bytes accessed | tf_op | source)
XLA Modules:
  0.0 43.2 jit_solution(3801409036751941493)
XLA Ops:
  0.6 0.8 %prepare.1 = (bf16[24,512]{1,0:T(8,128)(2,1)S(1)}, bf16[8,512]{1,0:T(8,128)(2,1)S(1)}) custom-call(f32[3,512]{1,0:T(4,128)} %refs_0_.1, f32[1,512]{1,0:T(1,128)} %bitcast.1, bf16[16,512]{1,0:T(8,128)(2,1)} %refs_2_.1), custom_call_target="tpu_custom_call" | custom-call | tf_op jit(solution)/shard_map/prepare/pallas_call | solution.py:102
  1.4 4.6 %collective-permute-start.1 = (bf16[24,512]{1,0:T(8,128)(2,1)S(1)}, bf16[24,512]{1,0:T(8,128)(2,1)S(1)}, u32[]{:S(2)}, u32[]{:S(2)}) collective-permute-start(bf16[24,512]{1,0:T(8,128)(2,1)S(1)} %get-tuple-element.22.refs_0_.refs_3_), channel_id=1, source_target_pairs={{0,13},{1,12},{2,15},{3,14},{4,9},{5,8},{6,11},{7,10},{8,5},{9,4},... | collective-permute-start | bytes 73736 | tf_op jit(solution)/shard_map/ppermute | solution.py:360
  6.0 0.0 collective-permute-start
  6.0 0.4 collective-permute-start.2
  6.4 2.1 %collective-permute-start.5 = (bf16[8,512]{1,0:T(8,128)(2,1)S(1)}, bf16[8,512]{1,0:T(8,128)(2,1)S(1)}, u32[]{:S(2)}, u32[]{:S(2)}) collective-permute-start(bf16[8,512]{1,0:T(8,128)(2,1)S(1)} %get-tuple-element.21.feats_ref), channel_id=1, source_target_pairs={{0,3},{1,2},{2,1},{3,0},{4,7},{5,6},{6,5},{7,4},{8,11},{9,10},{10,... | collective-permute-start | bytes 24584 | tf_op jit(solution)/shard_map/ppermute | solution.py:360
  8.4 0.5 %collective-permute-start.4 = (bf16[8,512]{1,0:T(8,128)(2,1)S(1)}, bf16[8,512]{1,0:T(8,128)(2,1)S(1)}, u32[]{:S(2)}, u32[]{:S(2)}) collective-permute-start(bf16[8,512]{1,0:T(8,128)(2,1)S(1)} %get-tuple-element.21.feats_ref), channel_id=1, source_target_pairs={{0,2},{1,3},{2,0},{3,1},{4,6},{5,7},{6,4},{7,5},{8,10},{9,11},{10,... | collective-permute-start | bytes 24584 | tf_op jit(solution)/shard_map/ppermute | solution.py:360
  8.9 0.0 collective-permute-done.1.refs_2_.refs_5_
  8.9 0.0 collective-permute-start.3
  8.9 1.8 %collective-permute-done.refs_1_.refs_4_ = bf16[24,512]{1,0:T(8,128)(2,1)S(1)} collective-permute-done((bf16[24,512]{1,0:T(8,128)(2,1)S(1)}, bf16[24,512]{1,0:T(8,128)(2,1)S(1)}, u32[]{:S(2)}, u32[]{:S(2)}) %collective-permute-start) | collective-permute-done | bytes 24608 | tf_op jit(solution)/shard_map/ppermute | solution.py:360
  10.7 1.5 %near.1 = (bf16[512,32]{1,0:T(8,128)(2,1)S(1)}, f32[512,128]{1,0:T(8,128)S(1)}, bf16[32,1536]{1,0:T(8,128)(2,1)S(1)}, f32[1,1536]{1,0:T(1,128)S(1)}, bf16[512,15...) custom-call(bf16[8,512]{1,0:T(8,128)(2,1)S(1)} %get-tuple-element.21.feats_ref, ...), custom_call_target="tpu_custom_call" | custom-call | flops 31457280 | bytes 1572864 | tf_op jit(solution)/shard_map/near/pallas_call | solution.py:138
  12.3 0.0 collective-permute-done.5.refs_2_
  12.3 0.0 collective-permute-done.4.refs_1_
  12.3 0.0 collective-permute-done.3.refs_0_
  12.3 0.0 collective-permute-done.2.last_ref
  12.3 5.7 %far.1 = (bf16[512,512]{1,0:T(8,128)(2,1)S(1)}, bf16[1536,2048]{1,0:T(8,128)(2,1)S(1)}, f32[4,16,512]{2,1,0:T(8,128)S(1)}, bf16[4,16,512]{2,1,0:T(8,128)(2,1)S(1)}) custom-call(f32[16,512]{1,0:T(8,128)S(1)} %get-tuple-element.23.near_ref, bf16[512,32]{1,0:T(8,128)(2,1)S(1)} %get-tuple-element.24.rows_ref, f32[512,128]{1,0:T(8,128)S(1)} %get-tuple-element.25.row_logs_ref, ...), custom_call_target="tpu_custom_call" | custom-call | flops 167772160 | bytes 8388608 | tf_op jit(solution)/shard_map/far/pallas_call | solution.py:185
  18.0 0.0 collective-permute-start.6
  18.0 1.6 %collective-permute-start.8 = (bf16[4,16,512]{2,1,0:T(8,128)(2,1)S(1)}, bf16[4,16,512]{2,1,0:T(8,128)(2,1)S(1)}, u32[]{:S(2)}, u32[]{:S(2)}) collective-permute-start(bf16[4,16,512]{2,1,0:T(8,128)(2,1)S(1)} %get-tuple-element.29), channel_id=1, source_target_pairs={{0,3},{1,2},{2,1},{3,0},{4,7},{5,6},{6,5},{7,4},{8,11},{9,10},{10,... | collective-permute-start | bytes 196616 | tf_op jit(solution)/shard_map/ppermute | solution.py:360
  19.6 0.5 %collective-permute-start.7 = (bf16[4,16,512]{2,1,0:T(8,128)(2,1)S(1)}, bf16[4,16,512]{2,1,0:T(8,128)(2,1)S(1)}, u32[]{:S(2)}, u32[]{:S(2)}) collective-permute-start(bf16[4,16,512]{2,1,0:T(8,128)(2,1)S(1)} %get-tuple-element.29), channel_id=1, source_target_pairs={{0,2},{1,3},{2,0},{3,1},{4,6},{5,7},{6,4},{7,5},{8,10},{9,11},{10,... | collective-permute-start | bytes 196616 | tf_op jit(solution)/shard_map/ppermute | solution.py:360
  20.1 1.9 %collective-permute-done.8.refs_2_ = bf16[4,16,512]{2,1,0:T(8,128)(2,1)S(1)} collective-permute-done((bf16[4,16,512]{2,1,0:T(8,128)(2,1)S(1)}, bf16[4,16,512]{2,1,0:T(8,128)(2,1)S(1)}, u32[]{:S(2)}, u32[]{:S(2)}) %collective-permute-start.8) | collective-permute-done | bytes 65568 | tf_op jit(solution)/shard_map/ppermute | solution.py:360
  22.1 1.8 %collective-permute-done.7.refs_1_ = bf16[4,16,512]{2,1,0:T(8,128)(2,1)S(1)} collective-permute-done((bf16[4,16,512]{2,1,0:T(8,128)(2,1)S(1)}, bf16[4,16,512]{2,1,0:T(8,128)(2,1)S(1)}, u32[]{:S(2)}, u32[]{:S(2)}) %collective-permute-start.7) | collective-permute-done | bytes 65568 | tf_op jit(solution)/shard_map/ppermute | solution.py:360
  23.9 0.0 collective-permute-done.6.refs_0_
  23.9 1.3 %second.1 = (f32[16,512]{1,0:T(8,128)S(1)}, f32[16,512]{1,0:T(8,128)S(1)}, f32[16,512]{1,0:T(8,128)S(1)}, f32[16,512]{1,0:T(8,128)S(1)}, f32[16,16]{1,0:T(8,128)S(1)}) custom-call(f32[4,16,512]{2,1,0:T(8,128)S(1)} %get-tuple-element.28.own_ref, f32[4,16,512]{2,1,0:T(8,128)S(1)} %collective-permute-done.6.refs_0_, ...), custom_call_target="tpu_custom_call" | custom-call | tf_op jit(solution)/shard_map/second/pallas_call | solution.py:227
  25.2 1.8 %collective-permute-start.9 = (f32[16,512]{1,0:T(8,128)S(1)}, f32[16,512]{1,0:T(8,128)S(1)}, u32[]{:S(2)}, u32[]{:S(2)}) collective-permute-start(f32[16,512]{1,0:T(8,128)S(1)} %get-tuple-element.35), channel_id=1, source_target_pairs={{0,8},{1,9},{2,10},{3,11},{4,12},{5,13},{6,14},{7,15},{8,0},{9,1},... | collective-permute-start | bytes 98312 | tf_op jit(solution)/shard_map/ppermute | solution.py:360
  27.0 0.3 collective-permute-start.10
  27.3 1.1 %collective-permute-start.11 = (f32[16,512]{1,0:T(8,128)S(1)}, f32[16,512]{1,0:T(8,128)S(1)}, u32[]{:S(2)}, u32[]{:S(2)}) collective-permute-start(f32[16,512]{1,0:T(8,128)S(1)} %get-tuple-element.37), channel_id=1, source_target_pairs={{0,5},{1,4},{2,7},{3,6},{4,1},{5,0},{6,3},{7,2},{8,13},{9,12},{10,... | collective-permute-start | bytes 98312 | tf_op jit(solution)/shard_map/ppermute | solution.py:360
  28.4 1.9 %collective-permute-done.9.refs_0_ = f32[16,512]{1,0:T(8,128)S(1)} collective-permute-done((f32[16,512]{1,0:T(8,128)S(1)}, f32[16,512]{1,0:T(8,128)S(1)}, u32[]{:S(2)}, u32[]{:S(2)}) %collective-permute-start.9) | collective-permute-done | bytes 32800 | tf_op jit(solution)/shard_map/ppermute | solution.py:360
  30.4 1.8 %collective-permute-done.10.refs_1_ = f32[16,512]{1,0:T(8,128)S(1)} collective-permute-done((f32[16,512]{1,0:T(8,128)S(1)}, f32[16,512]{1,0:T(8,128)S(1)}, u32[]{:S(2)}, u32[]{:S(2)}) %collective-permute-start.10) | collective-permute-done | bytes 32800 | tf_op jit(solution)/shard_map/ppermute | solution.py:360
  32.2 0.0 collective-permute-done.11.refs_2_
  32.2 0.2 gather_parts.1
  32.3 0.7 %collective-permute-start.14 = (f32[32,16]{1,0:T(8,128)S(1)}, f32[32,16]{1,0:T(8,128)S(1)}, u32[]{:S(2)}, u32[]{:S(2)}) collective-permute-start(f32[32,16]{1,0:T(8,128)S(1)} %get-tuple-element.39), channel_id=1, source_target_pairs={{0,2},{1,3},{2,0},{3,1},{4,6},{5,7},{6,4},{7,5},{8,10},{9,11},{10,... | collective-permute-start | bytes 6152 | tf_op jit(solution)/shard_map/ppermute | solution.py:360
  33.0 0.7 %collective-permute-start.13 = (f32[32,16]{1,0:T(8,128)S(1)}, f32[32,16]{1,0:T(8,128)S(1)}, u32[]{:S(2)}, u32[]{:S(2)}) collective-permute-start(f32[32,16]{1,0:T(8,128)S(1)} %get-tuple-element.39), channel_id=1, source_target_pairs={{0,3},{1,2},{2,1},{3,0},{4,7},{5,6},{6,5},{7,4},{8,11},{9,10},{10,... | collective-permute-start | bytes 6152 | tf_op jit(solution)/shard_map/ppermute | solution.py:360
  33.8 0.7 %collective-permute-start.12 = (f32[32,16]{1,0:T(8,128)S(1)}, f32[32,16]{1,0:T(8,128)S(1)}, u32[]{:S(2)}, u32[]{:S(2)}) collective-permute-start(f32[32,16]{1,0:T(8,128)S(1)} %get-tuple-element.39), channel_id=1, source_target_pairs={{0,1},{1,0},{2,3},{3,2},{4,5},{5,4},{6,7},{7,6},{8,9},{9,8},{10,11... | collective-permute-start | bytes 6152 | tf_op jit(solution)/shard_map/ppermute | solution.py:360
  34.5 1.7 %collective-permute-done.14 = f32[32,16]{1,0:T(8,128)S(1)} collective-permute-done((f32[32,16]{1,0:T(8,128)S(1)}, f32[32,16]{1,0:T(8,128)S(1)}, u32[]{:S(2)}, u32[]{:S(2)}) %collective-permute-start.14) | collective-permute-done | bytes 2080 | tf_op jit(solution)/shard_map/ppermute | solution.py:360
  36.2 0.2 collective-permute-done.13
  36.4 0.0 collective-permute-done.12
  36.4 1.6 %collective-permute-start.17 = (f32[32,16]{1,0:T(8,128)S(1)}, f32[32,16]{1,0:T(8,128)S(1)}, u32[]{:S(2)}, u32[]{:S(2)}) collective-permute-start(f32[32,16]{1,0:T(8,128)S(1)} %add_add_fusion.refs_0_), channel_id=1, source_target_pairs={{0,13},{1,12},{2,15},{3,14},{4,9},{5,8},{6,11},{7,10},{8,5},{9,4},... | collective-permute-start | bytes 6152 | tf_op jit(solution)/shard_map/ppermute | solution.py:360
  38.0 0.2 collective-permute-start.16
  38.2 2.1 %collective-permute-start.15 = (f32[32,16]{1,0:T(8,128)S(1)}, f32[32,16]{1,0:T(8,128)S(1)}, u32[]{:S(2)}, u32[]{:S(2)}) collective-permute-start(f32[32,16]{1,0:T(8,128)S(1)} %add_add_fusion.refs_0_), channel_id=1, source_target_pairs={{0,5},{1,4},{2,7},{3,6},{4,1},{5,0},{6,3},{7,2},{8,13},{9,12},{10,... | collective-permute-start | bytes 6152 | tf_op jit(solution)/shard_map/ppermute | solution.py:360
  40.3 1.1 %collective-permute-done.17.refs_3_ = f32[32,16]{1,0:T(8,128)S(1)} collective-permute-done((f32[32,16]{1,0:T(8,128)S(1)}, f32[32,16]{1,0:T(8,128)S(1)}, u32[]{:S(2)}, u32[]{:S(2)}) %collective-permute-start.17) | collective-permute-done | bytes 2080 | tf_op jit(solution)/shard_map/ppermute | solution.py:360
  41.4 0.7 %collective-permute-done.16.refs_2_ = f32[32,16]{1,0:T(8,128)S(1)} collective-permute-done((f32[32,16]{1,0:T(8,128)S(1)}, f32[32,16]{1,0:T(8,128)S(1)}, u32[]{:S(2)}, u32[]{:S(2)}) %collective-permute-start.16) | collective-permute-done | bytes 2080 | tf_op jit(solution)/shard_map/ppermute | solution.py:360
  42.1 0.0 collective-permute-done.15.refs_1_
  42.1 1.1 %finish.1 = (f32[16,512]{1,0:T(8,128)}, f32[16,16]{1,0:T(8,128)}) custom-call(f32[16,512]{1,0:T(8,128)S(1)} %get-tuple-element.38.product_ref, f32[32,16]{1,0:T(8,128)S(1)} %add_add_fusion.refs_0_, f32[32,16]{1,0:T(8,128)S(1)} %collective-permute-done.15.refs_1_, f32[32,16]{1,0:T(8,128)S(1)} %collective-permute-done.16.refs_2_, ...), custom_call_target="tpu_custom_call" | custom-call | tf_op jit(solution)/shard_map/finish/pallas_call | solution.py:341
  (1 shorter events, 0.0 us)
Async XLA Ops:
  1.4 7.5 %collective-permute-start.1 = (bf16[24,512]{1,0:T(8,128)(2,1)S(1)}, bf16[24,512]{1,0:T(8,128)(2,1)S(1)}, u32[]{:S(2)}, u32[]{:S(2)}) collective-permute-start(bf16[24,512]{1,0:T(8,128)(2,1)S(1)} %get-tuple-element.22.refs_0_.refs_3_), channel_id=1, source_target_pairs={{0,13},{1,12},{2,15},{3,14},{4,9},{5,8},{6,11},{7,10},{8,5},{9,4},... | collective-permute-start | bytes 73736 | tf_op jit(solution)/shard_map/ppermute | solution.py:360
  6.0 4.7 %collective-permute-start = (bf16[24,512]{1,0:T(8,128)(2,1)S(1)}, bf16[24,512]{1,0:T(8,128)(2,1)S(1)}, u32[]{:S(2)}, u32[]{:S(2)}) collective-permute-start(bf16[24,512]{1,0:T(8,128)(2,1)S(1)} %get-tuple-element.22.refs_0_.refs_3_), channel_id=1, source_target_pairs={{0,8},{1,9},{2,10},{3,11},{4,12},{5,13},{6,14},{7,15},{8,0},{9,1},... | collective-permute-start | bytes 73736 | tf_op jit(solution)/shard_map/ppermute | solution.py:360
  6.0 6.3 %collective-permute-start.2 = (bf16[24,512]{1,0:T(8,128)(2,1)S(1)}, bf16[24,512]{1,0:T(8,128)(2,1)S(1)}, u32[]{:S(2)}, u32[]{:S(2)}) collective-permute-start(bf16[24,512]{1,0:T(8,128)(2,1)S(1)} %get-tuple-element.22.refs_0_.refs_3_), channel_id=1, source_target_pairs={{0,5},{1,4},{2,7},{3,6},{4,1},{5,0},{6,3},{7,2},{8,13},{9,12},{10,... | collective-permute-start | bytes 73736 | tf_op jit(solution)/shard_map/ppermute | solution.py:360
  6.4 5.9 %collective-permute-start.5 = (bf16[8,512]{1,0:T(8,128)(2,1)S(1)}, bf16[8,512]{1,0:T(8,128)(2,1)S(1)}, u32[]{:S(2)}, u32[]{:S(2)}) collective-permute-start(bf16[8,512]{1,0:T(8,128)(2,1)S(1)} %get-tuple-element.21.feats_ref), channel_id=1, source_target_pairs={{0,3},{1,2},{2,1},{3,0},{4,7},{5,6},{6,5},{7,4},{8,11},{9,10},{10,... | collective-permute-start | bytes 24584 | tf_op jit(solution)/shard_map/ppermute | solution.py:360
  8.4 3.8 %collective-permute-start.4 = (bf16[8,512]{1,0:T(8,128)(2,1)S(1)}, bf16[8,512]{1,0:T(8,128)(2,1)S(1)}, u32[]{:S(2)}, u32[]{:S(2)}) collective-permute-start(bf16[8,512]{1,0:T(8,128)(2,1)S(1)} %get-tuple-element.21.feats_ref), channel_id=1, source_target_pairs={{0,2},{1,3},{2,0},{3,1},{4,6},{5,7},{6,4},{7,5},{8,10},{9,11},{10,... | collective-permute-start | bytes 24584 | tf_op jit(solution)/shard_map/ppermute | solution.py:360
  8.9 3.3 %collective-permute-start.3 = (bf16[8,512]{1,0:T(8,128)(2,1)S(1)}, bf16[8,512]{1,0:T(8,128)(2,1)S(1)}, u32[]{:S(2)}, u32[]{:S(2)}) collective-permute-start(bf16[8,512]{1,0:T(8,128)(2,1)S(1)} %get-tuple-element.21.feats_ref), channel_id=1, source_target_pairs={{0,1},{1,0},{2,3},{3,2},{4,5},{5,4},{6,7},{7,6},{8,9},{9,8},{10,11... | collective-permute-start | bytes 24584 | tf_op jit(solution)/shard_map/ppermute | solution.py:360
  18.0 5.9 %collective-permute-start.6 = (f32[4,16,512]{2,1,0:T(8,128)S(1)}, f32[4,16,512]{2,1,0:T(8,128)S(1)}, u32[]{:S(2)}, u32[]{:S(2)}) collective-permute-start(f32[4,16,512]{2,1,0:T(8,128)S(1)} %get-tuple-element.28.own_ref), channel_id=1, source_target_pairs={{0,1},{1,0},{2,3},{3,2},{4,5},{5,4},{6,7},{7,6},{8,9},{9,8},{10,11... | collective-permute-start | bytes 393224 | tf_op jit(solution)/shard_map/ppermute | solution.py:360
  18.0 4.1 %collective-permute-start.8 = (bf16[4,16,512]{2,1,0:T(8,128)(2,1)S(1)}, bf16[4,16,512]{2,1,0:T(8,128)(2,1)S(1)}, u32[]{:S(2)}, u32[]{:S(2)}) collective-permute-start(bf16[4,16,512]{2,1,0:T(8,128)(2,1)S(1)} %get-tuple-element.29), channel_id=1, source_target_pairs={{0,3},{1,2},{2,1},{3,0},{4,7},{5,6},{6,5},{7,4},{8,11},{9,10},{10,... | collective-permute-start | bytes 196616 | tf_op jit(solution)/shard_map/ppermute | solution.py:360
  19.6 4.3 %collective-permute-start.7 = (bf16[4,16,512]{2,1,0:T(8,128)(2,1)S(1)}, bf16[4,16,512]{2,1,0:T(8,128)(2,1)S(1)}, u32[]{:S(2)}, u32[]{:S(2)}) collective-permute-start(bf16[4,16,512]{2,1,0:T(8,128)(2,1)S(1)} %get-tuple-element.29), channel_id=1, source_target_pairs={{0,2},{1,3},{2,0},{3,1},{4,6},{5,7},{6,4},{7,5},{8,10},{9,11},{10,... | collective-permute-start | bytes 196616 | tf_op jit(solution)/shard_map/ppermute | solution.py:360
  25.2 5.2 %collective-permute-start.9 = (f32[16,512]{1,0:T(8,128)S(1)}, f32[16,512]{1,0:T(8,128)S(1)}, u32[]{:S(2)}, u32[]{:S(2)}) collective-permute-start(f32[16,512]{1,0:T(8,128)S(1)} %get-tuple-element.35), channel_id=1, source_target_pairs={{0,8},{1,9},{2,10},{3,11},{4,12},{5,13},{6,14},{7,15},{8,0},{9,1},... | collective-permute-start | bytes 98312 | tf_op jit(solution)/shard_map/ppermute | solution.py:360
  27.0 5.2 %collective-permute-start.10 = (f32[16,512]{1,0:T(8,128)S(1)}, f32[16,512]{1,0:T(8,128)S(1)}, u32[]{:S(2)}, u32[]{:S(2)}) collective-permute-start(f32[16,512]{1,0:T(8,128)S(1)} %get-tuple-element.36), channel_id=1, source_target_pairs={{0,13},{1,12},{2,15},{3,14},{4,9},{5,8},{6,11},{7,10},{8,5},{9,4},... | collective-permute-start | bytes 98312 | tf_op jit(solution)/shard_map/ppermute | solution.py:360
  27.3 4.9 %collective-permute-start.11 = (f32[16,512]{1,0:T(8,128)S(1)}, f32[16,512]{1,0:T(8,128)S(1)}, u32[]{:S(2)}, u32[]{:S(2)}) collective-permute-start(f32[16,512]{1,0:T(8,128)S(1)} %get-tuple-element.37), channel_id=1, source_target_pairs={{0,5},{1,4},{2,7},{3,6},{4,1},{5,0},{6,3},{7,2},{8,13},{9,12},{10,... | collective-permute-start | bytes 98312 | tf_op jit(solution)/shard_map/ppermute | solution.py:360
  32.3 3.9 %collective-permute-start.14 = (f32[32,16]{1,0:T(8,128)S(1)}, f32[32,16]{1,0:T(8,128)S(1)}, u32[]{:S(2)}, u32[]{:S(2)}) collective-permute-start(f32[32,16]{1,0:T(8,128)S(1)} %get-tuple-element.39), channel_id=1, source_target_pairs={{0,2},{1,3},{2,0},{3,1},{4,6},{5,7},{6,4},{7,5},{8,10},{9,11},{10,... | collective-permute-start | bytes 6152 | tf_op jit(solution)/shard_map/ppermute | solution.py:360
  33.0 3.3 %collective-permute-start.13 = (f32[32,16]{1,0:T(8,128)S(1)}, f32[32,16]{1,0:T(8,128)S(1)}, u32[]{:S(2)}, u32[]{:S(2)}) collective-permute-start(f32[32,16]{1,0:T(8,128)S(1)} %get-tuple-element.39), channel_id=1, source_target_pairs={{0,3},{1,2},{2,1},{3,0},{4,7},{5,6},{6,5},{7,4},{8,11},{9,10},{10,... | collective-permute-start | bytes 6152 | tf_op jit(solution)/shard_map/ppermute | solution.py:360
  33.8 2.6 %collective-permute-start.12 = (f32[32,16]{1,0:T(8,128)S(1)}, f32[32,16]{1,0:T(8,128)S(1)}, u32[]{:S(2)}, u32[]{:S(2)}) collective-permute-start(f32[32,16]{1,0:T(8,128)S(1)} %get-tuple-element.39), channel_id=1, source_target_pairs={{0,1},{1,0},{2,3},{3,2},{4,5},{5,4},{6,7},{7,6},{8,9},{9,8},{10,11... | collective-permute-start | bytes 6152 | tf_op jit(solution)/shard_map/ppermute | solution.py:360
  36.4 5.0 %collective-permute-start.17 = (f32[32,16]{1,0:T(8,128)S(1)}, f32[32,16]{1,0:T(8,128)S(1)}, u32[]{:S(2)}, u32[]{:S(2)}) collective-permute-start(f32[32,16]{1,0:T(8,128)S(1)} %add_add_fusion.refs_0_), channel_id=1, source_target_pairs={{0,13},{1,12},{2,15},{3,14},{4,9},{5,8},{6,11},{7,10},{8,5},{9,4},... | collective-permute-start | bytes 6152 | tf_op jit(solution)/shard_map/ppermute | solution.py:360
  38.0 4.1 %collective-permute-start.16 = (f32[32,16]{1,0:T(8,128)S(1)}, f32[32,16]{1,0:T(8,128)S(1)}, u32[]{:S(2)}, u32[]{:S(2)}) collective-permute-start(f32[32,16]{1,0:T(8,128)S(1)} %add_add_fusion.refs_0_), channel_id=1, source_target_pairs={{0,9},{1,8},{2,11},{3,10},{4,13},{5,12},{6,15},{7,14},{8,1},{9,0},... | collective-permute-start | bytes 6152 | tf_op jit(solution)/shard_map/ppermute | solution.py:360
  38.2 3.9 %collective-permute-start.15 = (f32[32,16]{1,0:T(8,128)S(1)}, f32[32,16]{1,0:T(8,128)S(1)}, u32[]{:S(2)}, u32[]{:S(2)}) collective-permute-start(f32[32,16]{1,0:T(8,128)S(1)} %add_add_fusion.refs_0_), channel_id=1, source_target_pairs={{0,5},{1,4},{2,7},{3,6},{4,1},{5,0},{6,3},{7,2},{8,13},{9,12},{10,... | collective-permute-start | bytes 6152 | tf_op jit(solution)/shard_map/ppermute | solution.py:360

commit v5 on v4

--- a/solution.py
+++ b/solution.py
@@ -200,6 +200,18 @@
     return lax.dot_general(product, product, NT, precision=lax.Precision.HIGHEST, preferred_element_type=F32)
 
 
+def fold(second_gram, first_gram):
+    half = second_gram.shape[0] // 2
+    both = jnp.concatenate([second_gram, first_gram], axis=1)
+    return jnp.concatenate([both[:half], both[half:]], axis=1)
+
+
+def unfold(folded):
+    size = 2 * folded.shape[0]
+    both = jnp.concatenate([folded[:, : 2 * size], folded[:, 2 * size :]], axis=0)
+    return both[:, :size], both[:, size:]
+
+
 def second_kernel(own_ref, *refs):
     part_refs, near_ref, edge_ref, far_ref, outs, gram_ref = refs[:3], refs[3], refs[4], refs[5], refs[6:-1], refs[-1]
     count, size, points = own_ref.shape
@@ -234,20 +246,18 @@
 
 def gather_kernel(first_ref, own_ref, *refs):
     part_refs, (product_ref, gram_ref) = refs[:-2], refs[-2:]
-    size = own_ref.shape[0]
     product = own_ref[...]
     for ref in part_refs:
         product += ref[...]
     product_ref[...] = product
-    gram_ref[:size] = gram_of(product)
-    gram_ref[size:] = first_ref[...]
+    gram_ref[...] = fold(gram_of(product), first_ref[...])
 
 
 def gather_parts(first_gram, own, parts):
     size, points = own.shape
     return pl.pallas_call(
         gather_kernel,
-        out_shape=(pltpu.VMEM((size, points), F32), pltpu.VMEM((2 * size, size), F32)),
+        out_shape=(pltpu.VMEM((size, points), F32), pltpu.VMEM((size // 2, 4 * size), F32)),
         compiler_params=SMALL,
         name="gather_parts",
     )(first_gram, own, *parts)
@@ -279,16 +289,14 @@
 
 
 def grams_kernel(second_ref, first_ref, gram_ref):
-    size = second_ref.shape[0]
-    gram_ref[:size] = gram_of(second_ref[...])
-    gram_ref[size:] = gram_of(first_ref[...])
+    gram_ref[...] = fold(gram_of(second_ref[...]), gram_of(first_ref[...]))
 
 
 def grams(second_product, first_product):
     size = first_product.shape[0]
     return pl.pallas_call(
         grams_kernel,
-        out_shape=jax.ShapeDtypeStruct((2 * size, size), F32),
+        out_shape=jax.ShapeDtypeStruct((size // 2, 4 * size), F32),
         compiler_params=SMALL,
         name="grams",
     )(second_product, first_product)
@@ -319,9 +327,9 @@
     gram = gram_refs[0][...] + gram_refs[1][...]
     if len(gram_refs) > 2:
         gram = gram + (gram_refs[2][...] + gram_refs[3][...])
-    gram = gram / total_points
-    steps, cols, scale = eliminate(gram[:size])
-    first_steps, _, first_scale = eliminate(gram[size:])
+    gram, first_gram = unfold(gram / total_points)
+    steps, cols, scale = eliminate(gram)
+    first_steps, _, first_scale = eliminate(first_gram)
     for at in range(0, points, LANES):
         part = product_ref[:, at : at + LANES]
         for k in range(size):

time: 43.4 us -> 43 us (level)
  no operation moved by 1% of the time
where the time goes in v5:
time: 43 us; the launch traced here: 42.8 us
  starting transfers between devices  18.9 us (44%)
  waiting for transfers between devices  12.6 us (29%)
  Pallas kernels  10.6 us (25%)
  between operations  0.68 us (2%)
    ppermute x18, starting transfers between devices, exchange(): lax.ppermute(value, 'wide', [(k, k ^ distance) for k in range(width)])  18.9 us
    ppermute x18, waiting for transfers between devices, exchange(): lax.ppermute(value, 'wide', [(k, k ^ distance) for k in range(width)])  12.6 us
    pallas_call x1, Pallas kernels, far(): pl.pallas_call(functools.partial(far_kernel, len(feats)), out_shape=(pltp...  5.69 us
    pallas_call x1, Pallas kernels, near(): pl.pallas_call(functools.partial(near_kernel, len(packed)), out_shape=(pl...  1.54 us
    pallas_call x1, Pallas kernels, second(): pl.pallas_call(second_kernel, out_shape=[pltpu.VMEM((size, points), F32)]...  1.32 us
    pallas_call x1, Pallas kernels, finish(): pl.pallas_call(functools.partial(finish_kernel, total_points), out_shape=...  1.07 us
  transfers between devices with their start and end apart: 18, of which 9 were waited for; matrix products, arithmetic and copies ran while one was open for 0% of the time, Pallas kernels for 4%

profile of v5, /device:TPU:0, one launch (start us, length us, event | category | flops | bytes accessed | tf_op | source)
XLA Modules:
  0.0 42.8 jit_solution(7419749921406638193)
XLA Ops:
  0.6 0.8 %prepare.1 = (bf16[24,512]{1,0:T(8,128)(2,1)S(1)}, bf16[8,512]{1,0:T(8,128)(2,1)S(1)}) custom-call(f32[3,512]{1,0:T(4,128)} %refs_0_.1, f32[1,512]{1,0:T(1,128)} %bitcast.1, bf16[16,512]{1,0:T(8,128)(2,1)} %refs_2_.1), custom_call_target="tpu_custom_call" | custom-call | tf_op jit(solution)/shard_map/prepare/pallas_call | solution.py:102
  1.4 4.6 %collective-permute-start.1 = (bf16[24,512]{1,0:T(8,128)(2,1)S(1)}, bf16[24,512]{1,0:T(8,128)(2,1)S(1)}, u32[]{:S(2)}, u32[]{:S(2)}) collective-permute-start(bf16[24,512]{1,0:T(8,128)(2,1)S(1)} %get-tuple-element.22.refs_0_.refs_3_), channel_id=1, source_target_pairs={{0,13},{1,12},{2,15},{3,14},{4,9},{5,8},{6,11},{7,10},{8,5},{9,4},... | collective-permute-start | bytes 73736 | tf_op jit(solution)/shard_map/ppermute | solution.py:368
  6.0 0.0 collective-permute-start
  6.0 0.4 collective-permute-start.2
  6.4 2.1 %collective-permute-start.5 = (bf16[8,512]{1,0:T(8,128)(2,1)S(1)}, bf16[8,512]{1,0:T(8,128)(2,1)S(1)}, u32[]{:S(2)}, u32[]{:S(2)}) collective-permute-start(bf16[8,512]{1,0:T(8,128)(2,1)S(1)} %get-tuple-element.21.feats_ref), channel_id=1, source_target_pairs={{0,3},{1,2},{2,1},{3,0},{4,7},{5,6},{6,5},{7,4},{8,11},{9,10},{10,... | collective-permute-start | bytes 24584 | tf_op jit(solution)/shard_map/ppermute | solution.py:368
  8.4 0.5 %collective-permute-start.4 = (bf16[8,512]{1,0:T(8,128)(2,1)S(1)}, bf16[8,512]{1,0:T(8,128)(2,1)S(1)}, u32[]{:S(2)}, u32[]{:S(2)}) collective-permute-start(bf16[8,512]{1,0:T(8,128)(2,1)S(1)} %get-tuple-element.21.feats_ref), channel_id=1, source_target_pairs={{0,2},{1,3},{2,0},{3,1},{4,6},{5,7},{6,4},{7,5},{8,10},{9,11},{10,... | collective-permute-start | bytes 24584 | tf_op jit(solution)/shard_map/ppermute | solution.py:368
  8.9 0.0 collective-permute-done.1.refs_2_.refs_5_
  8.9 0.0 collective-permute-start.3
  8.9 1.8 %collective-permute-done.refs_1_.refs_4_ = bf16[24,512]{1,0:T(8,128)(2,1)S(1)} collective-permute-done((bf16[24,512]{1,0:T(8,128)(2,1)S(1)}, bf16[24,512]{1,0:T(8,128)(2,1)S(1)}, u32[]{:S(2)}, u32[]{:S(2)}) %collective-permute-start) | collective-permute-done | bytes 24608 | tf_op jit(solution)/shard_map/ppermute | solution.py:368
  10.7 1.5 %near.1 = (bf16[512,32]{1,0:T(8,128)(2,1)S(1)}, f32[512,128]{1,0:T(8,128)S(1)}, bf16[32,1536]{1,0:T(8,128)(2,1)S(1)}, f32[1,1536]{1,0:T(1,128)S(1)}, bf16[512,15...) custom-call(bf16[8,512]{1,0:T(8,128)(2,1)S(1)} %get-tuple-element.21.feats_ref, ...), custom_call_target="tpu_custom_call" | custom-call | flops 31457280 | bytes 1572864 | tf_op jit(solution)/shard_map/near/pallas_call | solution.py:138
  12.3 0.0 collective-permute-done.5.refs_2_
  12.3 0.0 collective-permute-done.4.refs_1_
  12.3 0.0 collective-permute-done.3.refs_0_
  12.3 0.0 collective-permute-done.2.last_ref
  12.3 5.7 %far.1 = (bf16[512,512]{1,0:T(8,128)(2,1)S(1)}, bf16[1536,2048]{1,0:T(8,128)(2,1)S(1)}, f32[4,16,512]{2,1,0:T(8,128)S(1)}, bf16[4,16,512]{2,1,0:T(8,128)(2,1)S(1)}) custom-call(f32[16,512]{1,0:T(8,128)S(1)} %get-tuple-element.23.near_ref, bf16[512,32]{1,0:T(8,128)(2,1)S(1)} %get-tuple-element.24.rows_ref, f32[512,128]{1,0:T(8,128)S(1)} %get-tuple-element.25.row_logs_ref, ...), custom_call_target="tpu_custom_call" | custom-call | flops 167772160 | bytes 8388608 | tf_op jit(solution)/shard_map/far/pallas_call | solution.py:185
  18.0 0.0 collective-permute-start.6
  18.0 1.6 %collective-permute-start.8 = (bf16[4,16,512]{2,1,0:T(8,128)(2,1)S(1)}, bf16[4,16,512]{2,1,0:T(8,128)(2,1)S(1)}, u32[]{:S(2)}, u32[]{:S(2)}) collective-permute-start(bf16[4,16,512]{2,1,0:T(8,128)(2,1)S(1)} %get-tuple-element.29), channel_id=1, source_target_pairs={{0,3},{1,2},{2,1},{3,0},{4,7},{5,6},{6,5},{7,4},{8,11},{9,10},{10,... | collective-permute-start | bytes 196616 | tf_op jit(solution)/shard_map/ppermute | solution.py:368
  19.6 0.5 %collective-permute-start.7 = (bf16[4,16,512]{2,1,0:T(8,128)(2,1)S(1)}, bf16[4,16,512]{2,1,0:T(8,128)(2,1)S(1)}, u32[]{:S(2)}, u32[]{:S(2)}) collective-permute-start(bf16[4,16,512]{2,1,0:T(8,128)(2,1)S(1)} %get-tuple-element.29), channel_id=1, source_target_pairs={{0,2},{1,3},{2,0},{3,1},{4,6},{5,7},{6,4},{7,5},{8,10},{9,11},{10,... | collective-permute-start | bytes 196616 | tf_op jit(solution)/shard_map/ppermute | solution.py:368
  20.1 1.9 %collective-permute-done.8.refs_2_ = bf16[4,16,512]{2,1,0:T(8,128)(2,1)S(1)} collective-permute-done((bf16[4,16,512]{2,1,0:T(8,128)(2,1)S(1)}, bf16[4,16,512]{2,1,0:T(8,128)(2,1)S(1)}, u32[]{:S(2)}, u32[]{:S(2)}) %collective-permute-start.8) | collective-permute-done | bytes 65568 | tf_op jit(solution)/shard_map/ppermute | solution.py:368
  22.1 1.8 %collective-permute-done.7.refs_1_ = bf16[4,16,512]{2,1,0:T(8,128)(2,1)S(1)} collective-permute-done((bf16[4,16,512]{2,1,0:T(8,128)(2,1)S(1)}, bf16[4,16,512]{2,1,0:T(8,128)(2,1)S(1)}, u32[]{:S(2)}, u32[]{:S(2)}) %collective-permute-start.7) | collective-permute-done | bytes 65568 | tf_op jit(solution)/shard_map/ppermute | solution.py:368
  23.9 0.0 collective-permute-done.6.refs_0_
  23.9 1.3 %second.1 = (f32[16,512]{1,0:T(8,128)S(1)}, f32[16,512]{1,0:T(8,128)S(1)}, f32[16,512]{1,0:T(8,128)S(1)}, f32[16,512]{1,0:T(8,128)S(1)}, f32[16,16]{1,0:T(8,128)S(1)}) custom-call(f32[4,16,512]{2,1,0:T(8,128)S(1)} %get-tuple-element.28.own_ref, f32[4,16,512]{2,1,0:T(8,128)S(1)} %collective-permute-done.6.refs_0_, ...), custom_call_target="tpu_custom_call" | custom-call | tf_op jit(solution)/shard_map/second/pallas_call | solution.py:239
  25.2 1.8 %collective-permute-start.9 = (f32[16,512]{1,0:T(8,128)S(1)}, f32[16,512]{1,0:T(8,128)S(1)}, u32[]{:S(2)}, u32[]{:S(2)}) collective-permute-start(f32[16,512]{1,0:T(8,128)S(1)} %get-tuple-element.35), channel_id=1, source_target_pairs={{0,8},{1,9},{2,10},{3,11},{4,12},{5,13},{6,14},{7,15},{8,0},{9,1},... | collective-permute-start | bytes 98312 | tf_op jit(solution)/shard_map/ppermute | solution.py:368
  27.0 0.3 collective-permute-start.10
  27.3 1.1 %collective-permute-start.11 = (f32[16,512]{1,0:T(8,128)S(1)}, f32[16,512]{1,0:T(8,128)S(1)}, u32[]{:S(2)}, u32[]{:S(2)}) collective-permute-start(f32[16,512]{1,0:T(8,128)S(1)} %get-tuple-element.37), channel_id=1, source_target_pairs={{0,5},{1,4},{2,7},{3,6},{4,1},{5,0},{6,3},{7,2},{8,13},{9,12},{10,... | collective-permute-start | bytes 98312 | tf_op jit(solution)/shard_map/ppermute | solution.py:368
  28.4 1.9 %collective-permute-done.9.refs_0_ = f32[16,512]{1,0:T(8,128)S(1)} collective-permute-done((f32[16,512]{1,0:T(8,128)S(1)}, f32[16,512]{1,0:T(8,128)S(1)}, u32[]{:S(2)}, u32[]{:S(2)}) %collective-permute-start.9) | collective-permute-done | bytes 32800 | tf_op jit(solution)/shard_map/ppermute | solution.py:368
  30.4 1.8 %collective-permute-done.10.refs_1_ = f32[16,512]{1,0:T(8,128)S(1)} collective-permute-done((f32[16,512]{1,0:T(8,128)S(1)}, f32[16,512]{1,0:T(8,128)S(1)}, u32[]{:S(2)}, u32[]{:S(2)}) %collective-permute-start.10) | collective-permute-done | bytes 32800 | tf_op jit(solution)/shard_map/ppermute | solution.py:368
  32.2 0.0 collective-permute-done.11.refs_2_
  32.2 0.2 gather_parts.1
  32.4 0.7 %collective-permute-start.14 = (f32[8,64]{1,0:T(8,128)S(1)}, f32[8,64]{1,0:T(8,128)S(1)}, u32[]{:S(2)}, u32[]{:S(2)}) collective-permute-start(f32[8,64]{1,0:T(8,128)S(1)} %get-tuple-element.39), channel_id=1, source_target_pairs={{0,2},{1,3},{2,0},{3,1},{4,6},{5,7},{6,4},{7,5},{8,10},{9,11},{10,... | collective-permute-start | bytes 6152 | tf_op jit(solution)/shard_map/ppermute | solution.py:368
  33.1 0.7 %collective-permute-start.13 = (f32[8,64]{1,0:T(8,128)S(1)}, f32[8,64]{1,0:T(8,128)S(1)}, u32[]{:S(2)}, u32[]{:S(2)}) collective-permute-start(f32[8,64]{1,0:T(8,128)S(1)} %get-tuple-element.39), channel_id=1, source_target_pairs={{0,3},{1,2},{2,1},{3,0},{4,7},{5,6},{6,5},{7,4},{8,11},{9,10},{10,... | collective-permute-start | bytes 6152 | tf_op jit(solution)/shard_map/ppermute | solution.py:368
  33.8 0.7 %collective-permute-start.12 = (f32[8,64]{1,0:T(8,128)S(1)}, f32[8,64]{1,0:T(8,128)S(1)}, u32[]{:S(2)}, u32[]{:S(2)}) collective-permute-start(f32[8,64]{1,0:T(8,128)S(1)} %get-tuple-element.39), channel_id=1, source_target_pairs={{0,1},{1,0},{2,3},{3,2},{4,5},{5,4},{6,7},{7,6},{8,9},{9,8},{10,11... | collective-permute-start | bytes 6152 | tf_op jit(solution)/shard_map/ppermute | solution.py:368
  34.6 1.5 %collective-permute-done.14 = f32[8,64]{1,0:T(8,128)S(1)} collective-permute-done((f32[8,64]{1,0:T(8,128)S(1)}, f32[8,64]{1,0:T(8,128)S(1)}, u32[]{:S(2)}, u32[]{:S(2)}) %collective-permute-start.14) | collective-permute-done | bytes 2080 | tf_op jit(solution)/shard_map/ppermute | solution.py:368
  36.0 0.1 collective-permute-done.13
  36.1 0.0 collective-permute-done.12
  36.1 1.6 %collective-permute-start.17 = (f32[8,64]{1,0:T(8,128)S(1)}, f32[8,64]{1,0:T(8,128)S(1)}, u32[]{:S(2)}, u32[]{:S(2)}) collective-permute-start(f32[8,64]{1,0:T(8,128)S(1)} %add_add_fusion.refs_0_), channel_id=1, source_target_pairs={{0,13},{1,12},{2,15},{3,14},{4,9},{5,8},{6,11},{7,10},{8,5},{9,4},... | collective-permute-start | bytes 6152 | tf_op jit(solution)/shard_map/ppermute | solution.py:368
  37.8 0.2 collective-permute-start.16
  38.0 2.0 %collective-permute-start.15 = (f32[8,64]{1,0:T(8,128)S(1)}, f32[8,64]{1,0:T(8,128)S(1)}, u32[]{:S(2)}, u32[]{:S(2)}) collective-permute-start(f32[8,64]{1,0:T(8,128)S(1)} %add_add_fusion.refs_0_), channel_id=1, source_target_pairs={{0,5},{1,4},{2,7},{3,6},{4,1},{5,0},{6,3},{7,2},{8,13},{9,12},{10,... | collective-permute-start | bytes 6152 | tf_op jit(solution)/shard_map/ppermute | solution.py:368
  40.0 1.1 %collective-permute-done.17.refs_3_ = f32[8,64]{1,0:T(8,128)S(1)} collective-permute-done((f32[8,64]{1,0:T(8,128)S(1)}, f32[8,64]{1,0:T(8,128)S(1)}, u32[]{:S(2)}, u32[]{:S(2)}) %collective-permute-start.17) | collective-permute-done | bytes 2080 | tf_op jit(solution)/shard_map/ppermute | solution.py:368
  41.0 0.6 %collective-permute-done.16.refs_2_ = f32[8,64]{1,0:T(8,128)S(1)} collective-permute-done((f32[8,64]{1,0:T(8,128)S(1)}, f32[8,64]{1,0:T(8,128)S(1)}, u32[]{:S(2)}, u32[]{:S(2)}) %collective-permute-start.16) | collective-permute-done | bytes 2080 | tf_op jit(solution)/shard_map/ppermute | solution.py:368
  41.7 0.0 collective-permute-done.15.refs_1_
  41.7 1.1 %finish.1 = (f32[16,512]{1,0:T(8,128)}, f32[16,16]{1,0:T(8,128)}) custom-call(f32[16,512]{1,0:T(8,128)S(1)} %get-tuple-element.38.product_ref, f32[8,64]{1,0:T(8,128)S(1)} %add_add_fusion.refs_0_, f32[8,64]{1,0:T(8,128)S(1)} %collective-permute-done.15.refs_1_, f32[8,64]{1,0:T(8,128)S(1)} %collective-permute-done.16.refs_2_, ...), custom_call_target="tpu_custom_call" | custom-call | tf_op jit(solution)/shard_map/finish/pallas_call | solution.py:349
  (1 shorter events, 0.0 us)
Async XLA Ops:
  1.4 7.5 %collective-permute-start.1 = (bf16[24,512]{1,0:T(8,128)(2,1)S(1)}, bf16[24,512]{1,0:T(8,128)(2,1)S(1)}, u32[]{:S(2)}, u32[]{:S(2)}) collective-permute-start(bf16[24,512]{1,0:T(8,128)(2,1)S(1)} %get-tuple-element.22.refs_0_.refs_3_), channel_id=1, source_target_pairs={{0,13},{1,12},{2,15},{3,14},{4,9},{5,8},{6,11},{7,10},{8,5},{9,4},... | collective-permute-start | bytes 73736 | tf_op jit(solution)/shard_map/ppermute | solution.py:368
  6.0 4.7 %collective-permute-start = (bf16[24,512]{1,0:T(8,128)(2,1)S(1)}, bf16[24,512]{1,0:T(8,128)(2,1)S(1)}, u32[]{:S(2)}, u32[]{:S(2)}) collective-permute-start(bf16[24,512]{1,0:T(8,128)(2,1)S(1)} %get-tuple-element.22.refs_0_.refs_3_), channel_id=1, source_target_pairs={{0,8},{1,9},{2,10},{3,11},{4,12},{5,13},{6,14},{7,15},{8,0},{9,1},... | collective-permute-start | bytes 73736 | tf_op jit(solution)/shard_map/ppermute | solution.py:368
  6.0 6.3 %collective-permute-start.2 = (bf16[24,512]{1,0:T(8,128)(2,1)S(1)}, bf16[24,512]{1,0:T(8,128)(2,1)S(1)}, u32[]{:S(2)}, u32[]{:S(2)}) collective-permute-start(bf16[24,512]{1,0:T(8,128)(2,1)S(1)} %get-tuple-element.22.refs_0_.refs_3_), channel_id=1, source_target_pairs={{0,5},{1,4},{2,7},{3,6},{4,1},{5,0},{6,3},{7,2},{8,13},{9,12},{10,... | collective-permute-start | bytes 73736 | tf_op jit(solution)/shard_map/ppermute | solution.py:368
  6.4 5.9 %collective-permute-start.5 = (bf16[8,512]{1,0:T(8,128)(2,1)S(1)}, bf16[8,512]{1,0:T(8,128)(2,1)S(1)}, u32[]{:S(2)}, u32[]{:S(2)}) collective-permute-start(bf16[8,512]{1,0:T(8,128)(2,1)S(1)} %get-tuple-element.21.feats_ref), channel_id=1, source_target_pairs={{0,3},{1,2},{2,1},{3,0},{4,7},{5,6},{6,5},{7,4},{8,11},{9,10},{10,... | collective-permute-start | bytes 24584 | tf_op jit(solution)/shard_map/ppermute | solution.py:368
  8.4 3.8 %collective-permute-start.4 = (bf16[8,512]{1,0:T(8,128)(2,1)S(1)}, bf16[8,512]{1,0:T(8,128)(2,1)S(1)}, u32[]{:S(2)}, u32[]{:S(2)}) collective-permute-start(bf16[8,512]{1,0:T(8,128)(2,1)S(1)} %get-tuple-element.21.feats_ref), channel_id=1, source_target_pairs={{0,2},{1,3},{2,0},{3,1},{4,6},{5,7},{6,4},{7,5},{8,10},{9,11},{10,... | collective-permute-start | bytes 24584 | tf_op jit(solution)/shard_map/ppermute | solution.py:368
  8.9 3.3 %collective-permute-start.3 = (bf16[8,512]{1,0:T(8,128)(2,1)S(1)}, bf16[8,512]{1,0:T(8,128)(2,1)S(1)}, u32[]{:S(2)}, u32[]{:S(2)}) collective-permute-start(bf16[8,512]{1,0:T(8,128)(2,1)S(1)} %get-tuple-element.21.feats_ref), channel_id=1, source_target_pairs={{0,1},{1,0},{2,3},{3,2},{4,5},{5,4},{6,7},{7,6},{8,9},{9,8},{10,11... | collective-permute-start | bytes 24584 | tf_op jit(solution)/shard_map/ppermute | solution.py:368
  18.0 5.9 %collective-permute-start.6 = (f32[4,16,512]{2,1,0:T(8,128)S(1)}, f32[4,16,512]{2,1,0:T(8,128)S(1)}, u32[]{:S(2)}, u32[]{:S(2)}) collective-permute-start(f32[4,16,512]{2,1,0:T(8,128)S(1)} %get-tuple-element.28.own_ref), channel_id=1, source_target_pairs={{0,1},{1,0},{2,3},{3,2},{4,5},{5,4},{6,7},{7,6},{8,9},{9,8},{10,11... | collective-permute-start | bytes 393224 | tf_op jit(solution)/shard_map/ppermute | solution.py:368
  18.0 4.1 %collective-permute-start.8 = (bf16[4,16,512]{2,1,0:T(8,128)(2,1)S(1)}, bf16[4,16,512]{2,1,0:T(8,128)(2,1)S(1)}, u32[]{:S(2)}, u32[]{:S(2)}) collective-permute-start(bf16[4,16,512]{2,1,0:T(8,128)(2,1)S(1)} %get-tuple-element.29), channel_id=1, source_target_pairs={{0,3},{1,2},{2,1},{3,0},{4,7},{5,6},{6,5},{7,4},{8,11},{9,10},{10,... | collective-permute-start | bytes 196616 | tf_op jit(solution)/shard_map/ppermute | solution.py:368
  19.6 4.3 %collective-permute-start.7 = (bf16[4,16,512]{2,1,0:T(8,128)(2,1)S(1)}, bf16[4,16,512]{2,1,0:T(8,128)(2,1)S(1)}, u32[]{:S(2)}, u32[]{:S(2)}) collective-permute-start(bf16[4,16,512]{2,1,0:T(8,128)(2,1)S(1)} %get-tuple-element.29), channel_id=1, source_target_pairs={{0,2},{1,3},{2,0},{3,1},{4,6},{5,7},{6,4},{7,5},{8,10},{9,11},{10,... | collective-permute-start | bytes 196616 | tf_op jit(solution)/shard_map/ppermute | solution.py:368
  25.2 5.2 %collective-permute-start.9 = (f32[16,512]{1,0:T(8,128)S(1)}, f32[16,512]{1,0:T(8,128)S(1)}, u32[]{:S(2)}, u32[]{:S(2)}) collective-permute-start(f32[16,512]{1,0:T(8,128)S(1)} %get-tuple-element.35), channel_id=1, source_target_pairs={{0,8},{1,9},{2,10},{3,11},{4,12},{5,13},{6,14},{7,15},{8,0},{9,1},... | collective-permute-start | bytes 98312 | tf_op jit(solution)/shard_map/ppermute | solution.py:368
  27.0 5.2 %collective-permute-start.10 = (f32[16,512]{1,0:T(8,128)S(1)}, f32[16,512]{1,0:T(8,128)S(1)}, u32[]{:S(2)}, u32[]{:S(2)}) collective-permute-start(f32[16,512]{1,0:T(8,128)S(1)} %get-tuple-element.36), channel_id=1, source_target_pairs={{0,13},{1,12},{2,15},{3,14},{4,9},{5,8},{6,11},{7,10},{8,5},{9,4},... | collective-permute-start | bytes 98312 | tf_op jit(solution)/shard_map/ppermute | solution.py:368
  27.3 4.9 %collective-permute-start.11 = (f32[16,512]{1,0:T(8,128)S(1)}, f32[16,512]{1,0:T(8,128)S(1)}, u32[]{:S(2)}, u32[]{:S(2)}) collective-permute-start(f32[16,512]{1,0:T(8,128)S(1)} %get-tuple-element.37), channel_id=1, source_target_pairs={{0,5},{1,4},{2,7},{3,6},{4,1},{5,0},{6,3},{7,2},{8,13},{9,12},{10,... | collective-permute-start | bytes 98312 | tf_op jit(solution)/shard_map/ppermute | solution.py:368
  32.4 3.7 %collective-permute-start.14 = (f32[8,64]{1,0:T(8,128)S(1)}, f32[8,64]{1,0:T(8,128)S(1)}, u32[]{:S(2)}, u32[]{:S(2)}) collective-permute-start(f32[8,64]{1,0:T(8,128)S(1)} %get-tuple-element.39), channel_id=1, source_target_pairs={{0,2},{1,3},{2,0},{3,1},{4,6},{5,7},{6,4},{7,5},{8,10},{9,11},{10,... | collective-permute-start | bytes 6152 | tf_op jit(solution)/shard_map/ppermute | solution.py:368
  33.1 3.0 %collective-permute-start.13 = (f32[8,64]{1,0:T(8,128)S(1)}, f32[8,64]{1,0:T(8,128)S(1)}, u32[]{:S(2)}, u32[]{:S(2)}) collective-permute-start(f32[8,64]{1,0:T(8,128)S(1)} %get-tuple-element.39), channel_id=1, source_target_pairs={{0,3},{1,2},{2,1},{3,0},{4,7},{5,6},{6,5},{7,4},{8,11},{9,10},{10,... | collective-permute-start | bytes 6152 | tf_op jit(solution)/shard_map/ppermute | solution.py:368
  33.8 2.3 %collective-permute-start.12 = (f32[8,64]{1,0:T(8,128)S(1)}, f32[8,64]{1,0:T(8,128)S(1)}, u32[]{:S(2)}, u32[]{:S(2)}) collective-permute-start(f32[8,64]{1,0:T(8,128)S(1)} %get-tuple-element.39), channel_id=1, source_target_pairs={{0,1},{1,0},{2,3},{3,2},{4,5},{5,4},{6,7},{7,6},{8,9},{9,8},{10,11... | collective-permute-start | bytes 6152 | tf_op jit(solution)/shard_map/ppermute | solution.py:368
  36.1 4.9 %collective-permute-start.17 = (f32[8,64]{1,0:T(8,128)S(1)}, f32[8,64]{1,0:T(8,128)S(1)}, u32[]{:S(2)}, u32[]{:S(2)}) collective-permute-start(f32[8,64]{1,0:T(8,128)S(1)} %add_add_fusion.refs_0_), channel_id=1, source_target_pairs={{0,13},{1,12},{2,15},{3,14},{4,9},{5,8},{6,11},{7,10},{8,5},{9,4},... | collective-permute-start | bytes 6152 | tf_op jit(solution)/shard_map/ppermute | solution.py:368
  37.8 3.9 %collective-permute-start.16 = (f32[8,64]{1,0:T(8,128)S(1)}, f32[8,64]{1,0:T(8,128)S(1)}, u32[]{:S(2)}, u32[]{:S(2)}) collective-permute-start(f32[8,64]{1,0:T(8,128)S(1)} %add_add_fusion.refs_0_), channel_id=1, source_target_pairs={{0,9},{1,8},{2,11},{3,10},{4,13},{5,12},{6,15},{7,14},{8,1},{9,0},... | collective-permute-start | bytes 6152 | tf_op jit(solution)/shard_map/ppermute | solution.py:368
  38.0 3.7 %collective-permute-start.15 = (f32[8,64]{1,0:T(8,128)S(1)}, f32[8,64]{1,0:T(8,128)S(1)}, u32[]{:S(2)}, u32[]{:S(2)}) collective-permute-start(f32[8,64]{1,0:T(8,128)S(1)} %add_add_fusion.refs_0_), channel_id=1, source_target_pairs={{0,5},{1,4},{2,7},{3,6},{4,1},{5,0},{6,3},{7,2},{8,13},{9,12},{10,... | collective-permute-start | bytes 6152 | tf_op jit(solution)/shard_map/ppermute | solution.py:368

commit v6 on v5

--- a/solution.py
+++ b/solution.py
@@ -213,35 +213,61 @@
 
 
 def second_kernel(own_ref, *refs):
-    part_refs, near_ref, edge_ref, far_ref, outs, gram_ref = refs[:3], refs[3], refs[4], refs[5], refs[6:-1], refs[-1]
+    part_refs, near_ref, edge_ref, far_ref, outs = refs[:3], refs[3], refs[4], refs[5], refs[6:-2]
+    vectors_ref, first_ref = refs[-2:]
     count, size, points = own_ref.shape
+    last = len(outs)
     totals = [jnp.zeros((2 * size, points), F32) for _ in outs]
     for k in range(count):
         a, b, c = (ref[k ^ (n + 1)].astype(F32) for n, ref in enumerate(part_refs))
         product = (own_ref[k] + a) + (b + c)
         if k == 0:
-            gram_ref[...] = gram_of(product)
+            first_ref[...] = product
         vectors = jnp.concatenate(split(product, 2), axis=0).astype(BF16)
-        for n in range(len(outs)):
+        vectors_ref[k] = vectors
+        for n in range(1, last + 1):
             to = slice(n * points, (n + 1) * points)
             if k == 0:
-                cov = near_ref[:, to] if n < len(outs) - 1 else edge_ref[...]
+                cov = near_ref[:, to] if n < last else edge_ref[...]
             else:
                 cov = far_ref[(k - 1) * points : k * points, to]
-            totals[n] += jnp.dot(vectors, cov, preferred_element_type=F32)
+            totals[n - 1] += jnp.dot(vectors, cov, preferred_element_type=F32)
     for ref, total in zip(outs, totals):
         ref[...] = total[:size] + total[size:]
 
 
 def second(own, parts, near_cov, edge_cov, far_cov):
-    _, size, points = own.shape
-    blocks = far_cov.shape[1] // points
+    count, size, points = own.shape
+    others = far_cov.shape[1] // points - 1
     return pl.pallas_call(
         second_kernel,
-        out_shape=[pltpu.VMEM((size, points), F32)] * blocks + [pltpu.VMEM((size, size), F32)],
+        out_shape=[pltpu.VMEM((size, points), F32)] * others
+        + [pltpu.VMEM((count, 2 * size, points), BF16), pltpu.VMEM((size, points), F32)],
         compiler_params=PARAMS,
+        cost_estimate=cost(count * points * others * points // 8),
         name="second",
     )(own, *parts, near_cov, edge_cov, far_cov)
+
+
+def kept_kernel(vectors_ref, first_ref, near_ref, far_ref, out_ref, gram_ref):
+    count, double, points = vectors_ref.shape
+    total = jnp.dot(vectors_ref[0], near_ref[:, :points], preferred_element_type=F32)
+    for k in range(1, count):
+        cov = far_ref[(k - 1) * points : k * points, :points]
+        total += jnp.dot(vectors_ref[k], cov, preferred_element_type=F32)
+    out_ref[...] = total[: double // 2] + total[double // 2 :]
+    gram_ref[...] = gram_of(first_ref[...])
+
+
+def kept(vectors, first, near_cov, far_cov):
+    size, points = first.shape
+    return pl.pallas_call(
+        kept_kernel,
+        out_shape=(pltpu.VMEM((size, points), F32), pltpu.VMEM((size, size), F32)),
+        compiler_params=PARAMS,
+        cost_estimate=cost(vectors.shape[0] * points * points // 8),
+        name="kept",
+    )(vectors, first, near_cov, far_cov)
 
 
 def gather_kernel(first_ref, own_ref, *refs):
@@ -392,15 +418,16 @@
     size, points = start.shape
     packed, feats = prepare(coords, intensity, start)
     if width == 16:
-        near_steps, far_steps = (1, 2, 3), (8, 13, 5)
+        near_steps, far_steps = (1, 2, 3), (13, 4, 9)
         blocks = [packed] + [exchange(packed, d, width) for d in far_steps]
         others = [exchange(feats, d, width) for d in near_steps]
         *features, near_cov, part = near(feats, blocks[:-1])
         edge_cov, far_cov, own, sent = far(part, *features, others, blocks[:-1], blocks[-1])
         parts = [exchange(own if d == 1 else sent, d, width) for d in near_steps]
-        *products, first_gram = second(own, parts, near_cov, edge_cov, far_cov)
-        got = [exchange(p, d, width) for p, d in zip(products[1:], far_steps)]
-        product, gram = gather_parts(first_gram, products[0], got)
+        *products, vectors, first = second(own, parts, near_cov, edge_cov, far_cov)
+        got = [exchange(p, d, width) for p, d in zip(products, far_steps)]
+        product, first_gram = kept(vectors, first, near_cov, far_cov)
+        product, gram = gather_parts(first_gram, product, got)
     else:
         everything = gather_blocks(packed, width)
         first_product = row_product(everything, feats)

time: 43 us -> 42.5 us (0.988)
  waiting for transfers between devices: 12.6 us -> 11.1 us
  starting transfers between devices: 18.9 us -> 19.6 us
    ppermute x18, waiting for transfers between devices: 12.6 us -> 11.1 us  [exchange(): lax.ppermute(value, 'wide', [(k, k ^ distance) for k in range(width)])]
    ppermute x18, starting transfers between devices: 18.9 us -> 19.6 us  [exchange(): lax.ppermute(value, 'wide', [(k, k ^ distance) for k in range(width)])]
    pallas_call x0 -> x1, Pallas kernels: none -> 0.49 us  [kept(): pl.pallas_call(kept_kernel, out_shape=(pltpu.VMEM((size, points), F32), p...]
  transfers between devices with their start and end apart: 18 -> 18, of which waited for: 9 -> 11; matrix products, arithmetic and copies ran while one was open for 0% -> 0% of each run, Pallas kernels for 4% -> 5%
where the time goes in v6:
time: 42.5 us; the launch traced here: 42.2 us
  starting transfers between devices  19.6 us (46%)
  waiting for transfers between devices  11.1 us (26%)
  Pallas kernels  10.9 us (26%)
  between operations  0.66 us (2%)
    ppermute x18, starting transfers between devices, exchange(): lax.ppermute(value, 'wide', [(k, k ^ distance) for k in range(width)])  19.6 us
    ppermute x18, waiting for transfers between devices, exchange(): lax.ppermute(value, 'wide', [(k, k ^ distance) for k in range(width)])  11.1 us
    pallas_call x1, Pallas kernels, far(): pl.pallas_call(functools.partial(far_kernel, len(feats)), out_shape=(pltp...  5.67 us
    pallas_call x1, Pallas kernels, near(): pl.pallas_call(functools.partial(near_kernel, len(packed)), out_shape=(pl...  1.54 us
    pallas_call x1, Pallas kernels, second(): pl.pallas_call(second_kernel, out_shape=[pltpu.VMEM((size, points), F32)]...  1.09 us
    pallas_call x1, Pallas kernels, finish(): pl.pallas_call(functools.partial(finish_kernel, total_points), out_shape=...  1.07 us
  transfers between devices with their start and end apart: 18, of which 11 were waited for; matrix products, arithmetic and copies ran while one was open for 0% of the time, Pallas kernels for 5%

profile of v6, /device:TPU:0, one launch (start us, length us, event | category | flops | bytes accessed | tf_op | source)
XLA Modules:
  0.0 42.2 jit_solution(13677160823692473730)
XLA Ops:
  0.6 0.8 %prepare.1 = (bf16[24,512]{1,0:T(8,128)(2,1)S(1)}, bf16[8,512]{1,0:T(8,128)(2,1)S(1)}) custom-call(f32[3,512]{1,0:T(4,128)} %refs_0_.1, f32[1,512]{1,0:T(1,128)} %bitcast.1, bf16[16,512]{1,0:T(8,128)(2,1)} %refs_2_.1), custom_call_target="tpu_custom_call" | custom-call | tf_op jit(solution)/shard_map/prepare/pallas_call | solution.py:102
  1.4 3.1 %collective-permute-start.1 = (bf16[24,512]{1,0:T(8,128)(2,1)S(1)}, bf16[24,512]{1,0:T(8,128)(2,1)S(1)}, u32[]{:S(2)}, u32[]{:S(2)}) collective-permute-start(bf16[24,512]{1,0:T(8,128)(2,1)S(1)} %get-tuple-element.24.refs_0_.refs_3_), channel_id=1, source_target_pairs={{0,4},{1,5},{2,6},{3,7},{4,0},{5,1},{6,2},{7,3},{8,12},{9,13},{10,... | collective-permute-start | bytes 73736 | tf_op jit(solution)/shard_map/ppermute | solution.py:394
  4.5 1.6 %collective-permute-start = (bf16[24,512]{1,0:T(8,128)(2,1)S(1)}, bf16[24,512]{1,0:T(8,128)(2,1)S(1)}, u32[]{:S(2)}, u32[]{:S(2)}) collective-permute-start(bf16[24,512]{1,0:T(8,128)(2,1)S(1)} %get-tuple-element.24.refs_0_.refs_3_), channel_id=1, source_target_pairs={{0,13},{1,12},{2,15},{3,14},{4,9},{5,8},{6,11},{7,10},{8,5},{9,4},... | collective-permute-start | bytes 73736 | tf_op jit(solution)/shard_map/ppermute | solution.py:394
  6.2 0.1 collective-permute-start.2
  6.3 2.1 %collective-permute-start.5 = (bf16[8,512]{1,0:T(8,128)(2,1)S(1)}, bf16[8,512]{1,0:T(8,128)(2,1)S(1)}, u32[]{:S(2)}, u32[]{:S(2)}) collective-permute-start(bf16[8,512]{1,0:T(8,128)(2,1)S(1)} %get-tuple-element.23.feats_ref), channel_id=1, source_target_pairs={{0,3},{1,2},{2,1},{3,0},{4,7},{5,6},{6,5},{7,4},{8,11},{9,10},{10,... | collective-permute-start | bytes 24584 | tf_op jit(solution)/shard_map/ppermute | solution.py:394
  8.4 0.5 %collective-permute-start.4 = (bf16[8,512]{1,0:T(8,128)(2,1)S(1)}, bf16[8,512]{1,0:T(8,128)(2,1)S(1)}, u32[]{:S(2)}, u32[]{:S(2)}) collective-permute-start(bf16[8,512]{1,0:T(8,128)(2,1)S(1)} %get-tuple-element.23.feats_ref), channel_id=1, source_target_pairs={{0,2},{1,3},{2,0},{3,1},{4,6},{5,7},{6,4},{7,5},{8,10},{9,11},{10,... | collective-permute-start | bytes 24584 | tf_op jit(solution)/shard_map/ppermute | solution.py:394
  8.9 0.0 collective-permute-done.1.refs_2_.refs_5_
  8.9 0.0 collective-permute-start.3
  8.9 0.7 %collective-permute-done.refs_1_.refs_4_ = bf16[24,512]{1,0:T(8,128)(2,1)S(1)} collective-permute-done((bf16[24,512]{1,0:T(8,128)(2,1)S(1)}, bf16[24,512]{1,0:T(8,128)(2,1)S(1)}, u32[]{:S(2)}, u32[]{:S(2)}) %collective-permute-start) | collective-permute-done | bytes 24608 | tf_op jit(solution)/shard_map/ppermute | solution.py:394
  9.6 1.5 %near.1 = (bf16[512,32]{1,0:T(8,128)(2,1)S(1)}, f32[512,128]{1,0:T(8,128)S(1)}, bf16[32,1536]{1,0:T(8,128)(2,1)S(1)}, f32[1,1536]{1,0:T(1,128)S(1)}, bf16[512,15...) custom-call(bf16[8,512]{1,0:T(8,128)(2,1)S(1)} %get-tuple-element.23.feats_ref, ...), custom_call_target="tpu_custom_call" | custom-call | flops 31457280 | bytes 1572864 | tf_op jit(solution)/shard_map/near/pallas_call | solution.py:138
  11.1 0.0 collective-permute-done.5.refs_2_
  11.1 0.9 %collective-permute-done.4.refs_1_ = bf16[8,512]{1,0:T(8,128)(2,1)S(1)} collective-permute-done((bf16[8,512]{1,0:T(8,128)(2,1)S(1)}, bf16[8,512]{1,0:T(8,128)(2,1)S(1)}, u32[]{:S(2)}, u32[]{:S(2)}) %collective-permute-start.4) | collective-permute-done | bytes 8224 | tf_op jit(solution)/shard_map/ppermute | solution.py:394
  12.0 0.0 collective-permute-done.3.refs_0_
  12.0 0.0 collective-permute-done.2.last_ref
  12.0 5.7 %far.1 = (bf16[512,512]{1,0:T(8,128)(2,1)S(1)}, bf16[1536,2048]{1,0:T(8,128)(2,1)S(1)}, f32[4,16,512]{2,1,0:T(8,128)S(1)}, bf16[4,16,512]{2,1,0:T(8,128)(2,1)S(1)}) custom-call(f32[16,512]{1,0:T(8,128)S(1)} %get-tuple-element.25.near_ref, bf16[512,32]{1,0:T(8,128)(2,1)S(1)} %get-tuple-element.26.rows_ref, f32[512,128]{1,0:T(8,128)S(1)} %get-tuple-element.27.row_logs_ref, ...), custom_call_target="tpu_custom_call" | custom-call | flops 167772160 | bytes 8388608 | tf_op jit(solution)/shard_map/far/pallas_call | solution.py:185
  17.7 0.0 collective-permute-start.6
  17.7 0.8 %collective-permute-start.8 = (bf16[4,16,512]{2,1,0:T(8,128)(2,1)S(1)}, bf16[4,16,512]{2,1,0:T(8,128)(2,1)S(1)}, u32[]{:S(2)}, u32[]{:S(2)}) collective-permute-start(bf16[4,16,512]{2,1,0:T(8,128)(2,1)S(1)} %get-tuple-element.31), channel_id=1, source_target_pairs={{0,3},{1,2},{2,1},{3,0},{4,7},{5,6},{6,5},{7,4},{8,11},{9,10},{10,... | collective-permute-start | bytes 196616 | tf_op jit(solution)/shard_map/ppermute | solution.py:394
  18.5 1.4 %collective-permute-start.7 = (bf16[4,16,512]{2,1,0:T(8,128)(2,1)S(1)}, bf16[4,16,512]{2,1,0:T(8,128)(2,1)S(1)}, u32[]{:S(2)}, u32[]{:S(2)}) collective-permute-start(bf16[4,16,512]{2,1,0:T(8,128)(2,1)S(1)} %get-tuple-element.31), channel_id=1, source_target_pairs={{0,2},{1,3},{2,0},{3,1},{4,6},{5,7},{6,4},{7,5},{8,10},{9,11},{10,... | collective-permute-start | bytes 196616 | tf_op jit(solution)/shard_map/ppermute | solution.py:394
  19.8 1.7 %collective-permute-done.8.refs_2_ = bf16[4,16,512]{2,1,0:T(8,128)(2,1)S(1)} collective-permute-done((bf16[4,16,512]{2,1,0:T(8,128)(2,1)S(1)}, bf16[4,16,512]{2,1,0:T(8,128)(2,1)S(1)}, u32[]{:S(2)}, u32[]{:S(2)}) %collective-permute-start.8) | collective-permute-done | bytes 65568 | tf_op jit(solution)/shard_map/ppermute | solution.py:394
  21.5 2.0 %collective-permute-done.7.refs_1_ = bf16[4,16,512]{2,1,0:T(8,128)(2,1)S(1)} collective-permute-done((bf16[4,16,512]{2,1,0:T(8,128)(2,1)S(1)}, bf16[4,16,512]{2,1,0:T(8,128)(2,1)S(1)}, u32[]{:S(2)}, u32[]{:S(2)}) %collective-permute-start.7) | collective-permute-done | bytes 65568 | tf_op jit(solution)/shard_map/ppermute | solution.py:394
  23.5 0.0 collective-permute-done.6.refs_0_
  23.5 1.1 %second.1 = (f32[16,512]{1,0:T(8,128)S(1)}, f32[16,512]{1,0:T(8,128)S(1)}, f32[16,512]{1,0:T(8,128)S(1)}, bf16[4,32,512]{2,1,0:T(8,128)(2,1)S(1)}, f32[16,512]{1,0:T(8,128)S(1)}) custom-call(f32[4,16,512]{2,1,0:T(8,128)S(1)} %get-tuple-element.30.own_ref, f32[4,16,512]{2,1,0:T(8,128)S(1)} %collective-permute-done.6.refs_0_, ...), custom_call_target="tpu_custom_call" | custom-call | flops 15728640 | bytes 786432 | tf_op jit(solution)/shard_map/second/pallas_call | solution.py:242
  24.6 1.4 %collective-permute-start.9 = (f32[16,512]{1,0:T(8,128)S(1)}, f32[16,512]{1,0:T(8,128)S(1)}, u32[]{:S(2)}, u32[]{:S(2)}) collective-permute-start(f32[16,512]{1,0:T(8,128)S(1)} %get-tuple-element.39), channel_id=1, source_target_pairs={{0,13},{1,12},{2,15},{3,14},{4,9},{5,8},{6,11},{7,10},{8,5},{9,4},... | collective-permute-start | bytes 98312 | tf_op jit(solution)/shard_map/ppermute | solution.py:394
  26.1 0.4 collective-permute-start.10
  26.5 2.0 %collective-permute-start.11 = (f32[16,512]{1,0:T(8,128)S(1)}, f32[16,512]{1,0:T(8,128)S(1)}, u32[]{:S(2)}, u32[]{:S(2)}) collective-permute-start(f32[16,512]{1,0:T(8,128)S(1)} %get-tuple-element.41), channel_id=1, source_target_pairs={{0,9},{1,8},{2,11},{3,10},{4,13},{5,12},{6,15},{7,14},{8,1},{9,0},... | collective-permute-start | bytes 98312 | tf_op jit(solution)/shard_map/ppermute | solution.py:394
  28.5 0.5 %kept.1 = (f32[16,512]{1,0:T(8,128)S(1)}, f32[16,16]{1,0:T(8,128)S(1)}) custom-call(bf16[4,32,512]{2,1,0:T(8,128)(2,1)S(1)} %get-tuple-element.35.vectors_ref, f32[16,512]{1,0:T(8,128)S(1)} %get-tuple-element.36.first_ref, bf16[512,1536]{1,0:T(8,128)(2,1)S(1)} %get-tuple-element.32.refs_3_.near_ref, bf16[1536,2048]{1,0:T(8,128)(2,1)S(1)} %get-tuple-element.34.refs_5_.far_ref), custom_call_target="tpu_custom_call" | custom-call | flops 5242880 | bytes 262144 | tf_op jit(solution)/shard_map/kept/pallas_call | solution.py:264
  29.0 0.9 %collective-permute-done.9.refs_0_ = f32[16,512]{1,0:T(8,128)S(1)} collective-permute-done((f32[16,512]{1,0:T(8,128)S(1)}, f32[16,512]{1,0:T(8,128)S(1)}, u32[]{:S(2)}, u32[]{:S(2)}) %collective-permute-start.9) | collective-permute-done | bytes 32800 | tf_op jit(solution)/shard_map/ppermute | solution.py:394
  29.8 1.0 %collective-permute-done.10.refs_1_ = f32[16,512]{1,0:T(8,128)S(1)} collective-permute-done((f32[16,512]{1,0:T(8,128)S(1)}, f32[16,512]{1,0:T(8,128)S(1)}, u32[]{:S(2)}, u32[]{:S(2)}) %collective-permute-start.10) | collective-permute-done | bytes 32800 | tf_op jit(solution)/shard_map/ppermute | solution.py:394
  30.9 0.0 collective-permute-done.11.refs_2_
  30.9 0.2 gather_parts.1
  31.1 1.3 %collective-permute-start.14 = (f32[8,64]{1,0:T(8,128)S(1)}, f32[8,64]{1,0:T(8,128)S(1)}, u32[]{:S(2)}, u32[]{:S(2)}) collective-permute-start(f32[8,64]{1,0:T(8,128)S(1)} %get-tuple-element.43), channel_id=1, source_target_pairs={{0,2},{1,3},{2,0},{3,1},{4,6},{5,7},{6,4},{7,5},{8,10},{9,11},{10,... | collective-permute-start | bytes 6152 | tf_op jit(solution)/shard_map/ppermute | solution.py:394
  32.4 0.9 %collective-permute-start.13 = (f32[8,64]{1,0:T(8,128)S(1)}, f32[8,64]{1,0:T(8,128)S(1)}, u32[]{:S(2)}, u32[]{:S(2)}) collective-permute-start(f32[8,64]{1,0:T(8,128)S(1)} %get-tuple-element.43), channel_id=1, source_target_pairs={{0,3},{1,2},{2,1},{3,0},{4,7},{5,6},{6,5},{7,4},{8,11},{9,10},{10,... | collective-permute-start | bytes 6152 | tf_op jit(solution)/shard_map/ppermute | solution.py:394
  33.3 0.0 collective-permute-start.12
  33.3 1.4 %collective-permute-done.14 = f32[8,64]{1,0:T(8,128)S(1)} collective-permute-done((f32[8,64]{1,0:T(8,128)S(1)}, f32[8,64]{1,0:T(8,128)S(1)}, u32[]{:S(2)}, u32[]{:S(2)}) %collective-permute-start.14) | collective-permute-done | bytes 2080 | tf_op jit(solution)/shard_map/ppermute | solution.py:394
  34.7 0.7 %collective-permute-done.13 = f32[8,64]{1,0:T(8,128)S(1)} collective-permute-done((f32[8,64]{1,0:T(8,128)S(1)}, f32[8,64]{1,0:T(8,128)S(1)}, u32[]{:S(2)}, u32[]{:S(2)}) %collective-permute-start.13) | collective-permute-done | bytes 2080 | tf_op jit(solution)/shard_map/ppermute | solution.py:394
  35.4 0.0 collective-permute-done.12
  35.5 1.4 %collective-permute-start.17 = (f32[8,64]{1,0:T(8,128)S(1)}, f32[8,64]{1,0:T(8,128)S(1)}, u32[]{:S(2)}, u32[]{:S(2)}) collective-permute-start(f32[8,64]{1,0:T(8,128)S(1)} %add_add_fusion.refs_0_), channel_id=1, source_target_pairs={{0,13},{1,12},{2,15},{3,14},{4,9},{5,8},{6,11},{7,10},{8,5},{9,4},... | collective-permute-start | bytes 6152 | tf_op jit(solution)/shard_map/ppermute | solution.py:394
  36.9 1.3 %collective-permute-start.16 = (f32[8,64]{1,0:T(8,128)S(1)}, f32[8,64]{1,0:T(8,128)S(1)}, u32[]{:S(2)}, u32[]{:S(2)}) collective-permute-start(f32[8,64]{1,0:T(8,128)S(1)} %add_add_fusion.refs_0_), channel_id=1, source_target_pairs={{0,9},{1,8},{2,11},{3,10},{4,13},{5,12},{6,15},{7,14},{8,1},{9,0},... | collective-permute-start | bytes 6152 | tf_op jit(solution)/shard_map/ppermute | solution.py:394
  38.1 1.2 %collective-permute-start.15 = (f32[8,64]{1,0:T(8,128)S(1)}, f32[8,64]{1,0:T(8,128)S(1)}, u32[]{:S(2)}, u32[]{:S(2)}) collective-permute-start(f32[8,64]{1,0:T(8,128)S(1)} %add_add_fusion.refs_0_), channel_id=1, source_target_pairs={{0,5},{1,4},{2,7},{3,6},{4,1},{5,0},{6,3},{7,2},{8,13},{9,12},{10,... | collective-permute-start | bytes 6152 | tf_op jit(solution)/shard_map/ppermute | solution.py:394
  39.3 1.0 %collective-permute-done.17.refs_3_ = f32[8,64]{1,0:T(8,128)S(1)} collective-permute-done((f32[8,64]{1,0:T(8,128)S(1)}, f32[8,64]{1,0:T(8,128)S(1)}, u32[]{:S(2)}, u32[]{:S(2)}) %collective-permute-start.17) | collective-permute-done | bytes 2080 | tf_op jit(solution)/shard_map/ppermute | solution.py:394
  40.4 0.4 %collective-permute-done.16.refs_2_ = f32[8,64]{1,0:T(8,128)S(1)} collective-permute-done((f32[8,64]{1,0:T(8,128)S(1)}, f32[8,64]{1,0:T(8,128)S(1)}, u32[]{:S(2)}, u32[]{:S(2)}) %collective-permute-start.16) | collective-permute-done | bytes 2080 | tf_op jit(solution)/shard_map/ppermute | solution.py:394
  40.8 0.4 collective-permute-done.15.refs_1_
  41.2 1.1 %finish.1 = (f32[16,512]{1,0:T(8,128)}, f32[16,16]{1,0:T(8,128)}) custom-call(f32[16,512]{1,0:T(8,128)S(1)} %get-tuple-element.42.product_ref, f32[8,64]{1,0:T(8,128)S(1)} %add_add_fusion.refs_0_, f32[8,64]{1,0:T(8,128)S(1)} %collective-permute-done.15.refs_1_, f32[8,64]{1,0:T(8,128)S(1)} %collective-permute-done.16.refs_2_, ...), custom_call_target="tpu_custom_call" | custom-call | tf_op jit(solution)/shard_map/finish/pallas_call | solution.py:375
  (1 shorter events, 0.0 us)
Async XLA Ops:
  1.4 7.4 %collective-permute-start.1 = (bf16[24,512]{1,0:T(8,128)(2,1)S(1)}, bf16[24,512]{1,0:T(8,128)(2,1)S(1)}, u32[]{:S(2)}, u32[]{:S(2)}) collective-permute-start(bf16[24,512]{1,0:T(8,128)(2,1)S(1)} %get-tuple-element.24.refs_0_.refs_3_), channel_id=1, source_target_pairs={{0,4},{1,5},{2,6},{3,7},{4,0},{5,1},{6,2},{7,3},{8,12},{9,13},{10,... | collective-permute-start | bytes 73736 | tf_op jit(solution)/shard_map/ppermute | solution.py:394
  4.5 5.0 %collective-permute-start = (bf16[24,512]{1,0:T(8,128)(2,1)S(1)}, bf16[24,512]{1,0:T(8,128)(2,1)S(1)}, u32[]{:S(2)}, u32[]{:S(2)}) collective-permute-start(bf16[24,512]{1,0:T(8,128)(2,1)S(1)} %get-tuple-element.24.refs_0_.refs_3_), channel_id=1, source_target_pairs={{0,13},{1,12},{2,15},{3,14},{4,9},{5,8},{6,11},{7,10},{8,5},{9,4},... | collective-permute-start | bytes 73736 | tf_op jit(solution)/shard_map/ppermute | solution.py:394
  6.2 5.9 %collective-permute-start.2 = (bf16[24,512]{1,0:T(8,128)(2,1)S(1)}, bf16[24,512]{1,0:T(8,128)(2,1)S(1)}, u32[]{:S(2)}, u32[]{:S(2)}) collective-permute-start(bf16[24,512]{1,0:T(8,128)(2,1)S(1)} %get-tuple-element.24.refs_0_.refs_3_), channel_id=1, source_target_pairs={{0,9},{1,8},{2,11},{3,10},{4,13},{5,12},{6,15},{7,14},{8,1},{9,0},... | collective-permute-start | bytes 73736 | tf_op jit(solution)/shard_map/ppermute | solution.py:394
  6.3 4.8 %collective-permute-start.5 = (bf16[8,512]{1,0:T(8,128)(2,1)S(1)}, bf16[8,512]{1,0:T(8,128)(2,1)S(1)}, u32[]{:S(2)}, u32[]{:S(2)}) collective-permute-start(bf16[8,512]{1,0:T(8,128)(2,1)S(1)} %get-tuple-element.23.feats_ref), channel_id=1, source_target_pairs={{0,3},{1,2},{2,1},{3,0},{4,7},{5,6},{6,5},{7,4},{8,11},{9,10},{10,... | collective-permute-start | bytes 24584 | tf_op jit(solution)/shard_map/ppermute | solution.py:394
  8.4 3.7 %collective-permute-start.4 = (bf16[8,512]{1,0:T(8,128)(2,1)S(1)}, bf16[8,512]{1,0:T(8,128)(2,1)S(1)}, u32[]{:S(2)}, u32[]{:S(2)}) collective-permute-start(bf16[8,512]{1,0:T(8,128)(2,1)S(1)} %get-tuple-element.23.feats_ref), channel_id=1, source_target_pairs={{0,2},{1,3},{2,0},{3,1},{4,6},{5,7},{6,4},{7,5},{8,10},{9,11},{10,... | collective-permute-start | bytes 24584 | tf_op jit(solution)/shard_map/ppermute | solution.py:394
  8.9 3.1 %collective-permute-start.3 = (bf16[8,512]{1,0:T(8,128)(2,1)S(1)}, bf16[8,512]{1,0:T(8,128)(2,1)S(1)}, u32[]{:S(2)}, u32[]{:S(2)}) collective-permute-start(bf16[8,512]{1,0:T(8,128)(2,1)S(1)} %get-tuple-element.23.feats_ref), channel_id=1, source_target_pairs={{0,1},{1,0},{2,3},{3,2},{4,5},{5,4},{6,7},{7,6},{8,9},{9,8},{10,11... | collective-permute-start | bytes 24584 | tf_op jit(solution)/shard_map/ppermute | solution.py:394
  17.7 5.8 %collective-permute-start.6 = (f32[4,16,512]{2,1,0:T(8,128)S(1)}, f32[4,16,512]{2,1,0:T(8,128)S(1)}, u32[]{:S(2)}, u32[]{:S(2)}) collective-permute-start(f32[4,16,512]{2,1,0:T(8,128)S(1)} %get-tuple-element.30.own_ref), channel_id=1, source_target_pairs={{0,1},{1,0},{2,3},{3,2},{4,5},{5,4},{6,7},{7,6},{8,9},{9,8},{10,11... | collective-permute-start | bytes 393224 | tf_op jit(solution)/shard_map/ppermute | solution.py:394
  17.7 3.8 %collective-permute-start.8 = (bf16[4,16,512]{2,1,0:T(8,128)(2,1)S(1)}, bf16[4,16,512]{2,1,0:T(8,128)(2,1)S(1)}, u32[]{:S(2)}, u32[]{:S(2)}) collective-permute-start(bf16[4,16,512]{2,1,0:T(8,128)(2,1)S(1)} %get-tuple-element.31), channel_id=1, source_target_pairs={{0,3},{1,2},{2,1},{3,0},{4,7},{5,6},{6,5},{7,4},{8,11},{9,10},{10,... | collective-permute-start | bytes 196616 | tf_op jit(solution)/shard_map/ppermute | solution.py:394
  18.5 5.0 %collective-permute-start.7 = (bf16[4,16,512]{2,1,0:T(8,128)(2,1)S(1)}, bf16[4,16,512]{2,1,0:T(8,128)(2,1)S(1)}, u32[]{:S(2)}, u32[]{:S(2)}) collective-permute-start(bf16[4,16,512]{2,1,0:T(8,128)(2,1)S(1)} %get-tuple-element.31), channel_id=1, source_target_pairs={{0,2},{1,3},{2,0},{3,1},{4,6},{5,7},{6,4},{7,5},{8,10},{9,11},{10,... | collective-permute-start | bytes 196616 | tf_op jit(solution)/shard_map/ppermute | solution.py:394
  24.6 5.2 %collective-permute-start.9 = (f32[16,512]{1,0:T(8,128)S(1)}, f32[16,512]{1,0:T(8,128)S(1)}, u32[]{:S(2)}, u32[]{:S(2)}) collective-permute-start(f32[16,512]{1,0:T(8,128)S(1)} %get-tuple-element.39), channel_id=1, source_target_pairs={{0,13},{1,12},{2,15},{3,14},{4,9},{5,8},{6,11},{7,10},{8,5},{9,4},... | collective-permute-start | bytes 98312 | tf_op jit(solution)/shard_map/ppermute | solution.py:394
  26.1 4.8 %collective-permute-start.10 = (f32[16,512]{1,0:T(8,128)S(1)}, f32[16,512]{1,0:T(8,128)S(1)}, u32[]{:S(2)}, u32[]{:S(2)}) collective-permute-start(f32[16,512]{1,0:T(8,128)S(1)} %get-tuple-element.40), channel_id=1, source_target_pairs={{0,4},{1,5},{2,6},{3,7},{4,0},{5,1},{6,2},{7,3},{8,12},{9,13},{10,... | collective-permute-start | bytes 98312 | tf_op jit(solution)/shard_map/ppermute | solution.py:394
  26.5 4.4 %collective-permute-start.11 = (f32[16,512]{1,0:T(8,128)S(1)}, f32[16,512]{1,0:T(8,128)S(1)}, u32[]{:S(2)}, u32[]{:S(2)}) collective-permute-start(f32[16,512]{1,0:T(8,128)S(1)} %get-tuple-element.41), channel_id=1, source_target_pairs={{0,9},{1,8},{2,11},{3,10},{4,13},{5,12},{6,15},{7,14},{8,1},{9,0},... | collective-permute-start | bytes 98312 | tf_op jit(solution)/shard_map/ppermute | solution.py:394
  31.1 3.6 %collective-permute-start.14 = (f32[8,64]{1,0:T(8,128)S(1)}, f32[8,64]{1,0:T(8,128)S(1)}, u32[]{:S(2)}, u32[]{:S(2)}) collective-permute-start(f32[8,64]{1,0:T(8,128)S(1)} %get-tuple-element.43), channel_id=1, source_target_pairs={{0,2},{1,3},{2,0},{3,1},{4,6},{5,7},{6,4},{7,5},{8,10},{9,11},{10,... | collective-permute-start | bytes 6152 | tf_op jit(solution)/shard_map/ppermute | solution.py:394
  32.4 3.0 %collective-permute-start.13 = (f32[8,64]{1,0:T(8,128)S(1)}, f32[8,64]{1,0:T(8,128)S(1)}, u32[]{:S(2)}, u32[]{:S(2)}) collective-permute-start(f32[8,64]{1,0:T(8,128)S(1)} %get-tuple-element.43), channel_id=1, source_target_pairs={{0,3},{1,2},{2,1},{3,0},{4,7},{5,6},{6,5},{7,4},{8,11},{9,10},{10,... | collective-permute-start | bytes 6152 | tf_op jit(solution)/shard_map/ppermute | solution.py:394
  33.3 2.1 %collective-permute-start.12 = (f32[8,64]{1,0:T(8,128)S(1)}, f32[8,64]{1,0:T(8,128)S(1)}, u32[]{:S(2)}, u32[]{:S(2)}) collective-permute-start(f32[8,64]{1,0:T(8,128)S(1)} %get-tuple-element.43), channel_id=1, source_target_pairs={{0,1},{1,0},{2,3},{3,2},{4,5},{5,4},{6,7},{7,6},{8,9},{9,8},{10,11... | collective-permute-start | bytes 6152 | tf_op jit(solution)/shard_map/ppermute | solution.py:394
  35.5 4.9 %collective-permute-start.17 = (f32[8,64]{1,0:T(8,128)S(1)}, f32[8,64]{1,0:T(8,128)S(1)}, u32[]{:S(2)}, u32[]{:S(2)}) collective-permute-start(f32[8,64]{1,0:T(8,128)S(1)} %add_add_fusion.refs_0_), channel_id=1, source_target_pairs={{0,13},{1,12},{2,15},{3,14},{4,9},{5,8},{6,11},{7,10},{8,5},{9,4},... | collective-permute-start | bytes 6152 | tf_op jit(solution)/shard_map/ppermute | solution.py:394
  36.9 3.9 %collective-permute-start.16 = (f32[8,64]{1,0:T(8,128)S(1)}, f32[8,64]{1,0:T(8,128)S(1)}, u32[]{:S(2)}, u32[]{:S(2)}) collective-permute-start(f32[8,64]{1,0:T(8,128)S(1)} %add_add_fusion.refs_0_), channel_id=1, source_target_pairs={{0,9},{1,8},{2,11},{3,10},{4,13},{5,12},{6,15},{7,14},{8,1},{9,0},... | collective-permute-start | bytes 6152 | tf_op jit(solution)/shard_map/ppermute | solution.py:394
  38.1 3.0 %collective-permute-start.15 = (f32[8,64]{1,0:T(8,128)S(1)}, f32[8,64]{1,0:T(8,128)S(1)}, u32[]{:S(2)}, u32[]{:S(2)}) collective-permute-start(f32[8,64]{1,0:T(8,128)S(1)} %add_add_fusion.refs_0_), channel_id=1, source_target_pairs={{0,5},{1,4},{2,7},{3,6},{4,1},{5,0},{6,3},{7,2},{8,13},{9,12},{10,... | collective-permute-start | bytes 6152 | tf_op jit(solution)/shard_map/ppermute | solution.py:394

commit v7 on v6

--- a/solution.py
+++ b/solution.py
@@ -217,13 +217,13 @@
     vectors_ref, first_ref = refs[-2:]
     count, size, points = own_ref.shape
     last = len(outs)
-    totals = [jnp.zeros((2 * size, points), F32) for _ in outs]
+    totals = [jnp.zeros((size, points), F32) for _ in outs]
     for k in range(count):
         a, b, c = (ref[k ^ (n + 1)].astype(F32) for n, ref in enumerate(part_refs))
         product = (own_ref[k] + a) + (b + c)
         if k == 0:
             first_ref[...] = product
-        vectors = jnp.concatenate(split(product, 2), axis=0).astype(BF16)
+        vectors = product.astype(BF16)
         vectors_ref[k] = vectors
         for n in range(1, last + 1):
             to = slice(n * points, (n + 1) * points)
@@ -233,7 +233,7 @@
                 cov = far_ref[(k - 1) * points : k * points, to]
             totals[n - 1] += jnp.dot(vectors, cov, preferred_element_type=F32)
     for ref, total in zip(outs, totals):
-        ref[...] = total[:size] + total[size:]
+        ref[...] = total
 
 
 def second(own, parts, near_cov, edge_cov, far_cov):
@@ -242,7 +242,7 @@
     return pl.pallas_call(
         second_kernel,
         out_shape=[pltpu.VMEM((size, points), F32)] * others
-        + [pltpu.VMEM((count, 2 * size, points), BF16), pltpu.VMEM((size, points), F32)],
+        + [pltpu.VMEM((count, size, points), BF16), pltpu.VMEM((size, points), F32)],
         compiler_params=PARAMS,
         cost_estimate=cost(count * points * others * points // 8),
         name="second",
@@ -250,12 +250,12 @@
 
 
 def kept_kernel(vectors_ref, first_ref, near_ref, far_ref, out_ref, gram_ref):
-    count, double, points = vectors_ref.shape
+    count, _, points = vectors_ref.shape
     total = jnp.dot(vectors_ref[0], near_ref[:, :points], preferred_element_type=F32)
     for k in range(1, count):
         cov = far_ref[(k - 1) * points : k * points, :points]
         total += jnp.dot(vectors_ref[k], cov, preferred_element_type=F32)
-    out_ref[...] = total[: double // 2] + total[double // 2 :]
+    out_ref[...] = total
     gram_ref[...] = gram_of(first_ref[...])
 
 

time: 42.5 us -> 42.4 us (level)
  no operation moved by 1% of the time
where the time goes in v7:
time: 42.4 us; the launch traced here: 42.1 us
  starting transfers between devices  19.6 us (46%)
  waiting for transfers between devices  11.2 us (26%)
  Pallas kernels  10.6 us (25%)
  between operations  0.66 us (2%)
    ppermute x18, starting transfers between devices, exchange(): lax.ppermute(value, 'wide', [(k, k ^ distance) for k in range(width)])  19.6 us
    ppermute x18, waiting for transfers between devices, exchange(): lax.ppermute(value, 'wide', [(k, k ^ distance) for k in range(width)])  11.2 us
    pallas_call x1, Pallas kernels, far(): pl.pallas_call(functools.partial(far_kernel, len(feats)), out_shape=(pltp...  5.67 us
    pallas_call x1, Pallas kernels, near(): pl.pallas_call(functools.partial(near_kernel, len(packed)), out_shape=(pl...  1.54 us
    pallas_call x1, Pallas kernels, finish(): pl.pallas_call(functools.partial(finish_kernel, total_points), out_shape=...  1.07 us
    pallas_call x1, Pallas kernels, second(): pl.pallas_call(second_kernel, out_shape=[pltpu.VMEM((size, points), F32)]...  0.91 us
  transfers between devices with their start and end apart: 18, of which 11 were waited for; matrix products, arithmetic and copies ran while one was open for 0% of the time, Pallas kernels for 5%

profile of v7, /device:TPU:0, one launch (start us, length us, event | category | flops | bytes accessed | tf_op | source)
XLA Modules:
  0.0 42.1 jit_solution(2420296186746042819)
XLA Ops:
  0.6 0.8 %prepare.1 = (bf16[24,512]{1,0:T(8,128)(2,1)S(1)}, bf16[8,512]{1,0:T(8,128)(2,1)S(1)}) custom-call(f32[3,512]{1,0:T(4,128)} %refs_0_.1, f32[1,512]{1,0:T(1,128)} %bitcast.1, bf16[16,512]{1,0:T(8,128)(2,1)} %refs_2_.1), custom_call_target="tpu_custom_call" | custom-call | tf_op jit(solution)/shard_map/prepare/pallas_call | solution.py:102
  1.4 3.1 %collective-permute-start.1 = (bf16[24,512]{1,0:T(8,128)(2,1)S(1)}, bf16[24,512]{1,0:T(8,128)(2,1)S(1)}, u32[]{:S(2)}, u32[]{:S(2)}) collective-permute-start(bf16[24,512]{1,0:T(8,128)(2,1)S(1)} %get-tuple-element.24.refs_0_.refs_3_), channel_id=1, source_target_pairs={{0,4},{1,5},{2,6},{3,7},{4,0},{5,1},{6,2},{7,3},{8,12},{9,13},{10,... | collective-permute-start | bytes 73736 | tf_op jit(solution)/shard_map/ppermute | solution.py:394
  4.5 1.6 %collective-permute-start = (bf16[24,512]{1,0:T(8,128)(2,1)S(1)}, bf16[24,512]{1,0:T(8,128)(2,1)S(1)}, u32[]{:S(2)}, u32[]{:S(2)}) collective-permute-start(bf16[24,512]{1,0:T(8,128)(2,1)S(1)} %get-tuple-element.24.refs_0_.refs_3_), channel_id=1, source_target_pairs={{0,13},{1,12},{2,15},{3,14},{4,9},{5,8},{6,11},{7,10},{8,5},{9,4},... | collective-permute-start | bytes 73736 | tf_op jit(solution)/shard_map/ppermute | solution.py:394
  6.2 0.1 collective-permute-start.2
  6.3 2.1 %collective-permute-start.5 = (bf16[8,512]{1,0:T(8,128)(2,1)S(1)}, bf16[8,512]{1,0:T(8,128)(2,1)S(1)}, u32[]{:S(2)}, u32[]{:S(2)}) collective-permute-start(bf16[8,512]{1,0:T(8,128)(2,1)S(1)} %get-tuple-element.23.feats_ref), channel_id=1, source_target_pairs={{0,3},{1,2},{2,1},{3,0},{4,7},{5,6},{6,5},{7,4},{8,11},{9,10},{10,... | collective-permute-start | bytes 24584 | tf_op jit(solution)/shard_map/ppermute | solution.py:394
  8.4 0.5 %collective-permute-start.4 = (bf16[8,512]{1,0:T(8,128)(2,1)S(1)}, bf16[8,512]{1,0:T(8,128)(2,1)S(1)}, u32[]{:S(2)}, u32[]{:S(2)}) collective-permute-start(bf16[8,512]{1,0:T(8,128)(2,1)S(1)} %get-tuple-element.23.feats_ref), channel_id=1, source_target_pairs={{0,2},{1,3},{2,0},{3,1},{4,6},{5,7},{6,4},{7,5},{8,10},{9,11},{10,... | collective-permute-start | bytes 24584 | tf_op jit(solution)/shard_map/ppermute | solution.py:394
  8.9 0.0 collective-permute-done.1.refs_2_.refs_5_
  8.9 0.0 collective-permute-start.3
  8.9 0.7 %collective-permute-done.refs_1_.refs_4_ = bf16[24,512]{1,0:T(8,128)(2,1)S(1)} collective-permute-done((bf16[24,512]{1,0:T(8,128)(2,1)S(1)}, bf16[24,512]{1,0:T(8,128)(2,1)S(1)}, u32[]{:S(2)}, u32[]{:S(2)}) %collective-permute-start) | collective-permute-done | bytes 24608 | tf_op jit(solution)/shard_map/ppermute | solution.py:394
  9.6 1.5 %near.1 = (bf16[512,32]{1,0:T(8,128)(2,1)S(1)}, f32[512,128]{1,0:T(8,128)S(1)}, bf16[32,1536]{1,0:T(8,128)(2,1)S(1)}, f32[1,1536]{1,0:T(1,128)S(1)}, bf16[512,15...) custom-call(bf16[8,512]{1,0:T(8,128)(2,1)S(1)} %get-tuple-element.23.feats_ref, ...), custom_call_target="tpu_custom_call" | custom-call | flops 31457280 | bytes 1572864 | tf_op jit(solution)/shard_map/near/pallas_call | solution.py:138
  11.1 0.0 collective-permute-done.5.refs_2_
  11.1 0.9 %collective-permute-done.4.refs_1_ = bf16[8,512]{1,0:T(8,128)(2,1)S(1)} collective-permute-done((bf16[8,512]{1,0:T(8,128)(2,1)S(1)}, bf16[8,512]{1,0:T(8,128)(2,1)S(1)}, u32[]{:S(2)}, u32[]{:S(2)}) %collective-permute-start.4) | collective-permute-done | bytes 8224 | tf_op jit(solution)/shard_map/ppermute | solution.py:394
  12.0 0.0 collective-permute-done.3.refs_0_
  12.0 0.0 collective-permute-done.2.last_ref
  12.0 5.7 %far.1 = (bf16[512,512]{1,0:T(8,128)(2,1)S(1)}, bf16[1536,2048]{1,0:T(8,128)(2,1)S(1)}, f32[4,16,512]{2,1,0:T(8,128)S(1)}, bf16[4,16,512]{2,1,0:T(8,128)(2,1)S(1)}) custom-call(f32[16,512]{1,0:T(8,128)S(1)} %get-tuple-element.25.near_ref, bf16[512,32]{1,0:T(8,128)(2,1)S(1)} %get-tuple-element.26.rows_ref, f32[512,128]{1,0:T(8,128)S(1)} %get-tuple-element.27.row_logs_ref, ...), custom_call_target="tpu_custom_call" | custom-call | flops 167772160 | bytes 8388608 | tf_op jit(solution)/shard_map/far/pallas_call | solution.py:185
  17.7 0.0 collective-permute-start.6
  17.7 0.8 %collective-permute-start.8 = (bf16[4,16,512]{2,1,0:T(8,128)(2,1)S(1)}, bf16[4,16,512]{2,1,0:T(8,128)(2,1)S(1)}, u32[]{:S(2)}, u32[]{:S(2)}) collective-permute-start(bf16[4,16,512]{2,1,0:T(8,128)(2,1)S(1)} %get-tuple-element.31), channel_id=1, source_target_pairs={{0,3},{1,2},{2,1},{3,0},{4,7},{5,6},{6,5},{7,4},{8,11},{9,10},{10,... | collective-permute-start | bytes 196616 | tf_op jit(solution)/shard_map/ppermute | solution.py:394
  18.5 1.4 %collective-permute-start.7 = (bf16[4,16,512]{2,1,0:T(8,128)(2,1)S(1)}, bf16[4,16,512]{2,1,0:T(8,128)(2,1)S(1)}, u32[]{:S(2)}, u32[]{:S(2)}) collective-permute-start(bf16[4,16,512]{2,1,0:T(8,128)(2,1)S(1)} %get-tuple-element.31), channel_id=1, source_target_pairs={{0,2},{1,3},{2,0},{3,1},{4,6},{5,7},{6,4},{7,5},{8,10},{9,11},{10,... | collective-permute-start | bytes 196616 | tf_op jit(solution)/shard_map/ppermute | solution.py:394
  19.8 1.7 %collective-permute-done.8.refs_2_ = bf16[4,16,512]{2,1,0:T(8,128)(2,1)S(1)} collective-permute-done((bf16[4,16,512]{2,1,0:T(8,128)(2,1)S(1)}, bf16[4,16,512]{2,1,0:T(8,128)(2,1)S(1)}, u32[]{:S(2)}, u32[]{:S(2)}) %collective-permute-start.8) | collective-permute-done | bytes 65568 | tf_op jit(solution)/shard_map/ppermute | solution.py:394
  21.5 2.0 %collective-permute-done.7.refs_1_ = bf16[4,16,512]{2,1,0:T(8,128)(2,1)S(1)} collective-permute-done((bf16[4,16,512]{2,1,0:T(8,128)(2,1)S(1)}, bf16[4,16,512]{2,1,0:T(8,128)(2,1)S(1)}, u32[]{:S(2)}, u32[]{:S(2)}) %collective-permute-start.7) | collective-permute-done | bytes 65568 | tf_op jit(solution)/shard_map/ppermute | solution.py:394
  23.5 0.0 collective-permute-done.6.refs_0_
  23.5 0.9 %second.1 = (f32[16,512]{1,0:T(8,128)S(1)}, f32[16,512]{1,0:T(8,128)S(1)}, f32[16,512]{1,0:T(8,128)S(1)}, bf16[4,16,512]{2,1,0:T(8,128)(2,1)S(1)}, f32[16,512]{1,0:T(8,128)S(1)}) custom-call(f32[4,16,512]{2,1,0:T(8,128)S(1)} %get-tuple-element.30.own_ref, f32[4,16,512]{2,1,0:T(8,128)S(1)} %collective-permute-done.6.refs_0_, ...), custom_call_target="tpu_custom_call" | custom-call | flops 15728640 | bytes 786432 | tf_op jit(solution)/shard_map/second/pallas_call | solution.py:242
  24.4 1.4 %collective-permute-start.9 = (f32[16,512]{1,0:T(8,128)S(1)}, f32[16,512]{1,0:T(8,128)S(1)}, u32[]{:S(2)}, u32[]{:S(2)}) collective-permute-start(f32[16,512]{1,0:T(8,128)S(1)} %get-tuple-element.39), channel_id=1, source_target_pairs={{0,13},{1,12},{2,15},{3,14},{4,9},{5,8},{6,11},{7,10},{8,5},{9,4},... | collective-permute-start | bytes 98312 | tf_op jit(solution)/shard_map/ppermute | solution.py:394
  25.9 0.4 %collective-permute-start.10 = (f32[16,512]{1,0:T(8,128)S(1)}, f32[16,512]{1,0:T(8,128)S(1)}, u32[]{:S(2)}, u32[]{:S(2)}) collective-permute-start(f32[16,512]{1,0:T(8,128)S(1)} %get-tuple-element.40), channel_id=1, source_target_pairs={{0,4},{1,5},{2,6},{3,7},{4,0},{5,1},{6,2},{7,3},{8,12},{9,13},{10,... | collective-permute-start | bytes 98312 | tf_op jit(solution)/shard_map/ppermute | solution.py:394
  26.3 2.0 %collective-permute-start.11 = (f32[16,512]{1,0:T(8,128)S(1)}, f32[16,512]{1,0:T(8,128)S(1)}, u32[]{:S(2)}, u32[]{:S(2)}) collective-permute-start(f32[16,512]{1,0:T(8,128)S(1)} %get-tuple-element.41), channel_id=1, source_target_pairs={{0,9},{1,8},{2,11},{3,10},{4,13},{5,12},{6,15},{7,14},{8,1},{9,0},... | collective-permute-start | bytes 98312 | tf_op jit(solution)/shard_map/ppermute | solution.py:394
  28.3 0.4 %kept.1 = (f32[16,512]{1,0:T(8,128)S(1)}, f32[16,16]{1,0:T(8,128)S(1)}) custom-call(bf16[4,16,512]{2,1,0:T(8,128)(2,1)S(1)} %get-tuple-element.35.vectors_ref, f32[16,512]{1,0:T(8,128)S(1)} %get-tuple-element.36.first_ref, bf16[512,1536]{1,0:T(8,128)(2,1)S(1)} %get-tuple-element.32.refs_3_.near_ref, bf16[1536,2048]{1,0:T(8,128)(2,1)S(1)} %get-tuple-element.34.refs_5_.far_ref), custom_call_target="tpu_custom_call" | custom-call | flops 5242880 | bytes 262144 | tf_op jit(solution)/shard_map/kept/pallas_call | solution.py:264
  28.7 0.9 %collective-permute-done.9.refs_0_ = f32[16,512]{1,0:T(8,128)S(1)} collective-permute-done((f32[16,512]{1,0:T(8,128)S(1)}, f32[16,512]{1,0:T(8,128)S(1)}, u32[]{:S(2)}, u32[]{:S(2)}) %collective-permute-start.9) | collective-permute-done | bytes 32800 | tf_op jit(solution)/shard_map/ppermute | solution.py:394
  29.6 1.0 %collective-permute-done.10.refs_1_ = f32[16,512]{1,0:T(8,128)S(1)} collective-permute-done((f32[16,512]{1,0:T(8,128)S(1)}, f32[16,512]{1,0:T(8,128)S(1)}, u32[]{:S(2)}, u32[]{:S(2)}) %collective-permute-start.10) | collective-permute-done | bytes 32800 | tf_op jit(solution)/shard_map/ppermute | solution.py:394
  30.7 0.0 collective-permute-done.11.refs_2_
  30.7 0.2 gather_parts.1
  30.9 1.3 %collective-permute-start.14 = (f32[8,64]{1,0:T(8,128)S(1)}, f32[8,64]{1,0:T(8,128)S(1)}, u32[]{:S(2)}, u32[]{:S(2)}) collective-permute-start(f32[8,64]{1,0:T(8,128)S(1)} %get-tuple-element.43), channel_id=1, source_target_pairs={{0,2},{1,3},{2,0},{3,1},{4,6},{5,7},{6,4},{7,5},{8,10},{9,11},{10,... | collective-permute-start | bytes 6152 | tf_op jit(solution)/shard_map/ppermute | solution.py:394
  32.2 0.9 %collective-permute-start.13 = (f32[8,64]{1,0:T(8,128)S(1)}, f32[8,64]{1,0:T(8,128)S(1)}, u32[]{:S(2)}, u32[]{:S(2)}) collective-permute-start(f32[8,64]{1,0:T(8,128)S(1)} %get-tuple-element.43), channel_id=1, source_target_pairs={{0,3},{1,2},{2,1},{3,0},{4,7},{5,6},{6,5},{7,4},{8,11},{9,10},{10,... | collective-permute-start | bytes 6152 | tf_op jit(solution)/shard_map/ppermute | solution.py:394
  33.2 0.0 collective-permute-start.12
  33.2 1.4 %collective-permute-done.14 = f32[8,64]{1,0:T(8,128)S(1)} collective-permute-done((f32[8,64]{1,0:T(8,128)S(1)}, f32[8,64]{1,0:T(8,128)S(1)}, u32[]{:S(2)}, u32[]{:S(2)}) %collective-permute-start.14) | collective-permute-done | bytes 2080 | tf_op jit(solution)/shard_map/ppermute | solution.py:394
  34.5 0.7 %collective-permute-done.13 = f32[8,64]{1,0:T(8,128)S(1)} collective-permute-done((f32[8,64]{1,0:T(8,128)S(1)}, f32[8,64]{1,0:T(8,128)S(1)}, u32[]{:S(2)}, u32[]{:S(2)}) %collective-permute-start.13) | collective-permute-done | bytes 2080 | tf_op jit(solution)/shard_map/ppermute | solution.py:394
  35.3 0.0 collective-permute-done.12
  35.3 1.4 %collective-permute-start.17 = (f32[8,64]{1,0:T(8,128)S(1)}, f32[8,64]{1,0:T(8,128)S(1)}, u32[]{:S(2)}, u32[]{:S(2)}) collective-permute-start(f32[8,64]{1,0:T(8,128)S(1)} %add_add_fusion.refs_0_), channel_id=1, source_target_pairs={{0,13},{1,12},{2,15},{3,14},{4,9},{5,8},{6,11},{7,10},{8,5},{9,4},... | collective-permute-start | bytes 6152 | tf_op jit(solution)/shard_map/ppermute | solution.py:394
  36.7 1.3 %collective-permute-start.16 = (f32[8,64]{1,0:T(8,128)S(1)}, f32[8,64]{1,0:T(8,128)S(1)}, u32[]{:S(2)}, u32[]{:S(2)}) collective-permute-start(f32[8,64]{1,0:T(8,128)S(1)} %add_add_fusion.refs_0_), channel_id=1, source_target_pairs={{0,9},{1,8},{2,11},{3,10},{4,13},{5,12},{6,15},{7,14},{8,1},{9,0},... | collective-permute-start | bytes 6152 | tf_op jit(solution)/shard_map/ppermute | solution.py:394
  38.0 1.2 %collective-permute-start.15 = (f32[8,64]{1,0:T(8,128)S(1)}, f32[8,64]{1,0:T(8,128)S(1)}, u32[]{:S(2)}, u32[]{:S(2)}) collective-permute-start(f32[8,64]{1,0:T(8,128)S(1)} %add_add_fusion.refs_0_), channel_id=1, source_target_pairs={{0,5},{1,4},{2,7},{3,6},{4,1},{5,0},{6,3},{7,2},{8,13},{9,12},{10,... | collective-permute-start | bytes 6152 | tf_op jit(solution)/shard_map/ppermute | solution.py:394
  39.2 1.0 %collective-permute-done.17.refs_3_ = f32[8,64]{1,0:T(8,128)S(1)} collective-permute-done((f32[8,64]{1,0:T(8,128)S(1)}, f32[8,64]{1,0:T(8,128)S(1)}, u32[]{:S(2)}, u32[]{:S(2)}) %collective-permute-start.17) | collective-permute-done | bytes 2080 | tf_op jit(solution)/shard_map/ppermute | solution.py:394
  40.2 0.4 %collective-permute-done.16.refs_2_ = f32[8,64]{1,0:T(8,128)S(1)} collective-permute-done((f32[8,64]{1,0:T(8,128)S(1)}, f32[8,64]{1,0:T(8,128)S(1)}, u32[]{:S(2)}, u32[]{:S(2)}) %collective-permute-start.16) | collective-permute-done | bytes 2080 | tf_op jit(solution)/shard_map/ppermute | solution.py:394
  40.6 0.4 collective-permute-done.15.refs_1_
  41.0 1.1 %finish.1 = (f32[16,512]{1,0:T(8,128)}, f32[16,16]{1,0:T(8,128)}) custom-call(f32[16,512]{1,0:T(8,128)S(1)} %get-tuple-element.42.product_ref, f32[8,64]{1,0:T(8,128)S(1)} %add_add_fusion.refs_0_, f32[8,64]{1,0:T(8,128)S(1)} %collective-permute-done.15.refs_1_, f32[8,64]{1,0:T(8,128)S(1)} %collective-permute-done.16.refs_2_, ...), custom_call_target="tpu_custom_call" | custom-call | tf_op jit(solution)/shard_map/finish/pallas_call | solution.py:375
  (1 shorter events, 0.0 us)
Async XLA Ops:
  1.4 7.4 %collective-permute-start.1 = (bf16[24,512]{1,0:T(8,128)(2,1)S(1)}, bf16[24,512]{1,0:T(8,128)(2,1)S(1)}, u32[]{:S(2)}, u32[]{:S(2)}) collective-permute-start(bf16[24,512]{1,0:T(8,128)(2,1)S(1)} %get-tuple-element.24.refs_0_.refs_3_), channel_id=1, source_target_pairs={{0,4},{1,5},{2,6},{3,7},{4,0},{5,1},{6,2},{7,3},{8,12},{9,13},{10,... | collective-permute-start | bytes 73736 | tf_op jit(solution)/shard_map/ppermute | solution.py:394
  4.5 5.0 %collective-permute-start = (bf16[24,512]{1,0:T(8,128)(2,1)S(1)}, bf16[24,512]{1,0:T(8,128)(2,1)S(1)}, u32[]{:S(2)}, u32[]{:S(2)}) collective-permute-start(bf16[24,512]{1,0:T(8,128)(2,1)S(1)} %get-tuple-element.24.refs_0_.refs_3_), channel_id=1, source_target_pairs={{0,13},{1,12},{2,15},{3,14},{4,9},{5,8},{6,11},{7,10},{8,5},{9,4},... | collective-permute-start | bytes 73736 | tf_op jit(solution)/shard_map/ppermute | solution.py:394
  6.2 5.9 %collective-permute-start.2 = (bf16[24,512]{1,0:T(8,128)(2,1)S(1)}, bf16[24,512]{1,0:T(8,128)(2,1)S(1)}, u32[]{:S(2)}, u32[]{:S(2)}) collective-permute-start(bf16[24,512]{1,0:T(8,128)(2,1)S(1)} %get-tuple-element.24.refs_0_.refs_3_), channel_id=1, source_target_pairs={{0,9},{1,8},{2,11},{3,10},{4,13},{5,12},{6,15},{7,14},{8,1},{9,0},... | collective-permute-start | bytes 73736 | tf_op jit(solution)/shard_map/ppermute | solution.py:394
  6.3 4.8 %collective-permute-start.5 = (bf16[8,512]{1,0:T(8,128)(2,1)S(1)}, bf16[8,512]{1,0:T(8,128)(2,1)S(1)}, u32[]{:S(2)}, u32[]{:S(2)}) collective-permute-start(bf16[8,512]{1,0:T(8,128)(2,1)S(1)} %get-tuple-element.23.feats_ref), channel_id=1, source_target_pairs={{0,3},{1,2},{2,1},{3,0},{4,7},{5,6},{6,5},{7,4},{8,11},{9,10},{10,... | collective-permute-start | bytes 24584 | tf_op jit(solution)/shard_map/ppermute | solution.py:394
  8.4 3.7 %collective-permute-start.4 = (bf16[8,512]{1,0:T(8,128)(2,1)S(1)}, bf16[8,512]{1,0:T(8,128)(2,1)S(1)}, u32[]{:S(2)}, u32[]{:S(2)}) collective-permute-start(bf16[8,512]{1,0:T(8,128)(2,1)S(1)} %get-tuple-element.23.feats_ref), channel_id=1, source_target_pairs={{0,2},{1,3},{2,0},{3,1},{4,6},{5,7},{6,4},{7,5},{8,10},{9,11},{10,... | collective-permute-start | bytes 24584 | tf_op jit(solution)/shard_map/ppermute | solution.py:394
  8.9 3.1 %collective-permute-start.3 = (bf16[8,512]{1,0:T(8,128)(2,1)S(1)}, bf16[8,512]{1,0:T(8,128)(2,1)S(1)}, u32[]{:S(2)}, u32[]{:S(2)}) collective-permute-start(bf16[8,512]{1,0:T(8,128)(2,1)S(1)} %get-tuple-element.23.feats_ref), channel_id=1, source_target_pairs={{0,1},{1,0},{2,3},{3,2},{4,5},{5,4},{6,7},{7,6},{8,9},{9,8},{10,11... | collective-permute-start | bytes 24584 | tf_op jit(solution)/shard_map/ppermute | solution.py:394
  17.7 5.8 %collective-permute-start.6 = (f32[4,16,512]{2,1,0:T(8,128)S(1)}, f32[4,16,512]{2,1,0:T(8,128)S(1)}, u32[]{:S(2)}, u32[]{:S(2)}) collective-permute-start(f32[4,16,512]{2,1,0:T(8,128)S(1)} %get-tuple-element.30.own_ref), channel_id=1, source_target_pairs={{0,1},{1,0},{2,3},{3,2},{4,5},{5,4},{6,7},{7,6},{8,9},{9,8},{10,11... | collective-permute-start | bytes 393224 | tf_op jit(solution)/shard_map/ppermute | solution.py:394
  17.7 3.8 %collective-permute-start.8 = (bf16[4,16,512]{2,1,0:T(8,128)(2,1)S(1)}, bf16[4,16,512]{2,1,0:T(8,128)(2,1)S(1)}, u32[]{:S(2)}, u32[]{:S(2)}) collective-permute-start(bf16[4,16,512]{2,1,0:T(8,128)(2,1)S(1)} %get-tuple-element.31), channel_id=1, source_target_pairs={{0,3},{1,2},{2,1},{3,0},{4,7},{5,6},{6,5},{7,4},{8,11},{9,10},{10,... | collective-permute-start | bytes 196616 | tf_op jit(solution)/shard_map/ppermute | solution.py:394
  18.5 5.0 %collective-permute-start.7 = (bf16[4,16,512]{2,1,0:T(8,128)(2,1)S(1)}, bf16[4,16,512]{2,1,0:T(8,128)(2,1)S(1)}, u32[]{:S(2)}, u32[]{:S(2)}) collective-permute-start(bf16[4,16,512]{2,1,0:T(8,128)(2,1)S(1)} %get-tuple-element.31), channel_id=1, source_target_pairs={{0,2},{1,3},{2,0},{3,1},{4,6},{5,7},{6,4},{7,5},{8,10},{9,11},{10,... | collective-permute-start | bytes 196616 | tf_op jit(solution)/shard_map/ppermute | solution.py:394
  24.4 5.2 %collective-permute-start.9 = (f32[16,512]{1,0:T(8,128)S(1)}, f32[16,512]{1,0:T(8,128)S(1)}, u32[]{:S(2)}, u32[]{:S(2)}) collective-permute-start(f32[16,512]{1,0:T(8,128)S(1)} %get-tuple-element.39), channel_id=1, source_target_pairs={{0,13},{1,12},{2,15},{3,14},{4,9},{5,8},{6,11},{7,10},{8,5},{9,4},... | collective-permute-start | bytes 98312 | tf_op jit(solution)/shard_map/ppermute | solution.py:394
  25.9 4.8 %collective-permute-start.10 = (f32[16,512]{1,0:T(8,128)S(1)}, f32[16,512]{1,0:T(8,128)S(1)}, u32[]{:S(2)}, u32[]{:S(2)}) collective-permute-start(f32[16,512]{1,0:T(8,128)S(1)} %get-tuple-element.40), channel_id=1, source_target_pairs={{0,4},{1,5},{2,6},{3,7},{4,0},{5,1},{6,2},{7,3},{8,12},{9,13},{10,... | collective-permute-start | bytes 98312 | tf_op jit(solution)/shard_map/ppermute | solution.py:394
  26.3 4.4 %collective-permute-start.11 = (f32[16,512]{1,0:T(8,128)S(1)}, f32[16,512]{1,0:T(8,128)S(1)}, u32[]{:S(2)}, u32[]{:S(2)}) collective-permute-start(f32[16,512]{1,0:T(8,128)S(1)} %get-tuple-element.41), channel_id=1, source_target_pairs={{0,9},{1,8},{2,11},{3,10},{4,13},{5,12},{6,15},{7,14},{8,1},{9,0},... | collective-permute-start | bytes 98312 | tf_op jit(solution)/shard_map/ppermute | solution.py:394
  30.9 3.6 %collective-permute-start.14 = (f32[8,64]{1,0:T(8,128)S(1)}, f32[8,64]{1,0:T(8,128)S(1)}, u32[]{:S(2)}, u32[]{:S(2)}) collective-permute-start(f32[8,64]{1,0:T(8,128)S(1)} %get-tuple-element.43), channel_id=1, source_target_pairs={{0,2},{1,3},{2,0},{3,1},{4,6},{5,7},{6,4},{7,5},{8,10},{9,11},{10,... | collective-permute-start | bytes 6152 | tf_op jit(solution)/shard_map/ppermute | solution.py:394
  32.2 3.0 %collective-permute-start.13 = (f32[8,64]{1,0:T(8,128)S(1)}, f32[8,64]{1,0:T(8,128)S(1)}, u32[]{:S(2)}, u32[]{:S(2)}) collective-permute-start(f32[8,64]{1,0:T(8,128)S(1)} %get-tuple-element.43), channel_id=1, source_target_pairs={{0,3},{1,2},{2,1},{3,0},{4,7},{5,6},{6,5},{7,4},{8,11},{9,10},{10,... | collective-permute-start | bytes 6152 | tf_op jit(solution)/shard_map/ppermute | solution.py:394
  33.2 2.1 %collective-permute-start.12 = (f32[8,64]{1,0:T(8,128)S(1)}, f32[8,64]{1,0:T(8,128)S(1)}, u32[]{:S(2)}, u32[]{:S(2)}) collective-permute-start(f32[8,64]{1,0:T(8,128)S(1)} %get-tuple-element.43), channel_id=1, source_target_pairs={{0,1},{1,0},{2,3},{3,2},{4,5},{5,4},{6,7},{7,6},{8,9},{9,8},{10,11... | collective-permute-start | bytes 6152 | tf_op jit(solution)/shard_map/ppermute | solution.py:394
  35.3 4.9 %collective-permute-start.17 = (f32[8,64]{1,0:T(8,128)S(1)}, f32[8,64]{1,0:T(8,128)S(1)}, u32[]{:S(2)}, u32[]{:S(2)}) collective-permute-start(f32[8,64]{1,0:T(8,128)S(1)} %add_add_fusion.refs_0_), channel_id=1, source_target_pairs={{0,13},{1,12},{2,15},{3,14},{4,9},{5,8},{6,11},{7,10},{8,5},{9,4},... | collective-permute-start | bytes 6152 | tf_op jit(solution)/shard_map/ppermute | solution.py:394
  36.7 3.9 %collective-permute-start.16 = (f32[8,64]{1,0:T(8,128)S(1)}, f32[8,64]{1,0:T(8,128)S(1)}, u32[]{:S(2)}, u32[]{:S(2)}) collective-permute-start(f32[8,64]{1,0:T(8,128)S(1)} %add_add_fusion.refs_0_), channel_id=1, source_target_pairs={{0,9},{1,8},{2,11},{3,10},{4,13},{5,12},{6,15},{7,14},{8,1},{9,0},... | collective-permute-start | bytes 6152 | tf_op jit(solution)/shard_map/ppermute | solution.py:394
  38.0 3.0 %collective-permute-start.15 = (f32[8,64]{1,0:T(8,128)S(1)}, f32[8,64]{1,0:T(8,128)S(1)}, u32[]{:S(2)}, u32[]{:S(2)}) collective-permute-start(f32[8,64]{1,0:T(8,128)S(1)} %add_add_fusion.refs_0_), channel_id=1, source_target_pairs={{0,5},{1,4},{2,7},{3,6},{4,1},{5,0},{6,3},{7,2},{8,13},{9,12},{10,... | collective-permute-start | bytes 6152 | tf_op jit(solution)/shard_map/ppermute | solution.py:394

commit v8 on v6

--- a/solution.py
+++ b/solution.py
@@ -84,7 +84,7 @@
     copies = [pltpu.make_async_copy(a, b, sems.at[n]) for n, (a, b) in enumerate(zip(sources, buffers))]
     for copy in copies:
         copy.start()
-    for copy in copies:
+    for copy in copies[:2]:
         copy.wait()
     coords_ref, intensity_ref, start_ref = buffers
     hi, lo = split((coords_ref[...] - 0.5) * SCALE, 2)
@@ -93,8 +93,9 @@
     rows.update({3 + k: lo[k : k + 1] for k in range(3)})
     rows.update({6: log_hi, 7: log_lo})
     feats = stack_rows(rows, feats_ref.shape)
+    feats_ref[...] = feats.astype(BF16)
+    copies[2].wait()
     packed_ref[...] = jnp.concatenate([start_ref[...].astype(F32), feats], axis=0).astype(BF16)
-    feats_ref[...] = feats.astype(BF16)
 
 
 def prepare(coords, intensity, start):
@@ -164,17 +165,17 @@
     columns.append(last)
     logs.append(last_log)
     sources = list(packed_refs) + [last_ref]
+    vectors = jnp.concatenate([ref[:size] for ref in sources], axis=1)
     edge_ref[...] = tile_of(rows_ref[...], row_logs_ref[...], last, last_log)
     total = near_ref[...] + lax.dot_general(last_ref[:size], edge_ref[...], NT, preferred_element_type=F32)
     sum_ref[0] = total
     sent_ref[0] = total.astype(BF16)
     for k in range(count):
         at = slice(k * points, (k + 1) * points)
-        total = jnp.zeros(near_ref.shape, F32)
-        for c, ref in enumerate(sources):
+        for c in range(len(sources)):
             to = slice(c * points, (c + 1) * points)
             cov_ref[at, to] = tile_of(*made[k], columns[c], logs[c])
-            total += lax.dot_general(ref[:size], cov_ref[at, to], NT, preferred_element_type=F32)
+        total = lax.dot_general(vectors, cov_ref[at], NT, preferred_element_type=F32)
         sum_ref[k + 1] = total
         sent_ref[k + 1] = total.astype(BF16)
 

time: 42.5 us -> 42.6 us (level)
  no operation moved by 1% of the time
where the time goes in v8:
time: 42.6 us; the launch traced here: 42.3 us
  starting transfers between devices  19.6 us (46%)
  waiting for transfers between devices  11.1 us (26%)
  Pallas kernels  10.9 us (26%)
  between operations  0.66 us (2%)
    ppermute x18, starting transfers between devices, exchange(): lax.ppermute(value, 'wide', [(k, k ^ distance) for k in range(width)])  19.6 us
    ppermute x18, waiting for transfers between devices, exchange(): lax.ppermute(value, 'wide', [(k, k ^ distance) for k in range(width)])  11.1 us
    pallas_call x1, Pallas kernels, far(): pl.pallas_call(functools.partial(far_kernel, len(feats)), out_shape=(pltp...  5.68 us
    pallas_call x1, Pallas kernels, near(): pl.pallas_call(functools.partial(near_kernel, len(packed)), out_shape=(pl...  1.54 us
    pallas_call x1, Pallas kernels, second(): pl.pallas_call(second_kernel, out_shape=[pltpu.VMEM((size, points), F32)]...  1.1 us
    pallas_call x1, Pallas kernels, finish(): pl.pallas_call(functools.partial(finish_kernel, total_points), out_shape=...  1.07 us
  transfers between devices with their start and end apart: 18, of which 11 were waited for; matrix products, arithmetic and copies ran while one was open for 0% of the time, Pallas kernels for 5%

profile of v8, /device:TPU:0, one launch (start us, length us, event | category | flops | bytes accessed | tf_op | source)
XLA Modules:
  0.0 42.3 jit_solution(11503825673632830042)
XLA Ops:
  0.6 0.8 %prepare.1 = (bf16[24,512]{1,0:T(8,128)(2,1)S(1)}, bf16[8,512]{1,0:T(8,128)(2,1)S(1)}) custom-call(f32[3,512]{1,0:T(4,128)} %refs_0_.1, f32[1,512]{1,0:T(1,128)} %bitcast.1, bf16[16,512]{1,0:T(8,128)(2,1)} %refs_2_.1), custom_call_target="tpu_custom_call" | custom-call | tf_op jit(solution)/shard_map/prepare/pallas_call | solution.py:103
  1.4 3.1 %collective-permute-start.1 = (bf16[24,512]{1,0:T(8,128)(2,1)S(1)}, bf16[24,512]{1,0:T(8,128)(2,1)S(1)}, u32[]{:S(2)}, u32[]{:S(2)}) collective-permute-start(bf16[24,512]{1,0:T(8,128)(2,1)S(1)} %get-tuple-element.24.refs_0_.refs_3_), channel_id=1, source_target_pairs={{0,4},{1,5},{2,6},{3,7},{4,0},{5,1},{6,2},{7,3},{8,12},{9,13},{10,... | collective-permute-start | bytes 73736 | tf_op jit(solution)/shard_map/ppermute | solution.py:395
  4.5 1.6 %collective-permute-start = (bf16[24,512]{1,0:T(8,128)(2,1)S(1)}, bf16[24,512]{1,0:T(8,128)(2,1)S(1)}, u32[]{:S(2)}, u32[]{:S(2)}) collective-permute-start(bf16[24,512]{1,0:T(8,128)(2,1)S(1)} %get-tuple-element.24.refs_0_.refs_3_), channel_id=1, source_target_pairs={{0,13},{1,12},{2,15},{3,14},{4,9},{5,8},{6,11},{7,10},{8,5},{9,4},... | collective-permute-start | bytes 73736 | tf_op jit(solution)/shard_map/ppermute | solution.py:395
  6.1 0.1 collective-permute-start.2
  6.3 2.1 %collective-permute-start.5 = (bf16[8,512]{1,0:T(8,128)(2,1)S(1)}, bf16[8,512]{1,0:T(8,128)(2,1)S(1)}, u32[]{:S(2)}, u32[]{:S(2)}) collective-permute-start(bf16[8,512]{1,0:T(8,128)(2,1)S(1)} %get-tuple-element.23.feats_ref), channel_id=1, source_target_pairs={{0,3},{1,2},{2,1},{3,0},{4,7},{5,6},{6,5},{7,4},{8,11},{9,10},{10,... | collective-permute-start | bytes 24584 | tf_op jit(solution)/shard_map/ppermute | solution.py:395
  8.3 0.5 %collective-permute-start.4 = (bf16[8,512]{1,0:T(8,128)(2,1)S(1)}, bf16[8,512]{1,0:T(8,128)(2,1)S(1)}, u32[]{:S(2)}, u32[]{:S(2)}) collective-permute-start(bf16[8,512]{1,0:T(8,128)(2,1)S(1)} %get-tuple-element.23.feats_ref), channel_id=1, source_target_pairs={{0,2},{1,3},{2,0},{3,1},{4,6},{5,7},{6,4},{7,5},{8,10},{9,11},{10,... | collective-permute-start | bytes 24584 | tf_op jit(solution)/shard_map/ppermute | solution.py:395
  8.8 0.0 collective-permute-done.1.refs_2_.refs_5_
  8.8 0.0 collective-permute-start.3
  8.9 0.7 %collective-permute-done.refs_1_.refs_4_ = bf16[24,512]{1,0:T(8,128)(2,1)S(1)} collective-permute-done((bf16[24,512]{1,0:T(8,128)(2,1)S(1)}, bf16[24,512]{1,0:T(8,128)(2,1)S(1)}, u32[]{:S(2)}, u32[]{:S(2)}) %collective-permute-start) | collective-permute-done | bytes 24608 | tf_op jit(solution)/shard_map/ppermute | solution.py:395
  9.6 1.5 %near.1 = (bf16[512,32]{1,0:T(8,128)(2,1)S(1)}, f32[512,128]{1,0:T(8,128)S(1)}, bf16[32,1536]{1,0:T(8,128)(2,1)S(1)}, f32[1,1536]{1,0:T(1,128)S(1)}, bf16[512,15...) custom-call(bf16[8,512]{1,0:T(8,128)(2,1)S(1)} %get-tuple-element.23.feats_ref, ...), custom_call_target="tpu_custom_call" | custom-call | flops 31457280 | bytes 1572864 | tf_op jit(solution)/shard_map/near/pallas_call | solution.py:139
  11.1 0.0 collective-permute-done.5.refs_2_
  11.1 0.9 %collective-permute-done.4.refs_1_ = bf16[8,512]{1,0:T(8,128)(2,1)S(1)} collective-permute-done((bf16[8,512]{1,0:T(8,128)(2,1)S(1)}, bf16[8,512]{1,0:T(8,128)(2,1)S(1)}, u32[]{:S(2)}, u32[]{:S(2)}) %collective-permute-start.4) | collective-permute-done | bytes 8224 | tf_op jit(solution)/shard_map/ppermute | solution.py:395
  12.0 0.0 collective-permute-done.3.refs_0_
  12.0 0.0 collective-permute-done.2.last_ref
  12.0 5.7 %far.1 = (bf16[512,512]{1,0:T(8,128)(2,1)S(1)}, bf16[1536,2048]{1,0:T(8,128)(2,1)S(1)}, f32[4,16,512]{2,1,0:T(8,128)S(1)}, bf16[4,16,512]{2,1,0:T(8,128)(2,1)S(1)}) custom-call(f32[16,512]{1,0:T(8,128)S(1)} %get-tuple-element.25.near_ref, bf16[512,32]{1,0:T(8,128)(2,1)S(1)} %get-tuple-element.26.rows_ref, f32[512,128]{1,0:T(8,128)S(1)} %get-tuple-element.27.row_logs_ref, ...), custom_call_target="tpu_custom_call" | custom-call | flops 167772160 | bytes 8388608 | tf_op jit(solution)/shard_map/far/pallas_call | solution.py:186
  17.7 0.0 collective-permute-start.6
  17.7 0.8 %collective-permute-start.8 = (bf16[4,16,512]{2,1,0:T(8,128)(2,1)S(1)}, bf16[4,16,512]{2,1,0:T(8,128)(2,1)S(1)}, u32[]{:S(2)}, u32[]{:S(2)}) collective-permute-start(bf16[4,16,512]{2,1,0:T(8,128)(2,1)S(1)} %get-tuple-element.31), channel_id=1, source_target_pairs={{0,3},{1,2},{2,1},{3,0},{4,7},{5,6},{6,5},{7,4},{8,11},{9,10},{10,... | collective-permute-start | bytes 196616 | tf_op jit(solution)/shard_map/ppermute | solution.py:395
  18.5 1.4 %collective-permute-start.7 = (bf16[4,16,512]{2,1,0:T(8,128)(2,1)S(1)}, bf16[4,16,512]{2,1,0:T(8,128)(2,1)S(1)}, u32[]{:S(2)}, u32[]{:S(2)}) collective-permute-start(bf16[4,16,512]{2,1,0:T(8,128)(2,1)S(1)} %get-tuple-element.31), channel_id=1, source_target_pairs={{0,2},{1,3},{2,0},{3,1},{4,6},{5,7},{6,4},{7,5},{8,10},{9,11},{10,... | collective-permute-start | bytes 196616 | tf_op jit(solution)/shard_map/ppermute | solution.py:395
  19.9 1.7 %collective-permute-done.8.refs_2_ = bf16[4,16,512]{2,1,0:T(8,128)(2,1)S(1)} collective-permute-done((bf16[4,16,512]{2,1,0:T(8,128)(2,1)S(1)}, bf16[4,16,512]{2,1,0:T(8,128)(2,1)S(1)}, u32[]{:S(2)}, u32[]{:S(2)}) %collective-permute-start.8) | collective-permute-done | bytes 65568 | tf_op jit(solution)/shard_map/ppermute | solution.py:395
  21.5 2.0 %collective-permute-done.7.refs_1_ = bf16[4,16,512]{2,1,0:T(8,128)(2,1)S(1)} collective-permute-done((bf16[4,16,512]{2,1,0:T(8,128)(2,1)S(1)}, bf16[4,16,512]{2,1,0:T(8,128)(2,1)S(1)}, u32[]{:S(2)}, u32[]{:S(2)}) %collective-permute-start.7) | collective-permute-done | bytes 65568 | tf_op jit(solution)/shard_map/ppermute | solution.py:395
  23.5 0.0 collective-permute-done.6.refs_0_
  23.5 1.1 %second.1 = (f32[16,512]{1,0:T(8,128)S(1)}, f32[16,512]{1,0:T(8,128)S(1)}, f32[16,512]{1,0:T(8,128)S(1)}, bf16[4,32,512]{2,1,0:T(8,128)(2,1)S(1)}, f32[16,512]{1,0:T(8,128)S(1)}) custom-call(f32[4,16,512]{2,1,0:T(8,128)S(1)} %get-tuple-element.30.own_ref, f32[4,16,512]{2,1,0:T(8,128)S(1)} %collective-permute-done.6.refs_0_, ...), custom_call_target="tpu_custom_call" | custom-call | flops 15728640 | bytes 786432 | tf_op jit(solution)/shard_map/second/pallas_call | solution.py:243
  24.6 1.4 %collective-permute-start.9 = (f32[16,512]{1,0:T(8,128)S(1)}, f32[16,512]{1,0:T(8,128)S(1)}, u32[]{:S(2)}, u32[]{:S(2)}) collective-permute-start(f32[16,512]{1,0:T(8,128)S(1)} %get-tuple-element.39), channel_id=1, source_target_pairs={{0,13},{1,12},{2,15},{3,14},{4,9},{5,8},{6,11},{7,10},{8,5},{9,4},... | collective-permute-start | bytes 98312 | tf_op jit(solution)/shard_map/ppermute | solution.py:395
  26.1 0.4 collective-permute-start.10
  26.5 2.0 %collective-permute-start.11 = (f32[16,512]{1,0:T(8,128)S(1)}, f32[16,512]{1,0:T(8,128)S(1)}, u32[]{:S(2)}, u32[]{:S(2)}) collective-permute-start(f32[16,512]{1,0:T(8,128)S(1)} %get-tuple-element.41), channel_id=1, source_target_pairs={{0,9},{1,8},{2,11},{3,10},{4,13},{5,12},{6,15},{7,14},{8,1},{9,0},... | collective-permute-start | bytes 98312 | tf_op jit(solution)/shard_map/ppermute | solution.py:395
  28.5 0.5 %kept.1 = (f32[16,512]{1,0:T(8,128)S(1)}, f32[16,16]{1,0:T(8,128)S(1)}) custom-call(bf16[4,32,512]{2,1,0:T(8,128)(2,1)S(1)} %get-tuple-element.35.vectors_ref, f32[16,512]{1,0:T(8,128)S(1)} %get-tuple-element.36.first_ref, bf16[512,1536]{1,0:T(8,128)(2,1)S(1)} %get-tuple-element.32.refs_3_.near_ref, bf16[1536,2048]{1,0:T(8,128)(2,1)S(1)} %get-tuple-element.34.refs_5_.far_ref), custom_call_target="tpu_custom_call" | custom-call | flops 5242880 | bytes 262144 | tf_op jit(solution)/shard_map/kept/pallas_call | solution.py:265
  29.0 0.9 %collective-permute-done.9.refs_0_ = f32[16,512]{1,0:T(8,128)S(1)} collective-permute-done((f32[16,512]{1,0:T(8,128)S(1)}, f32[16,512]{1,0:T(8,128)S(1)}, u32[]{:S(2)}, u32[]{:S(2)}) %collective-permute-start.9) | collective-permute-done | bytes 32800 | tf_op jit(solution)/shard_map/ppermute | solution.py:395
  29.8 1.0 %collective-permute-done.10.refs_1_ = f32[16,512]{1,0:T(8,128)S(1)} collective-permute-done((f32[16,512]{1,0:T(8,128)S(1)}, f32[16,512]{1,0:T(8,128)S(1)}, u32[]{:S(2)}, u32[]{:S(2)}) %collective-permute-start.10) | collective-permute-done | bytes 32800 | tf_op jit(solution)/shard_map/ppermute | solution.py:395
  30.9 0.0 collective-permute-done.11.refs_2_
  30.9 0.2 gather_parts.1
  31.1 1.3 %collective-permute-start.14 = (f32[8,64]{1,0:T(8,128)S(1)}, f32[8,64]{1,0:T(8,128)S(1)}, u32[]{:S(2)}, u32[]{:S(2)}) collective-permute-start(f32[8,64]{1,0:T(8,128)S(1)} %get-tuple-element.43), channel_id=1, source_target_pairs={{0,2},{1,3},{2,0},{3,1},{4,6},{5,7},{6,4},{7,5},{8,10},{9,11},{10,... | collective-permute-start | bytes 6152 | tf_op jit(solution)/shard_map/ppermute | solution.py:395
  32.4 0.9 %collective-permute-start.13 = (f32[8,64]{1,0:T(8,128)S(1)}, f32[8,64]{1,0:T(8,128)S(1)}, u32[]{:S(2)}, u32[]{:S(2)}) collective-permute-start(f32[8,64]{1,0:T(8,128)S(1)} %get-tuple-element.43), channel_id=1, source_target_pairs={{0,3},{1,2},{2,1},{3,0},{4,7},{5,6},{6,5},{7,4},{8,11},{9,10},{10,... | collective-permute-start | bytes 6152 | tf_op jit(solution)/shard_map/ppermute | solution.py:395
  33.4 0.0 collective-permute-start.12
  33.4 1.4 %collective-permute-done.14 = f32[8,64]{1,0:T(8,128)S(1)} collective-permute-done((f32[8,64]{1,0:T(8,128)S(1)}, f32[8,64]{1,0:T(8,128)S(1)}, u32[]{:S(2)}, u32[]{:S(2)}) %collective-permute-start.14) | collective-permute-done | bytes 2080 | tf_op jit(solution)/shard_map/ppermute | solution.py:395
  34.7 0.7 %collective-permute-done.13 = f32[8,64]{1,0:T(8,128)S(1)} collective-permute-done((f32[8,64]{1,0:T(8,128)S(1)}, f32[8,64]{1,0:T(8,128)S(1)}, u32[]{:S(2)}, u32[]{:S(2)}) %collective-permute-start.13) | collective-permute-done | bytes 2080 | tf_op jit(solution)/shard_map/ppermute | solution.py:395
  35.5 0.0 collective-permute-done.12
  35.5 1.4 %collective-permute-start.17 = (f32[8,64]{1,0:T(8,128)S(1)}, f32[8,64]{1,0:T(8,128)S(1)}, u32[]{:S(2)}, u32[]{:S(2)}) collective-permute-start(f32[8,64]{1,0:T(8,128)S(1)} %add_add_fusion.refs_0_), channel_id=1, source_target_pairs={{0,13},{1,12},{2,15},{3,14},{4,9},{5,8},{6,11},{7,10},{8,5},{9,4},... | collective-permute-start | bytes 6152 | tf_op jit(solution)/shard_map/ppermute | solution.py:395
  36.8 1.3 %collective-permute-start.16 = (f32[8,64]{1,0:T(8,128)S(1)}, f32[8,64]{1,0:T(8,128)S(1)}, u32[]{:S(2)}, u32[]{:S(2)}) collective-permute-start(f32[8,64]{1,0:T(8,128)S(1)} %add_add_fusion.refs_0_), channel_id=1, source_target_pairs={{0,9},{1,8},{2,11},{3,10},{4,13},{5,12},{6,15},{7,14},{8,1},{9,0},... | collective-permute-start | bytes 6152 | tf_op jit(solution)/shard_map/ppermute | solution.py:395
  38.2 1.2 %collective-permute-start.15 = (f32[8,64]{1,0:T(8,128)S(1)}, f32[8,64]{1,0:T(8,128)S(1)}, u32[]{:S(2)}, u32[]{:S(2)}) collective-permute-start(f32[8,64]{1,0:T(8,128)S(1)} %add_add_fusion.refs_0_), channel_id=1, source_target_pairs={{0,5},{1,4},{2,7},{3,6},{4,1},{5,0},{6,3},{7,2},{8,13},{9,12},{10,... | collective-permute-start | bytes 6152 | tf_op jit(solution)/shard_map/ppermute | solution.py:395
  39.4 1.0 %collective-permute-done.17.refs_3_ = f32[8,64]{1,0:T(8,128)S(1)} collective-permute-done((f32[8,64]{1,0:T(8,128)S(1)}, f32[8,64]{1,0:T(8,128)S(1)}, u32[]{:S(2)}, u32[]{:S(2)}) %collective-permute-start.17) | collective-permute-done | bytes 2080 | tf_op jit(solution)/shard_map/ppermute | solution.py:395
  40.4 0.4 collective-permute-done.16.refs_2_
  40.8 0.4 collective-permute-done.15.refs_1_
  41.2 1.1 %finish.1 = (f32[16,512]{1,0:T(8,128)}, f32[16,16]{1,0:T(8,128)}) custom-call(f32[16,512]{1,0:T(8,128)S(1)} %get-tuple-element.42.product_ref, f32[8,64]{1,0:T(8,128)S(1)} %add_add_fusion.refs_0_, f32[8,64]{1,0:T(8,128)S(1)} %collective-permute-done.15.refs_1_, f32[8,64]{1,0:T(8,128)S(1)} %collective-permute-done.16.refs_2_, ...), custom_call_target="tpu_custom_call" | custom-call | tf_op jit(solution)/shard_map/finish/pallas_call | solution.py:376
  (1 shorter events, 0.0 us)
Async XLA Ops:
  1.4 7.4 %collective-permute-start.1 = (bf16[24,512]{1,0:T(8,128)(2,1)S(1)}, bf16[24,512]{1,0:T(8,128)(2,1)S(1)}, u32[]{:S(2)}, u32[]{:S(2)}) collective-permute-start(bf16[24,512]{1,0:T(8,128)(2,1)S(1)} %get-tuple-element.24.refs_0_.refs_3_), channel_id=1, source_target_pairs={{0,4},{1,5},{2,6},{3,7},{4,0},{5,1},{6,2},{7,3},{8,12},{9,13},{10,... | collective-permute-start | bytes 73736 | tf_op jit(solution)/shard_map/ppermute | solution.py:395
  4.5 5.0 %collective-permute-start = (bf16[24,512]{1,0:T(8,128)(2,1)S(1)}, bf16[24,512]{1,0:T(8,128)(2,1)S(1)}, u32[]{:S(2)}, u32[]{:S(2)}) collective-permute-start(bf16[24,512]{1,0:T(8,128)(2,1)S(1)} %get-tuple-element.24.refs_0_.refs_3_), channel_id=1, source_target_pairs={{0,13},{1,12},{2,15},{3,14},{4,9},{5,8},{6,11},{7,10},{8,5},{9,4},... | collective-permute-start | bytes 73736 | tf_op jit(solution)/shard_map/ppermute | solution.py:395
  6.1 5.9 %collective-permute-start.2 = (bf16[24,512]{1,0:T(8,128)(2,1)S(1)}, bf16[24,512]{1,0:T(8,128)(2,1)S(1)}, u32[]{:S(2)}, u32[]{:S(2)}) collective-permute-start(bf16[24,512]{1,0:T(8,128)(2,1)S(1)} %get-tuple-element.24.refs_0_.refs_3_), channel_id=1, source_target_pairs={{0,9},{1,8},{2,11},{3,10},{4,13},{5,12},{6,15},{7,14},{8,1},{9,0},... | collective-permute-start | bytes 73736 | tf_op jit(solution)/shard_map/ppermute | solution.py:395
  6.3 4.8 %collective-permute-start.5 = (bf16[8,512]{1,0:T(8,128)(2,1)S(1)}, bf16[8,512]{1,0:T(8,128)(2,1)S(1)}, u32[]{:S(2)}, u32[]{:S(2)}) collective-permute-start(bf16[8,512]{1,0:T(8,128)(2,1)S(1)} %get-tuple-element.23.feats_ref), channel_id=1, source_target_pairs={{0,3},{1,2},{2,1},{3,0},{4,7},{5,6},{6,5},{7,4},{8,11},{9,10},{10,... | collective-permute-start | bytes 24584 | tf_op jit(solution)/shard_map/ppermute | solution.py:395
  8.3 3.7 %collective-permute-start.4 = (bf16[8,512]{1,0:T(8,128)(2,1)S(1)}, bf16[8,512]{1,0:T(8,128)(2,1)S(1)}, u32[]{:S(2)}, u32[]{:S(2)}) collective-permute-start(bf16[8,512]{1,0:T(8,128)(2,1)S(1)} %get-tuple-element.23.feats_ref), channel_id=1, source_target_pairs={{0,2},{1,3},{2,0},{3,1},{4,6},{5,7},{6,4},{7,5},{8,10},{9,11},{10,... | collective-permute-start | bytes 24584 | tf_op jit(solution)/shard_map/ppermute | solution.py:395
  8.8 3.1 %collective-permute-start.3 = (bf16[8,512]{1,0:T(8,128)(2,1)S(1)}, bf16[8,512]{1,0:T(8,128)(2,1)S(1)}, u32[]{:S(2)}, u32[]{:S(2)}) collective-permute-start(bf16[8,512]{1,0:T(8,128)(2,1)S(1)} %get-tuple-element.23.feats_ref), channel_id=1, source_target_pairs={{0,1},{1,0},{2,3},{3,2},{4,5},{5,4},{6,7},{7,6},{8,9},{9,8},{10,11... | collective-permute-start | bytes 24584 | tf_op jit(solution)/shard_map/ppermute | solution.py:395
  17.7 5.9 %collective-permute-start.6 = (f32[4,16,512]{2,1,0:T(8,128)S(1)}, f32[4,16,512]{2,1,0:T(8,128)S(1)}, u32[]{:S(2)}, u32[]{:S(2)}) collective-permute-start(f32[4,16,512]{2,1,0:T(8,128)S(1)} %get-tuple-element.30.own_ref), channel_id=1, source_target_pairs={{0,1},{1,0},{2,3},{3,2},{4,5},{5,4},{6,7},{7,6},{8,9},{9,8},{10,11... | collective-permute-start | bytes 393224 | tf_op jit(solution)/shard_map/ppermute | solution.py:395
  17.7 3.8 %collective-permute-start.8 = (bf16[4,16,512]{2,1,0:T(8,128)(2,1)S(1)}, bf16[4,16,512]{2,1,0:T(8,128)(2,1)S(1)}, u32[]{:S(2)}, u32[]{:S(2)}) collective-permute-start(bf16[4,16,512]{2,1,0:T(8,128)(2,1)S(1)} %get-tuple-element.31), channel_id=1, source_target_pairs={{0,3},{1,2},{2,1},{3,0},{4,7},{5,6},{6,5},{7,4},{8,11},{9,10},{10,... | collective-permute-start | bytes 196616 | tf_op jit(solution)/shard_map/ppermute | solution.py:395
  18.5 5.0 %collective-permute-start.7 = (bf16[4,16,512]{2,1,0:T(8,128)(2,1)S(1)}, bf16[4,16,512]{2,1,0:T(8,128)(2,1)S(1)}, u32[]{:S(2)}, u32[]{:S(2)}) collective-permute-start(bf16[4,16,512]{2,1,0:T(8,128)(2,1)S(1)} %get-tuple-element.31), channel_id=1, source_target_pairs={{0,2},{1,3},{2,0},{3,1},{4,6},{5,7},{6,4},{7,5},{8,10},{9,11},{10,... | collective-permute-start | bytes 196616 | tf_op jit(solution)/shard_map/ppermute | solution.py:395
  24.6 5.2 %collective-permute-start.9 = (f32[16,512]{1,0:T(8,128)S(1)}, f32[16,512]{1,0:T(8,128)S(1)}, u32[]{:S(2)}, u32[]{:S(2)}) collective-permute-start(f32[16,512]{1,0:T(8,128)S(1)} %get-tuple-element.39), channel_id=1, source_target_pairs={{0,13},{1,12},{2,15},{3,14},{4,9},{5,8},{6,11},{7,10},{8,5},{9,4},... | collective-permute-start | bytes 98312 | tf_op jit(solution)/shard_map/ppermute | solution.py:395
  26.1 4.8 %collective-permute-start.10 = (f32[16,512]{1,0:T(8,128)S(1)}, f32[16,512]{1,0:T(8,128)S(1)}, u32[]{:S(2)}, u32[]{:S(2)}) collective-permute-start(f32[16,512]{1,0:T(8,128)S(1)} %get-tuple-element.40), channel_id=1, source_target_pairs={{0,4},{1,5},{2,6},{3,7},{4,0},{5,1},{6,2},{7,3},{8,12},{9,13},{10,... | collective-permute-start | bytes 98312 | tf_op jit(solution)/shard_map/ppermute | solution.py:395
  26.5 4.4 %collective-permute-start.11 = (f32[16,512]{1,0:T(8,128)S(1)}, f32[16,512]{1,0:T(8,128)S(1)}, u32[]{:S(2)}, u32[]{:S(2)}) collective-permute-start(f32[16,512]{1,0:T(8,128)S(1)} %get-tuple-element.41), channel_id=1, source_target_pairs={{0,9},{1,8},{2,11},{3,10},{4,13},{5,12},{6,15},{7,14},{8,1},{9,0},... | collective-permute-start | bytes 98312 | tf_op jit(solution)/shard_map/ppermute | solution.py:395
  31.1 3.6 %collective-permute-start.14 = (f32[8,64]{1,0:T(8,128)S(1)}, f32[8,64]{1,0:T(8,128)S(1)}, u32[]{:S(2)}, u32[]{:S(2)}) collective-permute-start(f32[8,64]{1,0:T(8,128)S(1)} %get-tuple-element.43), channel_id=1, source_target_pairs={{0,2},{1,3},{2,0},{3,1},{4,6},{5,7},{6,4},{7,5},{8,10},{9,11},{10,... | collective-permute-start | bytes 6152 | tf_op jit(solution)/shard_map/ppermute | solution.py:395
  32.4 3.0 %collective-permute-start.13 = (f32[8,64]{1,0:T(8,128)S(1)}, f32[8,64]{1,0:T(8,128)S(1)}, u32[]{:S(2)}, u32[]{:S(2)}) collective-permute-start(f32[8,64]{1,0:T(8,128)S(1)} %get-tuple-element.43), channel_id=1, source_target_pairs={{0,3},{1,2},{2,1},{3,0},{4,7},{5,6},{6,5},{7,4},{8,11},{9,10},{10,... | collective-permute-start | bytes 6152 | tf_op jit(solution)/shard_map/ppermute | solution.py:395
  33.4 2.1 %collective-permute-start.12 = (f32[8,64]{1,0:T(8,128)S(1)}, f32[8,64]{1,0:T(8,128)S(1)}, u32[]{:S(2)}, u32[]{:S(2)}) collective-permute-start(f32[8,64]{1,0:T(8,128)S(1)} %get-tuple-element.43), channel_id=1, source_target_pairs={{0,1},{1,0},{2,3},{3,2},{4,5},{5,4},{6,7},{7,6},{8,9},{9,8},{10,11... | collective-permute-start | bytes 6152 | tf_op jit(solution)/shard_map/ppermute | solution.py:395
  35.5 4.9 %collective-permute-start.17 = (f32[8,64]{1,0:T(8,128)S(1)}, f32[8,64]{1,0:T(8,128)S(1)}, u32[]{:S(2)}, u32[]{:S(2)}) collective-permute-start(f32[8,64]{1,0:T(8,128)S(1)} %add_add_fusion.refs_0_), channel_id=1, source_target_pairs={{0,13},{1,12},{2,15},{3,14},{4,9},{5,8},{6,11},{7,10},{8,5},{9,4},... | collective-permute-start | bytes 6152 | tf_op jit(solution)/shard_map/ppermute | solution.py:395
  36.8 3.9 %collective-permute-start.16 = (f32[8,64]{1,0:T(8,128)S(1)}, f32[8,64]{1,0:T(8,128)S(1)}, u32[]{:S(2)}, u32[]{:S(2)}) collective-permute-start(f32[8,64]{1,0:T(8,128)S(1)} %add_add_fusion.refs_0_), channel_id=1, source_target_pairs={{0,9},{1,8},{2,11},{3,10},{4,13},{5,12},{6,15},{7,14},{8,1},{9,0},... | collective-permute-start | bytes 6152 | tf_op jit(solution)/shard_map/ppermute | solution.py:395
  38.2 3.0 %collective-permute-start.15 = (f32[8,64]{1,0:T(8,128)S(1)}, f32[8,64]{1,0:T(8,128)S(1)}, u32[]{:S(2)}, u32[]{:S(2)}) collective-permute-start(f32[8,64]{1,0:T(8,128)S(1)} %add_add_fusion.refs_0_), channel_id=1, source_target_pairs={{0,5},{1,4},{2,7},{3,6},{4,1},{5,0},{6,3},{7,2},{8,13},{9,12},{10,... | collective-permute-start | bytes 6152 | tf_op jit(solution)/shard_map/ppermute | solution.py:395
